TPU v7x, 32 devices: a whole 2x2x4 slice. The times are simulated.
32 devices in a mesh: items: 4 (over y, x), seq: 8 (over z, core).
Axes of the slice: x: 2, y: 2, z: 4, core: 2. Of those that a mesh axis runs over, the one named last changes fastest.
Arguments:
- token_ids: int32 [16, 1024], P('items', 'seq'), may hold values from 0 to 127
- masked: int32 [16, 1024], P('items', 'seq'), may hold values 0 or 1
- item_flag: int32 [16], P('items'), may hold values 0 or 1
- prefix: int32 [16], P('items'), may hold values from 1 to 1024
- cotangent: bfloat16 [16, 1024, 2048], P('items', 'seq'), may hold values from -6 to 6
- embedding: bfloat16 [2048, 128], P(('items', 'seq')), may hold values from -6 to 6
- heads_weight: bfloat16 [2048, 6144], P(('items', 'seq')), may hold values from -0.21875 to 0.21875
- heads_bias: bfloat16 [6144], P(('items', 'seq')), may hold values from -4 to 4
- dense_weight: bfloat16 [2048, 2048], P(('items', 'seq')), may hold values from -0.75 to 0.75
- dense_bias: bfloat16 [2048], P(('items', 'seq')), may hold values from -6 to 6
- first_gain: bfloat16 [2048], P(('items', 'seq')), may hold values from 0.5 to 1.5
- first_bias: bfloat16 [2048], P(('items', 'seq')), may hold values from -4 to 4
- up_weight: bfloat16 [2048, 10922], P(('items', 'seq')), may hold values from -0.125 to 0.125
- up_bias: bfloat16 [10922], replicated, may hold values from -4 to 4
- down_weight: bfloat16 [5461, 2048], P(None, ('items', 'seq')), may hold values from -0.625 to 0.625
- down_bias: bfloat16 [2048], P(('items', 'seq')), may hold values from -6 to 6
- second_gain: bfloat16 [2048], P(('items', 'seq')), may hold values from 0.5 to 1.5
- second_bias: bfloat16 [2048], P(('items', 'seq')), may hold values from -4 to 4
Outputs:
- layer_out: bfloat16 [16, 1024, 2048], P('items', 'seq')
- input_grad: float32 [16, 1024, 2048], P('items', 'seq')
- embed_grad: float32 [2048, 128], P(('items', 'seq'))
- grad_heads_weight: float32 [2048, 6144], P(('items', 'seq'))
- grad_heads_bias: float32 [6144], P(('items', 'seq'))
- grad_dense_weight: float32 [2048, 2048], P(('items', 'seq'))
- grad_dense_bias: float32 [2048], P(('items', 'seq'))
- grad_first_gain: float32 [2048], P(('items', 'seq'))
- grad_first_bias: float32 [2048], P(('items', 'seq'))
- grad_up_weight: float32 [2048, 10922], P(('items', 'seq'))
- grad_up_bias: float32 [10922], replicated
- grad_down_weight: float32 [5461, 2048], P(None, ('items', 'seq'))
- grad_down_bias: float32 [2048], P(('items', 'seq'))
- grad_second_gain: float32 [2048], P(('items', 'seq'))
- grad_second_bias: float32 [2048], P(('items', 'seq'))
All inputs are finite; a program needn't handle non-finite values. No bound on the sum of `masked` or of `item_flag` on one device may be relied on, other than what follows from the above.
Results may differ from a plain program's by a relative error of at most 0.015.
Values may be sent and summed in bfloat16 or wider, within the bound.
A program may use at most 384 MiB of HBM per device.

v0:
```python
import math

import jax
import jax.numpy as jnp
from jax import lax
from jax.sharding import PartitionSpec as P

HEADS = 16
HEAD = 128


deep_alpha = math.sqrt(48.0)
epsilon = 1e-05
mask_token = 3


def for_sending(shard):

    def short(part):
        return part.astype(jnp.bfloat16) if part.dtype == jnp.float32 else part

    return jax.tree.map(short, shard)


def rotary(values, positions):
    half_width = values.shape[-1] // 2
    frequency = jnp.exp(
        jnp.arange(half_width, dtype=jnp.float32) * (-2.0 * math.log(10000.0) / values.shape[-1])
    )
    angles = positions[:, None] * frequency[None, :]
    cosine = jnp.cos(angles)[:, None, :]
    sine_part = jnp.sin(angles)[:, None, :]
    first = values[..., :half_width]
    second = values[..., half_width:]
    return jnp.concatenate(
        [first * cosine - second * sine_part, second * cosine + first * sine_part], axis=-1
    )


def norm_forward(residual, gain_vec, bias_vec):
    center = residual - jnp.mean(residual, axis=-1, keepdims=True)
    inverse = lax.rsqrt(jnp.mean(center * center, axis=-1, keepdims=True) + epsilon)
    normed = center * inverse
    return (normed * gain_vec + bias_vec, normed, inverse)


def norm_backward(grad_out, normed, inverse, gain_vec):
    scaled = grad_out * gain_vec
    grad_in = inverse * (
        scaled
        - jnp.mean(scaled, axis=-1, keepdims=True)
        - normed * jnp.mean(scaled * normed, axis=-1, keepdims=True)
    )
    return (grad_in, jnp.sum(grad_out * normed, axis=0), jnp.sum(grad_out, axis=0))


def contract_rows(left, right):
    return lax.dot_general(
        left, right, (((0,), (0,)), ((), ())), preferred_element_type=jnp.float32
    )


def contract_cols(left, right):
    return lax.dot_general(
        left, right, (((1,), (1,)), ((), ())), preferred_element_type=jnp.float32
    )


def exact_gelu(values):
    return jax.nn.gelu(values, approximate=False)


def visible_mask(offset, block_rows, total_length, visible):
    query_pos = offset + jnp.arange(block_rows, dtype=jnp.int32)[:, None]
    key_pos = jnp.arange(total_length, dtype=jnp.int32)[None, :]
    return (key_pos <= query_pos) | (key_pos < visible)


def block_scores(query_block, keys_all, offset, visible):
    block_rows = query_block.shape[0]
    total_length = keys_all.shape[0]
    scores = jnp.einsum(
        "qhd,khd->hqk", query_block, keys_all, preferred_element_type=jnp.float32
    ) * HEAD ** (-0.5)
    return jnp.where(
        visible_mask(offset, block_rows, total_length, visible)[None], scores, -jnp.inf
    )


def attend(paired):
    unit, visible = paired
    total_length = unit.shape[0]
    block_rows = min(512, total_length)
    queries = unit[..., :HEAD]
    keys_all = unit[..., HEAD : 2 * HEAD]
    values = unit[..., 2 * HEAD :]
    contexts = []
    log_sums = []
    for offset in range(0, total_length, block_rows):
        scores = block_scores(queries[offset : offset + block_rows], keys_all, offset, visible)
        row_peak = jnp.max(scores, axis=-1, keepdims=True)
        expos = jnp.exp(scores - row_peak)
        row_total = jnp.sum(expos, axis=-1, keepdims=True)
        weights_low = (expos / row_total).astype(jnp.bfloat16)
        contexts.append(
            jnp.einsum(
                "hqk,khd->qhd", weights_low, values, preferred_element_type=jnp.float32
            ).astype(jnp.bfloat16)
        )
        log_sums.append((row_peak + jnp.log(row_total))[..., 0])
    return (jnp.concatenate(contexts, axis=0), jnp.concatenate(log_sums, axis=1))


def attend_back(grouped):
    unit, grad_context, log_sums, visible = grouped
    total_length = unit.shape[0]
    block_rows = min(512, total_length)
    queries = unit[..., :HEAD]
    keys_all = unit[..., HEAD : 2 * HEAD]
    values = unit[..., 2 * HEAD :]
    grad_queries = []
    grad_keys = jnp.zeros(keys_all.shape, jnp.float32)
    grad_values = jnp.zeros(values.shape, jnp.float32)
    for offset in range(0, total_length, block_rows):
        query_block = queries[offset : offset + block_rows]
        grad_block = grad_context[offset : offset + block_rows]
        scores = block_scores(query_block, keys_all, offset, visible)
        weights = jnp.exp(scores - log_sums[:, offset : offset + block_rows, None])
        weights_low = weights.astype(jnp.bfloat16)
        grad_values = grad_values + jnp.einsum(
            "hqk,qhd->khd", weights_low, grad_block, preferred_element_type=jnp.float32
        )
        grad_weights = jnp.einsum(
            "qhd,khd->hqk", grad_block, values, preferred_element_type=jnp.float32
        )
        inner = jnp.sum(weights * grad_weights, axis=-1, keepdims=True)
        grad_scores = (weights * (grad_weights - inner)).astype(jnp.bfloat16)
        grad_queries.append(
            jnp.einsum("hqk,khd->qhd", grad_scores, keys_all, preferred_element_type=jnp.float32)
            * HEAD ** (-0.5)
        )
        grad_keys = grad_keys + jnp.einsum(
            "hqk,qhd->khd", grad_scores, query_block, preferred_element_type=jnp.float32
        ) * HEAD ** (-0.5)
    return jnp.concatenate(
        [jnp.concatenate(grad_queries, axis=0), grad_keys, grad_values], axis=-1
    ).astype(jnp.bfloat16)


def on_device(
    token_ids,
    masked,
    item_flag,
    prefix,
    cotangent,
    embedding,
    heads_weight,
    heads_bias,
    dense_weight,
    dense_bias,
    first_gain,
    first_bias,
    up_weight,
    up_bias,
    down_weight,
    down_bias,
    second_gain,
    second_bias,
):
    items_here, local_span = token_ids.shape
    local_rows = items_here * local_span
    total_length = local_span * lax.axis_size("seq")
    table, w_heads, w_dense, gain_one, shift_one, b_heads, b_dense = (
        lax.all_gather(embedding, ("items", "seq"), axis=0, tiled=True),
        lax.all_gather(heads_weight, ("items", "seq"), axis=0, tiled=True),
        lax.all_gather(dense_weight, ("items", "seq"), axis=0, tiled=True),
        lax.all_gather(first_gain, ("items", "seq"), axis=0, tiled=True),
        lax.all_gather(first_bias, ("items", "seq"), axis=0, tiled=True),
        lax.all_gather(heads_bias, ("items", "seq"), axis=0, tiled=True),
        lax.all_gather(dense_bias, ("items", "seq"), axis=0, tiled=True),
    )
    w_up, w_down, gain_two, shift_two, b_down = (
        lax.all_gather(up_weight, ("items", "seq"), axis=0, tiled=True),
        lax.all_gather(down_weight, ("items", "seq"), axis=1, tiled=True),
        lax.all_gather(second_gain, ("items", "seq"), axis=0, tiled=True),
        lax.all_gather(second_bias, ("items", "seq"), axis=0, tiled=True),
        lax.all_gather(down_bias, ("items", "seq"), axis=0, tiled=True),
    )
    gain_one = gain_one.astype(jnp.float32)
    shift_one = shift_one.astype(jnp.float32)
    gain_two = gain_two.astype(jnp.float32)
    shift_two = shift_two.astype(jnp.float32)
    input_ids = jnp.where(masked == 1, mask_token, token_ids).reshape(local_rows)
    onehot = (input_ids[:, None] == jnp.arange(table.shape[1], dtype=jnp.int32)[None, :]).astype(
        jnp.bfloat16
    )
    inputs = contract_cols(onehot, table)
    inputs_low = inputs.astype(jnp.bfloat16)
    mixed_rows = (
        jnp.dot(inputs_low, w_heads, preferred_element_type=jnp.float32)
        + b_heads.astype(jnp.float32)
    ).reshape(local_rows, HEADS, 3 * HEAD)
    positions = jnp.tile(
        (lax.axis_index("seq") * local_span + jnp.arange(local_span, dtype=jnp.int32)).astype(
            jnp.float32
        ),
        items_here,
    )
    packed = jnp.concatenate(
        [
            rotary(mixed_rows[..., :HEAD], positions),
            rotary(mixed_rows[..., HEAD : 2 * HEAD], positions),
            mixed_rows[..., 2 * HEAD :],
        ],
        axis=-1,
    )
    packed = packed.astype(jnp.bfloat16).reshape(items_here, local_span, HEADS, 3 * HEAD)
    by_head = lax.all_to_all(packed, "seq", split_axis=2, concat_axis=1, tiled=True)
    visible = jnp.where(item_flag == 1, total_length, prefix)
    contexts, log_sums = lax.map(attend, (by_head, visible))
    context_rows = jax.tree.map(
        lambda part, own: part.astype(own.dtype),
        lax.all_to_all(for_sending(contexts), "seq", split_axis=1, concat_axis=2, tiled=True),
        contexts,
    ).reshape(local_rows, HEADS * HEAD)
    branch = jnp.dot(context_rows, w_dense, preferred_element_type=jnp.float32) + b_dense.astype(
        jnp.float32
    )
    hidden, normed_one, inverse_one = norm_forward(
        deep_alpha * inputs + branch, gain_one, shift_one
    )
    hidden_low = hidden.astype(jnp.bfloat16)
    gate_up = jnp.dot(hidden_low, w_up, preferred_element_type=jnp.float32) + up_bias.astype(
        jnp.float32
    )
    ff_width = w_down.shape[0]
    up_part = gate_up[:, :ff_width]
    activated, gelu_pull = jax.vjp(exact_gelu, gate_up[:, ff_width:])
    product_low = (up_part * activated).astype(jnp.bfloat16)
    mlp_branch = jnp.dot(product_low, w_down, preferred_element_type=jnp.float32) + b_down.astype(
        jnp.float32
    )
    layer_out, normed_two, inverse_two = norm_forward(
        deep_alpha * hidden + mlp_branch, gain_two, shift_two
    )
    w_up, w_down = (
        lax.all_gather(up_weight, ("items", "seq"), axis=0, tiled=True),
        lax.all_gather(down_weight, ("items", "seq"), axis=1, tiled=True),
    )
    grad_top = cotangent.reshape(local_rows, -1).astype(jnp.float32)
    grad_resid_two, grad_gain_two, grad_shift_two = norm_backward(
        grad_top, normed_two, inverse_two, gain_two
    )
    grad_mlp_low = grad_resid_two.astype(jnp.bfloat16)
    grad_product = contract_cols(grad_mlp_low, w_down)
    grad_gate = gelu_pull(grad_product * up_part)[0]
    grad_gate_up_low = jnp.concatenate([grad_product * activated, grad_gate], axis=1).astype(
        jnp.bfloat16
    )
    grad_hidden = contract_cols(grad_gate_up_low, w_up) + deep_alpha * grad_resid_two
    rear_terms = (
        contract_rows(hidden_low, grad_gate_up_low),
        contract_rows(product_low, grad_mlp_low),
        grad_gain_two,
        grad_shift_two,
        jnp.sum(grad_mlp_low.astype(jnp.float32), axis=0),
    )
    rear_grads = (
        lax.psum_scatter(rear_terms[0], ("items", "seq"), scatter_dimension=0, tiled=True),
        lax.psum_scatter(rear_terms[1], ("items", "seq"), scatter_dimension=1, tiled=True),
        lax.psum_scatter(rear_terms[2], ("items", "seq"), scatter_dimension=0, tiled=True),
        lax.psum_scatter(rear_terms[3], ("items", "seq"), scatter_dimension=0, tiled=True),
        lax.psum_scatter(rear_terms[4], ("items", "seq"), scatter_dimension=0, tiled=True),
    )
    grad_up_bias = lax.psum(jnp.sum(grad_gate_up_low.astype(jnp.float32), axis=0), ("items", "seq"))
    w_heads, w_dense = (
        lax.all_gather(heads_weight, ("items", "seq"), axis=0, tiled=True),
        lax.all_gather(dense_weight, ("items", "seq"), axis=0, tiled=True),
    )
    grad_resid_one, grad_gain_one, grad_shift_one = norm_backward(
        grad_hidden, normed_one, inverse_one, gain_one
    )
    grad_branch_low = grad_resid_one.astype(jnp.bfloat16)
    grad_context = (
        contract_cols(grad_branch_low, w_dense)
        .astype(jnp.bfloat16)
        .reshape(items_here, local_span, HEADS, HEAD)
    )
    grad_by_head = lax.all_to_all(grad_context, "seq", split_axis=2, concat_axis=1, tiled=True)
    grad_packed = lax.map(attend_back, (by_head, grad_by_head, log_sums, visible))
    grad_rows = (
        jax.tree.map(
            lambda part, own: part.astype(own.dtype),
            lax.all_to_all(
                for_sending(grad_packed), "seq", split_axis=1, concat_axis=2, tiled=True
            ),
            grad_packed,
        )
        .astype(jnp.float32)
        .reshape(local_rows, HEADS, 3 * HEAD)
    )
    backward_pos = -positions
    grad_mixed_low = jnp.concatenate(
        [
            rotary(grad_rows[..., :HEAD], backward_pos),
            rotary(grad_rows[..., HEAD : 2 * HEAD], backward_pos),
            grad_rows[..., 2 * HEAD :],
        ],
        axis=-1,
    )
    grad_mixed_low = grad_mixed_low.reshape(local_rows, 3 * HEADS * HEAD).astype(jnp.bfloat16)
    input_grad = contract_cols(grad_mixed_low, w_heads) + deep_alpha * grad_resid_one
    embed_term = lax.dot_general(
        input_grad,
        onehot.astype(jnp.float32),
        (((0,), (0,)), ((), ())),
        precision=lax.Precision.HIGHEST,
        preferred_element_type=jnp.float32,
    )
    front_terms = (
        embed_term,
        contract_rows(inputs_low, grad_mixed_low),
        contract_rows(context_rows, grad_branch_low),
        grad_gain_one,
        grad_shift_one,
        jnp.sum(grad_mixed_low.astype(jnp.float32), axis=0),
        jnp.sum(grad_branch_low.astype(jnp.float32), axis=0),
    )
    front_grads = (
        lax.psum_scatter(front_terms[0], ("items", "seq"), scatter_dimension=0, tiled=True),
        lax.psum_scatter(front_terms[1], ("items", "seq"), scatter_dimension=0, tiled=True),
        lax.psum_scatter(front_terms[2], ("items", "seq"), scatter_dimension=0, tiled=True),
        lax.psum_scatter(front_terms[3], ("items", "seq"), scatter_dimension=0, tiled=True),
        lax.psum_scatter(front_terms[4], ("items", "seq"), scatter_dimension=0, tiled=True),
        lax.psum_scatter(front_terms[5], ("items", "seq"), scatter_dimension=0, tiled=True),
        lax.psum_scatter(front_terms[6], ("items", "seq"), scatter_dimension=0, tiled=True),
    )
    return (
        layer_out.astype(jnp.bfloat16).reshape(items_here, local_span, -1),
        input_grad.reshape(items_here, local_span, -1),
        0.1 * front_grads[0],
        front_grads[1],
        front_grads[5],
        front_grads[2],
        front_grads[6],
        front_grads[3],
        front_grads[4],
        rear_grads[0],
        grad_up_bias,
        rear_grads[1],
        rear_grads[4],
        rear_grads[2],
        rear_grads[3],
    )


def solution(mesh):
    in_specs = (
        P("items", "seq"),
        P("items", "seq"),
        P("items"),
        P("items"),
        P("items", "seq", None),
        P(("items", "seq"), None),
        P(("items", "seq"), None),
        P(("items", "seq")),
        P(("items", "seq"), None),
        P(("items", "seq")),
        P(("items", "seq")),
        P(("items", "seq")),
        P(("items", "seq"), None),
        P(),
        P(None, ("items", "seq")),
        P(("items", "seq")),
        P(("items", "seq")),
        P(("items", "seq")),
    )
    out_specs = (
        P("items", "seq", None),
        P("items", "seq", None),
        P(("items", "seq"), None),
        P(("items", "seq"), None),
        P(("items", "seq")),
        P(("items", "seq"), None),
        P(("items", "seq")),
        P(("items", "seq")),
        P(("items", "seq")),
        P(("items", "seq"), None),
        P(),
        P(None, ("items", "seq")),
        P(("items", "seq")),
        P(("items", "seq")),
        P(("items", "seq")),
    )
    return jax.shard_map(
        on_device, mesh=mesh, in_specs=in_specs, out_specs=out_specs, check_vma=False
    )
```

profile of v0, /device:TPU:0, one launch (start us, length us, event | category | flops | bytes accessed | tf_op | source)
XLA Modules:
  0.0 3615.1 jit_solution(10442578209963783982)
XLA Ops:
  15.3 44.1 %all-reduce.15 = (bf16[6144]{0:T(1024)(128)(2,1)S(1)}, bf16[2048]{0:T(1024)(128)(2,1)}, bf16[2048]{0:T(1024)(128)(2,1)}, bf16[2048]{0:T(1024)(128)(2,1)}, bf16[2...) all-reduce(bf16[6144]{0:T(1024)(128)(2,1)S(1)} %dynamic-update-slic, ...), channel_id=1, replica_groups=mesh['items'=4,'seq'=8] {'items','seq'}, use_global_device_ids=true, to_apply=%add | all-reduce | flops 18432 | bytes 73728
  62.9 46.4 %all_gather.40 = bf16[2048,128]{1,0:T(8,128)(2,1)S(1)} all-gather(bf16[64,128]{1,0:T(8,128)(2,1)} %param.27), channel_id=1, replica_groups=mesh['items'=4,'seq'=8] {'items','seq'}, dimensions={0}, use_global_device_ids=true | all-gather | bytes 540672 | tf_op jit(solution)/shard_map/all_gather | solution.py:174
  112.1 60.5 %all-gather.5.cloned.1.call-done = bf16[2048,6144]{1,0:T(8,128)(2,1)} async-done(((bf16[64,6144]{1,0:T(8,128)(2,1)}), bf16[2048,6144]{1,0:T(8,128)(2,1)}) %all-gather.5.cloned.1.call-update) | async-done | bytes 25165840 | tf_op jit(solution)/shard_map/all_gather | solution.py:175
  172.6 21.9 convolution_add_fusion.2
  245.8 229.4 %all-to-all-done = bf16[4,128,16,384]{3,1,0,2:T(8,128)(2,1)} async-done(((bf16[4,128,16,384]{3,1,0,2:T(8,128)(2,1)}), bf16[4,128,16,384]{3,1,0,2:T(8,128)(2,1)}, u32[]{:S(2)}, u32[]{:S(2)}) %all-to-all-start) | async-done | bytes 6291488 | tf_op jit(solution)/shard_map/all_to_all | solution.py:218
  485.2 56.8 %while.22 = (s32[]{:T(128)}, bf16[4,1024,2,128]{3,2,0,1:T(2,128)(2,1)}, f32[4,2,1024]{2,1,0:T(2,128)}, bf16[4,1024,2,384]{3,1,2,0:T(8,128)(2,1)}, s32[4]{0:T(128)}, /*index=5*/s32[]{:T(128)}) while((s32[]{:T(128)}, bf16[4,1024,2,128]{3,2,0,1:T(2,128)(2,1)}, f32[4,2,1024]{2,1,0:T(2,128)}, bf16[4,1024,2,384]{3,1,2,0:T(8,128)(2,1)}, s32[4]{0:T(128)}, ...), condition=%wide.region_5.6_spmd, body=%wide.region_0.5_spmd.sunk | while | flops 1102317056 | bytes 38885480 | solution.py:220
  548.3 95.0 %all-to-all-done.1 = bf16[4,1024,2,128]{3,2,0,1:T(2,128)(2,1)} async-done(((bf16[4,1024,2,128]{3,2,0,1:T(2,128)(2,1)}), bf16[4,1024,2,128]{3,2,0,1:T(2,128)(2,1)}, u32[]{:S(2)}, u32[]{:S(2)}) %all-to-all-start.1) | async-done | bytes 2097184 | tf_op jit(solution)/shard_map/all_to_all | solution.py:223
  664.6 35.8 convolution_add_fusion.1
  700.5 28.3 multiply_convert_fusion.3
  728.7 64.5 %all-gather.11.cloned.1.call-done = bf16[5461,2048]{0,1:T(8,128)(2,1)} async-done(((bf16[5461,64]{0,1:T(8,128)(2,1)}), bf16[5461,2048]{0,1:T(8,128)(2,1)}) %all-gather.11.cloned.1.call-update) | async-done | bytes 22368272 | tf_op jit(solution)/shard_map/all_gather | solution.py:184
  793.3 21.0 fusion.120
  823.9 29.4 multiply_convert_fusion.2
  853.3 46.3 %multiply_reduce_fusion.2 = (f32[2048]{0:T(1024)}, f32[512]{0:T(512)S(1)}, f32[512]{0:T(512)S(1)}, f32[2048]{0:T(1024)}, f32[512,2048]{1,0:T(8,128)}) fusion(f32[512,2048]{1,0:T(8,128)} %copy-done.3, f32[512]{0:T(512)S(1)} %add_rsqrt_fusion.1, f32[512]{0:T(512)S(1)} %broadcast_multiply_fusion.5, f32[2048]{0:T(1024)S(1)} %convert_element_type.142, ...), kind=kOutput, calls=%fused_computation.147 | convolution fusion | flops 22938992640 | bytes 68536320 | tf_op jit(solution)/shard_map/dot_general | solution.py:64
  920.4 49.0 %all-to-all-done.2 = bf16[4,128,16,128]{3,1,0,2:T(8,128)(2,1)S(1)} async-done(((bf16[4,128,16,128]{3,1,0,2:T(8,128)(2,1)}), bf16[4,128,16,128]{3,1,0,2:T(8,128)(2,1)S(1)}, u32[]{:S(2)}, u32[]{:S(2)}) %all-to-all-start.2) | async-done | bytes 2097184 | tf_op jit(solution)/shard_map/all_to_all | solution.py:289
  970.8 118.9 %while.23 = (s32[]{:T(128)}, bf16[4,1024,2,384]{3,2,0,1:T(2,128)(2,1)}, bf16[4,1024,2,384]{3,1,2,0:T(8,128)(2,1)}, s32[4]{0:T(128)}, f32[4,2,1024]{2,1,0:T(2,128...) while((s32[]{:T(128)}, bf16[4,1024,2,384]{3,2,0,1:T(2,128)(2,1)}, ...), condition=%wide.region_17.18_spmd, body=%wide.region_14.17_spmd.sunk | while | flops 2725510656 | bytes 108607680 | solution.py:290
  1110.9 122.5 %all-to-all-done.3 = bf16[4,1024,2,384]{3,2,0,1:T(2,128)(2,1)} async-done(((bf16[4,1024,2,384]{3,2,0,1:T(2,128)(2,1)}), bf16[4,1024,2,384]{3,2,0,1:T(2,128)(2,1)}, u32[]{:S(2)}, u32[]{:S(2)}) %all-to-all-start.3) | async-done | bytes 6291488 | tf_op jit(solution)/shard_map/all_to_all | solution.py:294
  1330.8 24.6 fusion.98
  1355.5 22.7 fusion.110
  1378.9 41.4 %fusion.95 = f32[2048,10922]{1,0:T(8,128)} fusion(bf16[512,5461]{0,1:T(8,128)(2,1)} %get-tuple-element.148, bf16[512,5461]{0,1:T(8,128)(2,1)} %get-tuple-element.147, f32[512,2048]{1,0:T(8,128)} %copy-done.3, f32[2048]{0:T(1024)S(1)} %copy-done.17, f32[2048]{0:T(1024)S(1)} %copy-done.10, f32[512]{0:T(512)S(1)} %copy-done.19, f32[512]{0:T(512)S(1)} %copy-done.15), kind=kOutput, calls=%fused_computation.171 | convolution fusion | flops 22932705280 | bytes 104871936 | tf_op jit(solution)/shard_map/dot_general | solution.py:58
  1429.3 124.0 %reduce-scatter.6.cloned.1.call-done = f32[64,128]{1,0:T(8,128)} async-done(((f32[2048,128]{1,0:T(8,128)}), f32[64,128]{1,0:T(8,128)}) %reduce-scatter.6.cloned.1.call-update) | async-done | bytes 32784 | tf_op jit(solution)/shard_map/reduce_scatter | solution.py:330
  1554.7 184.5 %reduce-scatter.10.cloned.1.call-done = f32[64,2048]{1,0:T(8,128)} async-done(((f32[2048,2048]{1,0:T(8,128)}), f32[64,2048]{1,0:T(8,128)}) %reduce-scatter.10.cloned.1.call-update) | async-done | bytes 524304 | tf_op jit(solution)/shard_map/reduce_scatter | solution.py:332
  1739.2 436.2 %reduce-scatter.8.cloned.1.call-done = f32[64,6144]{1,0:T(8,128)} async-done(((f32[2048,6144]{1,0:T(8,128)}), f32[64,6144]{1,0:T(8,128)}) %reduce-scatter.8.cloned.1.call-update) | async-done | bytes 1572880 | tf_op jit(solution)/shard_map/reduce_scatter | solution.py:331
  2175.3 482.9 %reduce-scatter.14.cloned.1.call-done = f32[5461,64]{0,1:T(8,128)} async-done(((f32[5461,2048]{0,1:T(8,128)}), f32[5461,64]{0,1:T(8,128)}) %reduce-scatter.14.cloned.1.call-update) | async-done | bytes 1398032 | tf_op jit(solution)/shard_map/reduce_scatter | solution.py:270
  2658.2 948.4 %reduce-scatter.12.cloned.1.call-done = f32[64,10922]{1,0:T(8,128)} async-done(((f32[2048,10922]{1,0:T(8,128)}), f32[64,10922]{1,0:T(8,128)}) %reduce-scatter.12.cloned.1.call-update) | async-done | bytes 2796048 | tf_op jit(solution)/shard_map/reduce_scatter | solution.py:269
  (322 shorter events, 440.3 us)
Async XLA Ops:
  7.2 165.4 %all-gather.5.cloned.1.call-start = ((), (), s32[]{:S(2)}) async-start(), calls=%async_computation.9 | async-start | bytes 25952256 | tf_op jit(solution)/shard_map/all_gather | solution.py:175
  7.9 644.2 %all-gather.7.cloned.1.call-start = ((), (), s32[]{:S(2)}) async-start(), calls=%async_computation.10 | async-start | bytes 8650752 | tf_op jit(solution)/shard_map/all_gather | solution.py:176
  8.7 655.9 %all-gather.9.cloned.1.call-start = ((), (), s32[]{:S(2)}) async-start(), calls=%async_computation.11 | async-start | bytes 46497792 | tf_op jit(solution)/shard_map/all_gather | solution.py:183
  60.2 134.2 %copy-start.12 = (s32[512]{0:T(512)}, s32[512]{0:T(512)S(1)}, u32[]{:S(2)}) copy-start(s32[512]{0:T(512)S(1)} %select_bitcast_fusion) | copy-start | bytes 6148
  239.6 5.7 copy-start.26
  239.6 5.7 copy-start.27
  239.6 235.6 %all-to-all-start = ((bf16[4,128,16,384]{3,1,0,2:T(8,128)(2,1)}), bf16[4,128,16,384]{3,1,0,2:T(8,128)(2,1)}, u32[]{:S(2)}, u32[]{:S(2)}) async-start(bf16[4,128,16,384]{3,1,0,2:T(8,128)(2,1)} %copy.91), calls=%async_computation | async-start | bytes 12582912 | tf_op jit(solution)/shard_map/all_to_all | solution.py:218
  244.7 548.6 %all-gather.11.cloned.1.call-start = ((), (), s32[]{:S(2)}) async-start(), calls=%async_computation.12 | async-start | bytes 23248896 | tf_op jit(solution)/shard_map/all_gather | solution.py:184
  542.0 4.9 copy-start.2
  542.0 101.3 %all-to-all-start.1 = ((bf16[4,1024,2,128]{3,2,0,1:T(2,128)(2,1)}), bf16[4,1024,2,128]{3,2,0,1:T(2,128)(2,1)}, u32[]{:S(2)}, u32[]{:S(2)}) async-start(bf16[4,1024,2,128]{3,2,0,1:T(2,128)(2,1)} %get-tuple-element.75), calls=%async_computation.1 | async-start | bytes 4194304 | tf_op jit(solution)/shard_map/all_to_all | solution.py:223
  546.8 246.4 %copy-start.16 = (f32[2048]{0:T(1024)}, f32[2048]{0:T(1024)S(1)}, u32[]{:S(2)}) copy-start(f32[2048]{0:T(1024)S(1)} %convert_element_type.143) | copy-start | bytes 24580
  546.9 352.8 %copy-start.9 = (f32[2048]{0:T(1024)}, f32[2048]{0:T(1024)S(1)}, u32[]{:S(2)}) copy-start(f32[2048]{0:T(1024)S(1)} %convert_element_type.142) | copy-start | bytes 24580
  662.0 237.7 %copy-start.14 = (f32[512]{0:T(512)}, f32[512]{0:T(512)S(1)}, u32[]{:S(2)}) copy-start(f32[512]{0:T(512)S(1)} %broadcast_multiply_fusion.5) | copy-start | bytes 6148
  664.6 235.1 %copy-start.18 = (f32[512]{0:T(512)}, f32[512]{0:T(512)S(1)}, u32[]{:S(2)}) copy-start(f32[512]{0:T(512)S(1)} %add_rsqrt_fusion.1) | copy-start | bytes 6148
  904.5 9.7 copy-start.5
  916.7 52.6 %all-to-all-start.2 = ((bf16[4,128,16,128]{3,1,0,2:T(8,128)(2,1)}), bf16[4,128,16,128]{3,1,0,2:T(8,128)(2,1)S(1)}, u32[]{:S(2)}, u32[]{:S(2)}) async-start(bf16[4,128,16,128]{3,1,0,2:T(8,128)(2,1)} %copy.96), calls=%async_computation.2 | async-start | bytes 4194304 | tf_op jit(solution)/shard_map/all_to_all | solution.py:289
  1089.7 143.7 %all-to-all-start.3 = ((bf16[4,1024,2,384]{3,2,0,1:T(2,128)(2,1)}), bf16[4,1024,2,384]{3,2,0,1:T(2,128)(2,1)}, u32[]{:S(2)}, u32[]{:S(2)}) async-start(bf16[4,1024,2,384]{3,2,0,1:T(2,128)(2,1)} %get-tuple-element.77), calls=%async_computation.3 | async-start | bytes 12582912 | tf_op jit(solution)/shard_map/all_to_all | solution.py:294
  1094.5 325.9 %all-reduce.18.cloned.1.call-start = ((), (), s32[]{:S(2)}) async-start(), calls=%async_computation.18 | async-start | bytes 237568
  1293.2 260.1 %reduce-scatter.6.cloned.1.call-start = ((), (), s32[]{:S(2)}) async-start(), calls=%async_computation.13 | async-start | bytes 1081344 | tf_op jit(solution)/shard_map/reduce_scatter | solution.py:330
  1293.3 22.4 copy-start.13
  1320.4 418.8 %reduce-scatter.10.cloned.1.call-start = ((), (), s32[]{:S(2)}) async-start(), calls=%async_computation.15 | async-start | bytes 17301504 | tf_op jit(solution)/shard_map/reduce_scatter | solution.py:332
  1330.8 844.6 %reduce-scatter.8.cloned.1.call-start = ((), (), s32[]{:S(2)}) async-start(), calls=%async_computation.14 | async-start | bytes 51904512 | tf_op jit(solution)/shard_map/reduce_scatter | solution.py:331
  1355.4 1302.8 %reduce-scatter.14.cloned.1.call-start = ((), (), s32[]{:S(2)}) async-start(), calls=%async_computation.17 | async-start | bytes 46497792 | tf_op jit(solution)/shard_map/reduce_scatter | solution.py:270
  1378.2 2228.4 %reduce-scatter.12.cloned.1.call-start = ((), (), s32[]{:S(2)}) async-start(), calls=%async_computation.16 | async-start | bytes 92995584 | tf_op jit(solution)/shard_map/reduce_scatter | solution.py:269
  (21 other events, 67.0 us)
Sparse Core Ops, SparseCore 0:
  11.0 161.5 all-gather.4
  175.6 77.1 all-gather.6
  255.6 393.7 all-gather.8
  652.1 141.0 all-gather.10
  1293.4 123.0 all-reduce.17
  1418.7 134.6 reduce-scatter.5
  1556.2 182.9 reduce-scatter.9
  1746.2 429.1 reduce-scatter.7
  2178.2 479.9 reduce-scatter.13
  2661.0 945.5 reduce-scatter.11
where the time goes:
time: 3620 us
  waiting for transfers between devices  2800 us (77%)
  matrix products  392 us (11%)
  local copies, waits for them, and re-layouts  170 us (5%)
  other arithmetic  128 us (4%)
  blocking collectives  90.5 us (2%)
    reduce_scatter x1, waiting for transfers between devices, on_device(): lax.psum_scatter(rear_terms[0], ('items', 'seq'), scatter_dimension=0, ti...  948 us
    reduce_scatter x1, waiting for transfers between devices, on_device(): lax.psum_scatter(rear_terms[1], ('items', 'seq'), scatter_dimension=1, ti...  483 us
    reduce_scatter x1, waiting for transfers between devices, on_device(): lax.psum_scatter(front_terms[1], ('items', 'seq'), scatter_dimension=0, t...  436 us
    all_to_all x1, waiting for transfers between devices, on_device(): lax.all_to_all(packed, 'seq', split_axis=2, concat_axis=1, tiled=True)  229 us
    reduce_scatter x1, waiting for transfers between devices, on_device(): lax.psum_scatter(front_terms[2], ('items', 'seq'), scatter_dimension=0, t...  184 us
    reduce_scatter x1, waiting for transfers between devices, on_device(): lax.psum_scatter(front_terms[0], ('items', 'seq'), scatter_dimension=0, t...  124 us
    all_to_all x1, waiting for transfers between devices, on_device(): lax.all_to_all(for_sending(grad_packed), 'seq', split_axis=1, concat_axis...  122 us
    dot_general x5, matrix products, contract_cols(): lax.dot_general(left, right, (((1,), (1,)), ((), ())), preferred_element_...  109 us
  transfers between devices with their start and end apart: 14, of which 11 were waited for; matrix products, arithmetic and copies ran while one was open for 11% of the time, Pallas kernels for 0%

commit v1 on v0

v1 whole, which is shorter than its diff:
```python
import math

import jax
import jax.numpy as jnp
from jax import lax
from jax.sharding import PartitionSpec as P

HEADS = 16
HEAD = 128


deep_alpha = math.sqrt(48.0)
epsilon = 1e-05
mask_token = 3
both = ("items", "seq")
bf16 = jnp.bfloat16
f32 = jnp.float32


def swap(part, axis, bit):
    return lax.ppermute(part, axis, [(j, j ^ bit) for j in range(lax.axis_size(axis))])


def bits_of(axis):
    found = []
    bit = 1
    while bit < lax.axis_size(axis):
        found.append((axis, bit))
        bit *= 2
    return found


def my_bit(axis, bit):
    return (lax.axis_index(axis) // bit) % 2


def in_order(own, got, place, dim):
    return jnp.where(
        place == 0, jnp.concatenate([own, got], axis=dim), jnp.concatenate([got, own], axis=dim)
    )


def pick(whole, place, dim):
    return lax.dynamic_index_in_dim(whole, place, dim, keepdims=False)


def gather_pieces(own, steps):
    pieces = [(0, 0, own)]
    for axis, bit in steps:
        pieces = pieces + [
            (
                mask_i ^ (bit if axis == "items" else 0),
                mask_s ^ (bit if axis == "seq" else 0),
                swap(piece, axis, bit),
            )
            for mask_i, mask_s, piece in pieces
        ]
    return pieces


def place_pieces(buffer, pieces, group, column):
    seq_size = lax.axis_size("seq")
    for mask_i, mask_s, piece in pieces:
        index = (
            (lax.axis_index("items") ^ mask_i) * seq_size + (lax.axis_index("seq") ^ mask_s)
        ) // group
        buffer = lax.dynamic_update_slice(buffer, piece[None], (index, 0, column))
    return buffer


def gather_merge(own, steps):
    for axis, bit in steps:
        own = in_order(own, swap(own, axis, bit), my_bit(axis, bit), 0)
    return own


def halve(whole, dim, axis, bit):
    place = my_bit(axis, bit)
    mine = pick(whole, place, dim)
    got = swap(pick(whole, 1 - place, dim), axis, bit)
    return (mine.astype(f32) + got.astype(f32)).astype(whole.dtype)


def butterfly(part, steps):
    for axis, bit in steps:
        part = part + swap(part, axis, bit)
    return part


def member_exchange(parts):
    for dim, bit in ((0, 2), (1, 1)):
        place = my_bit("seq", bit)
        mine = jnp.expand_dims(pick(parts, place, dim), dim)
        got = jnp.expand_dims(swap(pick(parts, 1 - place, dim), "seq", bit), dim)
        parts = in_order(mine, got, place, dim)
    return parts


def gather_four(own):
    far = swap(own, "seq", 2)
    near = swap(own, "seq", 1)
    return jnp.concatenate([own, near, far, swap(far, "seq", 1)], axis=0)


def sum_four(parts):
    own, near, far, cross = jnp.split(parts, 4, axis=0)
    far = (far.astype(f32) + swap(cross, "seq", 1).astype(f32)).astype(bf16)
    own = own.astype(f32) + swap(near, "seq", 1).astype(f32)
    return own + swap(far, "seq", 2).astype(f32)


def contract_rows(left, right):
    return lax.dot_general(
        left, right, (((0,), (0,)), ((), ())), preferred_element_type=f32
    )


def contract_cols(left, right):
    return lax.dot_general(
        left, right, (((1,), (1,)), ((), ())), preferred_element_type=f32
    )


def dot(left, right):
    return jnp.dot(left, right, preferred_element_type=f32)


def rotate(values, cosine, sine_part):
    half_width = values.shape[-1] // 2
    first = values[..., :half_width]
    second = values[..., half_width:]
    cosine = cosine[:, None, :]
    sine_part = sine_part[:, None, :]
    return jnp.concatenate(
        [first * cosine - second * sine_part, second * cosine + first * sine_part], axis=-1
    )


def norm_forward(residual, gain_vec, bias_vec):
    center = residual - jnp.mean(residual, axis=-1, keepdims=True)
    inverse = lax.rsqrt(jnp.mean(center * center, axis=-1, keepdims=True) + epsilon)
    normed = center * inverse
    return (normed * gain_vec + bias_vec, normed, inverse)


def norm_backward(grad_out, normed, inverse, gain_vec):
    scaled = grad_out * gain_vec
    grad_in = inverse * (
        scaled
        - jnp.mean(scaled, axis=-1, keepdims=True)
        - normed * jnp.mean(scaled * normed, axis=-1, keepdims=True)
    )
    return (grad_in, jnp.sum(grad_out * normed, axis=0), jnp.sum(grad_out, axis=0))


def visible_mask(offset, block_rows, total_length, visible):
    query_pos = offset + jnp.arange(block_rows, dtype=jnp.int32)[:, None]
    key_pos = jnp.arange(total_length, dtype=jnp.int32)[None, :]
    return (key_pos <= query_pos) | (key_pos < visible)


def block_scores(query_block, keys_all, offset, visible):
    block_rows = query_block.shape[0]
    total_length = keys_all.shape[0]
    scores = jnp.einsum(
        "qhd,khd->hqk", query_block, keys_all, preferred_element_type=f32
    ) * HEAD ** (-0.5)
    return jnp.where(
        visible_mask(offset, block_rows, total_length, visible)[None], scores, -jnp.inf
    )


def attend(unit, visible):
    total_length = unit.shape[0]
    block_rows = min(512, total_length)
    queries = unit[..., :HEAD]
    keys_all = unit[..., HEAD : 2 * HEAD]
    values = unit[..., 2 * HEAD :]
    contexts = []
    log_sums = []
    for offset in range(0, total_length, block_rows):
        scores = block_scores(queries[offset : offset + block_rows], keys_all, offset, visible)
        row_peak = jnp.max(scores, axis=-1, keepdims=True)
        expos = jnp.exp(scores - row_peak)
        row_total = jnp.sum(expos, axis=-1, keepdims=True)
        weights_low = (expos / row_total).astype(bf16)
        contexts.append(
            jnp.einsum(
                "hqk,khd->qhd", weights_low, values, preferred_element_type=f32
            ).astype(bf16)
        )
        log_sums.append((row_peak + jnp.log(row_total))[..., 0])
    return (jnp.concatenate(contexts, axis=0), jnp.concatenate(log_sums, axis=1))


def attend_back(unit, grad_context, log_sums, visible):
    total_length = unit.shape[0]
    block_rows = min(512, total_length)
    queries = unit[..., :HEAD]
    keys_all = unit[..., HEAD : 2 * HEAD]
    values = unit[..., 2 * HEAD :]
    grad_queries = []
    grad_keys = jnp.zeros(keys_all.shape, f32)
    grad_values = jnp.zeros(values.shape, f32)
    for offset in range(0, total_length, block_rows):
        query_block = queries[offset : offset + block_rows]
        grad_block = grad_context[offset : offset + block_rows]
        scores = block_scores(query_block, keys_all, offset, visible)
        weights = jnp.exp(scores - log_sums[:, offset : offset + block_rows, None])
        weights_low = weights.astype(bf16)
        grad_values = grad_values + jnp.einsum(
            "hqk,qhd->khd", weights_low, grad_block, preferred_element_type=f32
        )
        grad_weights = jnp.einsum(
            "qhd,khd->hqk", grad_block, values, preferred_element_type=f32
        )
        inner = jnp.sum(weights * grad_weights, axis=-1, keepdims=True)
        grad_scores = (weights * (grad_weights - inner)).astype(bf16)
        grad_queries.append(
            jnp.einsum("hqk,khd->qhd", grad_scores, keys_all, preferred_element_type=f32)
            * HEAD ** (-0.5)
        )
        grad_keys = grad_keys + jnp.einsum(
            "hqk,qhd->khd", grad_scores, query_block, preferred_element_type=f32
        ) * HEAD ** (-0.5)
    return jnp.concatenate(
        [jnp.concatenate(grad_queries, axis=0), grad_keys, grad_values], axis=-1
    ).astype(bf16)


def on_device(
    token_ids,
    masked,
    item_flag,
    prefix,
    cotangent,
    embedding,
    heads_weight,
    heads_bias,
    dense_weight,
    dense_bias,
    first_gain,
    first_bias,
    up_weight,
    up_bias,
    down_weight,
    down_bias,
    second_gain,
    second_bias,
):
    items_here, span = token_ids.shape
    items_size, seq_size = lax.axis_size("items"), lax.axis_size("seq")
    item_place, seq_place = lax.axis_index("items"), lax.axis_index("seq")
    count = items_size * seq_size
    length = span * seq_size
    local_rows = items_here * span
    width = embedding.shape[0] * count
    vocab = embedding.shape[1]
    heads_here = HEADS // seq_size
    packed_width = heads_here * 3 * HEAD
    weight_rows = up_weight.shape[0]
    ff_width = down_weight.shape[0]
    members = 4
    groups = count // members
    member = seq_place % members
    ff_part = -(-ff_width // (members * 128)) * 128

    item_bits, seq_bits = bits_of("items"), bits_of("seq")
    outer_bits = seq_bits[2:]

    input_ids = jnp.where(masked == 1, mask_token, token_ids)
    small = [
        embedding.reshape(-1),
        input_ids.astype(bf16).reshape(-1),
        heads_bias,
        dense_bias,
        first_gain,
        first_bias,
        down_bias,
        second_gain,
        second_bias,
    ]
    ends = [0]
    for part in small:
        ends.append(ends[-1] + part.shape[0])
    flat = jnp.concatenate(small)
    flat = jnp.pad(flat, (0, -flat.shape[0] % 1024)).reshape(1, -1, 128)
    everyone = lax.all_gather(flat, both, axis=0, tiled=True).reshape(count, -1)
    pieces = [everyone[:, a:b] for a, b in zip(ends[:-1], ends[1:])]
    table = pieces[0].reshape(width, vocab)
    ids_here = pick(pieces[1].reshape(items_size, seq_size, items_here, span), item_place, 0)
    ids_here = jnp.transpose(ids_here, (1, 0, 2)).reshape(items_here, length).astype(jnp.int32)
    b_heads, b_dense, gain_one, shift_one, b_down, gain_two, shift_two = (
        part.reshape(-1).astype(f32) for part in pieces[2:]
    )

    w_block = lax.all_to_all(
        jnp.transpose(heads_weight.reshape(weight_rows, seq_size, packed_width), (1, 0, 2)),
        "seq",
        split_axis=0,
        concat_axis=0,
        tiled=True,
    ).reshape(seq_size * weight_rows, packed_width)
    table_block = lax.dynamic_slice_in_dim(
        table, item_place * seq_size * weight_rows, seq_size * weight_rows, 0
    )
    mixed_table = butterfly(contract_rows(table_block, w_block), item_bits)
    mixed_table = mixed_table + lax.dynamic_slice_in_dim(
        b_heads, seq_place * packed_width, packed_width, 0
    )

    def by_member(part):
        padded = jnp.pad(part, ((0, 0), (0, members * ff_part - ff_width)))
        parts = jnp.transpose(padded.reshape(weight_rows, 2, 2, ff_part), (1, 2, 0, 3))
        return member_exchange(parts).reshape(members * weight_rows, ff_part)

    w_dense = dense_weight
    w_dense = gather_merge(w_dense, seq_bits[1:][::-1][::-1])
    dense_pieces = gather_pieces(w_dense, item_bits[1:] + item_bits[:1] + seq_bits[:1])
    dense_buffer = jnp.zeros((items_size, 2, seq_size // 2, weight_rows, width), bf16)
    for mask_i, mask_s, piece in dense_pieces:
        dense_buffer = lax.dynamic_update_slice(
            dense_buffer,
            piece.reshape(1, 1, seq_size // 2, weight_rows, width),
            (item_place ^ mask_i, (seq_place ^ mask_s) % 2, 0, 0, 0),
        )
    w_dense = jnp.transpose(dense_buffer, (0, 2, 1, 3, 4)).reshape(width, width)

    order_a = outer_bits + item_bits[:1] + item_bits[1:]
    order_b = outer_bits + item_bits[1:] + item_bits[:1]
    w_in = jnp.zeros((groups, members * weight_rows, 2 * ff_part), bf16)
    w_in = place_pieces(
        w_in, gather_pieces(by_member(up_weight[:, :ff_width]), order_a), members, 0
    )
    w_in = place_pieces(
        w_in, gather_pieces(by_member(up_weight[:, ff_width:]), order_b), members, ff_part
    )
    w_in = w_in.reshape(width, 2 * ff_part)
    w_out = jnp.zeros((2 * groups, members * weight_rows // 2, ff_part), bf16)
    out_first, out_second = jnp.split(by_member(down_weight.T), 2, axis=0)

    def place_half(buffer, found, which):
        for mask_i, mask_s, piece in found:
            index = ((item_place ^ mask_i) * seq_size + (seq_place ^ mask_s)) // members
            buffer = lax.dynamic_update_slice(buffer, piece[None], (2 * index + which, 0, 0))
        return buffer

    w_out = place_half(w_out, gather_pieces(out_first, order_a), 0)
    w_out = place_half(w_out, gather_pieces(out_second, order_b), 1)
    w_out = w_out.reshape(width, ff_part)
    in_bias = jnp.pad(
        up_bias.astype(f32).reshape(2, ff_width), ((0, 0), (0, members * ff_part - ff_width))
    )
    in_bias = lax.dynamic_slice(in_bias, (0, member * ff_part), (2, ff_part)).reshape(-1)

    vocab_index = jnp.arange(vocab, dtype=jnp.int32)
    positions = jnp.arange(length, dtype=f32)
    frequency = jnp.exp(
        jnp.arange(HEAD // 2, dtype=f32) * (-2.0 * math.log(10000.0) / HEAD)
    )
    angles = positions[:, None] * frequency[None, :]
    cosine, sine_part = jnp.cos(angles), jnp.sin(angles)
    visible = jnp.where(item_flag == 1, length, prefix)
    packed, log_sums, onehots, context_rows = [], [], [], []
    for item in range(items_here):
        onehot = (ids_here[item][:, None] == vocab_index[None, :]).astype(bf16)
        mixed = jnp.dot(onehot.astype(f32), mixed_table, precision=lax.Precision.HIGHEST).reshape(
            length, heads_here, 3 * HEAD
        )
        unit = jnp.concatenate(
            [
                rotate(mixed[..., :HEAD], cosine, sine_part),
                rotate(mixed[..., HEAD : 2 * HEAD], cosine, sine_part),
                mixed[..., 2 * HEAD :],
            ],
            axis=-1,
        ).astype(bf16)
        context, log_sum = attend(unit, visible[item])
        onehots.append(onehot)
        packed.append(unit)
        log_sums.append(log_sum)
        rows = lax.all_to_all(
            context.reshape(seq_size, span, heads_here * HEAD),
            "seq",
            split_axis=0,
            concat_axis=0,
            tiled=True,
        )
        context_rows.append(jnp.transpose(rows, (1, 0, 2)).reshape(span, HEADS * HEAD))

    halves = 2 if items_here % 2 == 0 else 1
    per_half = items_here // halves
    kept = []
    for half in range(halves):
        chosen = range(half * per_half, (half + 1) * per_half)
        context = jnp.concatenate([context_rows[item] for item in chosen], axis=0)
        own_ids = input_ids[half * per_half : (half + 1) * per_half].reshape(-1)
        onehot = (own_ids[:, None] == vocab_index[None, :]).astype(bf16)
        inputs = contract_cols(onehot, table)
        branch = dot(context, w_dense) + b_dense
        hidden, normed_one, inverse_one = norm_forward(
            deep_alpha * inputs + branch, gain_one, shift_one
        )
        shared = gather_four(hidden.astype(bf16))
        gate_up = dot(shared, w_in) + in_bias
        up_part, gate = gate_up[:, :ff_part], gate_up[:, ff_part:]
        below = 0.5 * (1.0 + lax.erf(gate * (0.5**0.5)))
        activated = gate * below
        slope = below + gate * jnp.exp(-0.5 * gate * gate) * (1.0 / math.sqrt(2.0 * math.pi))
        product_low = (up_part * activated).astype(bf16)
        act_low = activated.astype(bf16)
        slope_low = (up_part * slope).astype(bf16)
        mlp_branch = sum_four(contract_cols(product_low, w_out).astype(bf16)) + b_down
        layer_out, normed_two, inverse_two = norm_forward(
            deep_alpha * hidden + mlp_branch, gain_two, shift_two
        )
        grad_top = (
            cotangent[half * per_half : (half + 1) * per_half]
            .reshape(per_half * span, width)
            .astype(f32)
        )
        grad_resid_two, grad_gain_two, grad_shift_two = norm_backward(
            grad_top, normed_two, inverse_two, gain_two
        )
        grad_mlp_low = grad_resid_two.astype(bf16)
        grad_shared = gather_four(grad_mlp_low)
        grad_product = dot(grad_shared, w_out)
        grad_in_low = jnp.concatenate(
            [grad_product * act_low.astype(f32), grad_product * slope_low.astype(f32)], axis=1
        ).astype(bf16)
        grad_hidden = (
            sum_four(contract_cols(grad_in_low, w_in).astype(bf16)) + deep_alpha * grad_resid_two
        )
        grad_resid_one, grad_gain_one, grad_shift_one = norm_backward(
            grad_hidden, normed_one, inverse_one, gain_one
        )
        grad_branch_low = grad_resid_one.astype(bf16)
        grad_context = contract_cols(grad_branch_low, w_dense).astype(bf16)
        kept.append(
            dict(
                layer_out=layer_out.astype(bf16),
                context=context,
                shared=shared,
                product=product_low,
                grad_shared=grad_shared,
                grad_in=grad_in_low,
                grad_branch=grad_branch_low,
                grad_resid_one=grad_resid_one,
                grad_context=grad_context,
                vectors=jnp.stack(
                    [
                        grad_gain_one,
                        grad_shift_one,
                        jnp.sum(grad_branch_low.astype(f32), axis=0),
                        grad_gain_two,
                        grad_shift_two,
                        jnp.sum(grad_mlp_low.astype(f32), axis=0),
                    ]
                ),
                in_sum=jnp.sum(grad_in_low.astype(f32), axis=0),
                token_sum=lax.dot_general(
                    grad_resid_one,
                    onehot.astype(f32),
                    (((0,), (0,)), ((), ())),
                    precision=lax.Precision.HIGHEST,
                    preferred_element_type=f32,
                ),
            )
        )

    def total(function):
        result = function(kept[0])
        for one in kept[1:]:
            result = result + function(one)
        return result

    def to_owner(whole, order):
        dims = [("items", bit) for _, bit in item_bits[::-1]] + outer_bits[::-1]
        whole = whole.reshape((2,) * len(dims) + (members * weight_rows, -1))
        for step in order[::-1]:
            place = dims.index(step)
            whole = halve(whole, place, *step)
            dims.pop(place)
        return whole

    grad_in_weight = total(lambda one: contract_rows(one["shared"], one["grad_in"])).astype(bf16)
    grad_out_weight = total(lambda one: contract_rows(one["grad_shared"], one["product"])).astype(
        bf16
    )
    sums = [
        to_owner(grad_in_weight[:, :ff_part], order_a),
        to_owner(grad_in_weight[:, ff_part:], order_b),
        to_owner(grad_out_weight, order_a),
    ]

    def from_members(part):
        parts = member_exchange(part.reshape(2, 2, weight_rows, ff_part))
        parts = jnp.transpose(parts, (2, 0, 1, 3)).reshape(weight_rows, members * ff_part)
        return parts[:, :ff_width].astype(f32)

    grad_up, grad_gate, grad_down = (from_members(part) for part in sums)

    def sum_rows(whole):
        dims = item_bits[::-1] + seq_bits[::-1]
        whole = whole.reshape((2,) * len(dims) + (weight_rows, -1))
        for step in seq_bits[:1] + item_bits + seq_bits[1:]:
            place = dims.index(step)
            whole = halve(whole, place, *step)
            dims.pop(place)
        return whole

    grad_dense = sum_rows(
        total(lambda one: contract_rows(one["context"], one["grad_branch"])).astype(bf16)
    ).astype(f32)
    token_sum = sum_rows(total(lambda one: one["token_sum"]))

    in_sum = total(lambda one: one["in_sum"]).reshape(2, ff_part)
    in_all = lax.dynamic_update_slice(
        jnp.zeros((2, members * ff_part), f32), in_sum, (0, member * ff_part)
    )
    vectors = jnp.concatenate([total(lambda one: one["vectors"]).reshape(-1), in_all.reshape(-1)])
    vectors = jnp.pad(vectors, (0, -vectors.shape[0] % 1024)).reshape(-1, 128)
    vectors = butterfly(vectors, seq_bits + item_bits).reshape(-1)
    in_all = vectors[6 * width :][: 2 * members * ff_part].reshape(2, members * ff_part)
    grad_up_bias = in_all[:, :ff_width].reshape(-1)
    vectors = vectors[: 6 * width].reshape(6, count, weight_rows)
    own_vectors = pick(vectors, item_place * seq_size + seq_place, 1)

    w_slices = jnp.zeros((items_size, seq_size * weight_rows, packed_width), bf16)
    w_slices = place_pieces(w_slices, gather_pieces(w_block, item_bits), seq_size, 0)
    w_slice = w_slices.reshape(width, packed_width)
    token_mixed = jnp.zeros((vocab, packed_width), f32)
    input_grads = []
    for item in range(items_here):
        half, row = item // per_half, (item % per_half) * span
        grad_context = kept[half]["grad_context"][row : row + span]
        grad_context = lax.all_to_all(
            jnp.transpose(grad_context.reshape(span, seq_size, heads_here * HEAD), (1, 0, 2)),
            "seq",
            split_axis=0,
            concat_axis=0,
            tiled=True,
        ).reshape(length, heads_here, HEAD)
        grad_packed = attend_back(packed[item], grad_context, log_sums[item], visible[item])
        grad_packed = grad_packed.astype(f32)
        grad_mixed = jnp.concatenate(
            [
                rotate(grad_packed[..., :HEAD], cosine, -sine_part),
                rotate(grad_packed[..., HEAD : 2 * HEAD], cosine, -sine_part),
                grad_packed[..., 2 * HEAD :],
            ],
            axis=-1,
        )
        grad_mixed = grad_mixed.reshape(length, packed_width).astype(bf16)
        token_mixed = token_mixed + contract_rows(onehots[item], grad_mixed)
        part = contract_cols(grad_mixed, w_slice).astype(bf16).reshape(seq_size, span, width)
        for step in seq_bits:
            part = halve(part.reshape(-1, 2, span, width), 1, *step)
        input_grads.append(
            part.reshape(span, width).astype(f32)
            + deep_alpha * kept[half]["grad_resid_one"][row : row + span]
        )

    token_mixed = butterfly(token_mixed, item_bits)
    token_all = token_mixed[None]
    token_all = gather_merge(token_all, seq_bits)
    token_all = jnp.transpose(token_all, (1, 0, 2)).reshape(vocab, -1)
    grad_heads = jnp.dot(embedding.astype(f32), token_all, precision=lax.Precision.HIGHEST)
    grad_heads_bias = lax.dynamic_slice_in_dim(
        jnp.sum(token_all, axis=0),
        (item_place * seq_size + seq_place) * heads_bias.shape[0],
        heads_bias.shape[0],
        0,
    )
    embed_grad = 0.1 * (
        lax.dot_general(
            heads_weight.astype(f32),
            token_all,
            (((1,), (1,)), ((), ())),
            precision=lax.Precision.HIGHEST,
            preferred_element_type=f32,
        )
        + deep_alpha * token_sum
    )
    return (
        jnp.concatenate([one["layer_out"] for one in kept], axis=0).reshape(
            items_here, span, width
        ),
        jnp.stack(input_grads),
        embed_grad,
        grad_heads,
        grad_heads_bias,
        grad_dense,
        own_vectors[2],
        own_vectors[0],
        own_vectors[1],
        jnp.concatenate([grad_up, grad_gate], axis=1),
        grad_up_bias,
        grad_down.T,
        own_vectors[5],
        own_vectors[3],
        own_vectors[4],
    )


def solution(mesh):
    in_specs = (
        P("items", "seq"),
        P("items", "seq"),
        P("items"),
        P("items"),
        P("items", "seq", None),
        P(("items", "seq"), None),
        P(("items", "seq"), None),
        P(("items", "seq")),
        P(("items", "seq"), None),
        P(("items", "seq")),
        P(("items", "seq")),
        P(("items", "seq")),
        P(("items", "seq"), None),
        P(),
        P(None, ("items", "seq")),
        P(("items", "seq")),
        P(("items", "seq")),
        P(("items", "seq")),
    )
    out_specs = (
        P("items", "seq", None),
        P("items", "seq", None),
        P(("items", "seq"), None),
        P(("items", "seq"), None),
        P(("items", "seq")),
        P(("items", "seq"), None),
        P(("items", "seq")),
        P(("items", "seq")),
        P(("items", "seq")),
        P(("items", "seq"), None),
        P(),
        P(None, ("items", "seq")),
        P(("items", "seq")),
        P(("items", "seq")),
        P(("items", "seq")),
    )
    return jax.shard_map(
        on_device, mesh=mesh, in_specs=in_specs, out_specs=out_specs, check_vma=False
    )
```

time: 3620 us -> 1730 us (0.48)
  waiting for transfers between devices: 2800 us -> 636 us
  local copies, waits for them, and re-layouts: 170 us -> 333 us
  starting transfers between devices: 18.6 us -> 137 us
  other arithmetic: 128 us -> 178 us
    reduce_scatter x5 -> x0, waiting for transfers between devices: 2180 us -> none  [the longest x1 948 us: on_device(): lax.psum_scatter(rear_terms[0], ('items', 'seq'), scatter_dimension=0, ti...]
    ppermute x0 -> x119, waiting for transfers between devices: none -> 615 us  [swap(): lax.ppermute(part, axis, [(j, j ^ bit) for j in range(lax.axis_size(axis))])]
    all_to_all x4 -> x9, waiting for transfers between devices: 496 us -> 20.9 us  [the longest x4 16 us: on_device(): lax.all_to_all(context.reshape(seq_size, span, heads_here * HEAD), 'seq',...]
    all_gather x4 -> x0, waiting for transfers between devices: 125 us -> none  [the longest x1 64.5 us: on_device(): lax.all_gather(down_weight, ('items', 'seq'), axis=1, tiled=True)]
    ppermute x0 -> x119, starting transfers between devices: none -> 97.8 us  [swap(): lax.ppermute(part, axis, [(j, j ^ bit) for j in range(lax.axis_size(axis))])]
    unnamed x78 -> x645, local copies, waits for them, and re-layouts: 34.1 us -> 89 us
    slice x6 -> x40, local copies, waits for them, and re-layouts: 7.85 us -> 56 us  [the longest x20 32.3 us: attend_back(): grad_block = grad_context[offset:offset + block_rows]]
    unnamed x1 -> x0, blocking collectives: 44.1 us -> none
  transfers between devices with their start and end apart: 14 -> 128, of which waited for: 11 -> 46; matrix products, arithmetic and copies ran while one was open for 11% -> 48% of each run, Pallas kernels for 0% -> 0%
where the time goes in v1:
time: 1730 us
  waiting for transfers between devices  636 us (37%)
  matrix products  373 us (22%)
  local copies, waits for them, and re-layouts  333 us (19%)
  other arithmetic  178 us (10%)
  starting transfers between devices  137 us (8%)
  blocking collectives  63.2 us (4%)
    ppermute x119, waiting for transfers between devices, swap(): lax.ppermute(part, axis, [(j, j ^ bit) for j in range(lax.axis_size(axis))])  615 us
    dot_general x12, matrix products, contract_cols(): lax.dot_general(left, right, (((1,), (1,)), ((), ())), preferred_element_...  97.9 us
    ppermute x119, starting transfers between devices, swap(): lax.ppermute(part, axis, [(j, j ^ bit) for j in range(lax.axis_size(axis))])  97.8 us
    unnamed x645, local copies, waits for them, and re-layouts  89 us
    dot_general x11, matrix products, contract_rows(): lax.dot_general(left, right, (((0,), (0,)), ((), ())), preferred_element_...  85.5 us
    dot_general x6, matrix products, dot(): return jnp.dot(left, right, preferred_element_type=f32)  79.3 us
    all_gather x1, blocking collectives, on_device(): everyone = lax.all_gather(flat, both, axis=0, tiled=True).reshape(count, -1)  63.2 us
  transfers between devices with their start and end apart: 128, of which 46 were waited for; matrix products, arithmetic and copies ran while one was open for 48% of the time, Pallas kernels for 0%

profile of v1, /device:TPU:0, one launch (start us, length us, event | category | flops | bytes accessed | tf_op | source)
XLA Modules:
  0.0 1725.8 jit_solution(9373486220918092275)
XLA Ops:
  21.6 63.2 %all_gather.3 = bf16[32,80,128]{2,1,0:T(8,128)(2,1)S(1)} all-gather(bf16[1,80,128]{2,1,0:T(8,128)(2,1)S(1)} %pad_bitcast_fusion), channel_id=1, replica_groups=mesh['items'=4,'seq'=8] {'items','seq'}, dimensions={0}, use_global_device_ids=true | all-gather | bytes 675840 | tf_op jit(solution)/shard_map/all_gather | solution.py:288
  224.9 25.8 %collective-permute-done.43 = bf16[128,1408]{1,0:T(8,128)(2,1)S(1)} collective-permute-done((bf16[128,1408]{1,0:T(8,128)(2,1)S(1)}, bf16[128,1408]{1,0:T(8,128)(2,1)S(1)}, u32[]{:S(2)}, u32[]{:S(2)}) %collective-permute-start.43) | collective-permute-done | bytes 360480 | tf_op jit(solution)/shard_map/ppermute | solution.py:21
  254.3 27.7 %collective-permute-done.45 = bf16[128,1408]{1,0:T(8,128)(2,1)S(1)} collective-permute-done((bf16[128,1408]{1,0:T(8,128)(2,1)S(1)}, bf16[128,1408]{1,0:T(8,128)(2,1)S(1)}, u32[]{:S(2)}, u32[]{:S(2)}) %collective-permute-start.45) | collective-permute-done | bytes 360480 | tf_op jit(solution)/shard_map/ppermute | solution.py:21
  554.7 17.9 %collective-permute-done.12 = bf16[256,2048]{1,0:T(8,128)(2,1)S(1)} collective-permute-done((bf16[256,2048]{1,0:T(8,128)(2,1)S(1)}, bf16[256,2048]{1,0:T(8,128)(2,1)S(1)}, u32[]{:S(2)}, u32[]{:S(2)}) %collective-permute-start.12) | collective-permute-done | bytes 1048608 | tf_op jit(solution)/shard_map/ppermute | solution.py:21
  595.7 17.2 convolution_add_fusion.1
  629.6 18.9 %convolution_add_fusion = f32[1024,2816]{1,0:T(8,128)S(1)} fusion(bf16[2048,2816]{1,0:T(8,128)(2,1)} %bitcast.62, f32[2816]{0:T(1024)S(1)} %copy-done.266, bf16[256,2048]{1,0:T(8,128)(2,1)} %collective-permute-done.53, bf16[256,2048]{1,0:T(8,128)(2,1)} %collective-permute-done.52, bf16[256,2048]{1,0:T(8,128)(2,1)} %collective-permute-done.51, ...), kind=kOutput, calls=%fused_computation.10 | convolution fusion | flops 11830820864 | bytes 27274240 | tf_op jit(solution)/shard_map/dot_general | solution.py:125
  695.6 21.6 %collective-permute-done.56 = bf16[256,2048]{1,0:T(8,128)(2,1)S(1)} collective-permute-done((bf16[256,2048]{1,0:T(8,128)(2,1)S(1)}, bf16[256,2048]{1,0:T(8,128)(2,1)S(1)}, u32[]{:S(2)}, u32[]{:S(2)}) %collective-permute-start.56) | collective-permute-done | bytes 1048608 | tf_op jit(solution)/shard_map/ppermute | solution.py:21
  733.4 19.3 %collective-permute-done.73 = bf16[256,2048]{1,0:T(8,128)(2,1)S(1)} collective-permute-done((bf16[256,2048]{1,0:T(8,128)(2,1)S(1)}, bf16[256,2048]{1,0:T(8,128)(2,1)S(1)}, u32[]{:S(2)}, u32[]{:S(2)}) %collective-permute-start.73) | collective-permute-done | bytes 1048608 | tf_op jit(solution)/shard_map/ppermute | solution.py:21
  757.2 16.2 collective-permute-done.58
  788.8 16.9 convolution_convert_fusion
  807.9 15.8 multiply_convert_fusion.3
  825.3 16.0 convolution_convert_fusion.1
  845.9 18.3 %fusion.104 = f32[2048,2816]{1,0:T(8,128)} fusion(bf16[1024,1408]{1,0:T(8,128)(2,1)S(1)} %copy-done.137, bf16[1024,1408]{1,0:T(8,128)(2,1)S(1)} %get-tuple-element.55, bf16[256,2048]{1,0:T(8,128)(2,1)} %collective-permute-done.53, bf16[256,2048]{1,0:T(8,128)(2,1)} %collective-permute-done.52, bf16[256,2048]{1,0:T(8,128)(2,1)} %collective-permute-done.51, ...), kind=kOutput, calls=%fused_computation.257 | convolution fusion | flops 11839471616 | bytes 33030144 | tf_op jit(solution)/shard_map/dot_general | solution.py:113
  864.2 20.5 %add_convert_fusion = bf16[2048,2816]{1,0:T(8,128)(2,1)} fusion(f32[2048,2816]{1,0:T(8,128)} %fusion.104, bf16[1024,1408]{1,0:T(8,128)(2,1)} %get-tuple-element.54, bf16[1024,1408]{1,0:T(8,128)(2,1)} %copy-done.139, bf16[256,2048]{1,0:T(8,128)(2,1)} %copy-done.291, bf16[256,2048]{1,0:T(8,128)(2,1)} %copy-done.289, bf16[256,2048]{1,0:T(8,128)(2,1)} %copy-done.290, ...), kind=kOutput, calls=%fused_computation | convolution fusion | flops 11851005952 | bytes 44564480 | tf_op jit(solution)/shard_map/dot_general | solution.py:113
  937.6 17.3 %collective-permute-done.62 = bf16[256,2048]{1,0:T(8,128)(2,1)S(1)} collective-permute-done((bf16[256,2048]{1,0:T(8,128)(2,1)S(1)}, bf16[256,2048]{1,0:T(8,128)(2,1)S(1)}, u32[]{:S(2)}, u32[]{:S(2)}) %collective-permute-start.62) | collective-permute-done | bytes 1048608 | tf_op jit(solution)/shard_map/ppermute | solution.py:21
  959.6 17.1 collective-permute-done.77
  1310.3 26.5 %collective-permute-done.105 = bf16[2,256,1408]{2,1,0:T(8,128)(2,1)S(1)} collective-permute-done((bf16[2,256,1408]{2,1,0:T(8,128)(2,1)S(1)}, bf16[2,256,1408]{2,1,0:T(8,128)(2,1)S(1)}, u32[]{:S(2)}, u32[]{:S(2)}) %collective-permute-start.105) | collective-permute-done | bytes 1441824 | tf_op jit(solution)/shard_map/ppermute | solution.py:21
  1341.6 45.6 %collective-permute-done.116 = bf16[256,1408]{1,0:T(8,128)(2,1)S(1)} collective-permute-done((bf16[256,1408]{1,0:T(8,128)(2,1)S(1)}, bf16[256,1408]{1,0:T(8,128)(2,1)S(1)}, u32[]{:S(2)}, u32[]{:S(2)}) %collective-permute-start.116) | collective-permute-done | bytes 720928 | tf_op jit(solution)/shard_map/ppermute | solution.py:21
  1389.6 28.4 %collective-permute-done.111 = bf16[256,1408]{1,0:T(8,128)(2,1)S(1)} collective-permute-done((bf16[256,1408]{1,0:T(8,128)(2,1)S(1)}, bf16[256,1408]{1,0:T(8,128)(2,1)S(1)}, u32[]{:S(2)}, u32[]{:S(2)}) %collective-permute-start.111) | collective-permute-done | bytes 720928 | tf_op jit(solution)/shard_map/ppermute | solution.py:21
  1448.7 35.6 %collective-permute-done.117 = bf16[2,64,1408]{2,0,1:T(2,128)(2,1)S(1)} collective-permute-done((bf16[2,64,1408]{2,0,1:T(2,128)(2,1)S(1)}, bf16[2,64,1408]{2,0,1:T(2,128)(2,1)S(1)}, u32[]{:S(2)}, u32[]{:S(2)}) %collective-permute-start.117) | collective-permute-done | bytes 360480 | tf_op jit(solution)/shard_map/ppermute | solution.py:21
  1496.2 22.1 %collective-permute-done.107 = bf16[2,64,1408]{2,0,1:T(2,128)(2,1)S(1)} collective-permute-done((bf16[2,64,1408]{2,0,1:T(2,128)(2,1)S(1)}, bf16[2,64,1408]{2,0,1:T(2,128)(2,1)S(1)}, u32[]{:S(2)}, u32[]{:S(2)}) %collective-permute-start.107) | collective-permute-done | bytes 360480 | tf_op jit(solution)/shard_map/ppermute | solution.py:21
  1557.4 15.3 collective-permute-done.82
  1597.8 30.6 %collective-permute-done.70 = bf16[2,128,2048]{2,1,0:T(8,128)(2,1)S(1)} collective-permute-done((bf16[2,128,2048]{2,1,0:T(8,128)(2,1)S(1)}, bf16[2,128,2048]{2,1,0:T(8,128)(2,1)S(1)}, u32[]{:S(2)}, u32[]{:S(2)}) %collective-permute-start.70) | collective-permute-done | bytes 1048608 | tf_op jit(solution)/shard_map/ppermute | solution.py:21
  1656.3 20.7 %collective-permute-done.83 = bf16[1,128,2048]{2,1,0:T(8,128)(2,1)} collective-permute-done((bf16[1,128,2048]{2,1,0:T(8,128)(2,1)}, bf16[1,128,2048]{2,1,0:T(8,128)(2,1)}, u32[]{:S(2)}, u32[]{:S(2)}) %collective-permute-start.83) | collective-permute-done | bytes 524320 | tf_op jit(solution)/shard_map/ppermute | solution.py:21
  (1329 shorter events, 1145.6 us)
Async XLA Ops:
  0.7 103.1 %collective-permute-start.2 = (bf16[64,2048]{1,0:T(8,128)(2,1)}, bf16[64,2048]{1,0:T(8,128)(2,1)}, u32[]{:S(2)}, u32[]{:S(2)}) collective-permute-start(bf16[64,2048]{1,0:T(8,128)(2,1)} %param.26), channel_id=1, source_target_pairs={{0,2},{1,3},{2,0},{3,1},{4,6},{5,7},{6,4},{7,5},{8,10},{9,11},{10,... | collective-permute-start | bytes 786440 | tf_op jit(solution)/shard_map/ppermute | solution.py:21
  6.0 175.3 %all-to-all-start = ((bf16[8,64,768]{2,1,0:T(8,128)(2,1)}), bf16[8,64,768]{2,1,0:T(8,128)(2,1)S(1)}, u32[]{:S(2)}, u32[]{:S(2)}) async-start(bf16[8,64,768]{2,1,0:T(8,128)(2,1)} %copy.358), calls=%async_computation | async-start | bytes 1572864 | tf_op jit(solution)/shard_map/all_to_all | solution.py:297
  12.5 92.5 %collective-permute-start.14 = (bf16[2,64,1408]{2,0,1:T(2,128)(2,1)}, bf16[2,64,1408]{2,0,1:T(2,128)(2,1)}, u32[]{:S(2)}, u32[]{:S(2)}) collective-permute-start(bf16[2,64,1408]{2,0,1:T(2,128)(2,1)} %get-tuple-element.178), channel_id=1, source_target_pairs={{0,2},{1,3},{2,0},{3,1},{4,6},{5,7},{6,4},{7,5},{8,10},{9,11},{10,... | collective-permute-start | bytes 1081352 | tf_op jit(solution)/shard_map/ppermute | solution.py:21
  17.5 92.0 %collective-permute-start.23 = (bf16[2,64,1408]{2,0,1:T(2,128)(2,1)}, bf16[2,64,1408]{2,0,1:T(2,128)(2,1)}, u32[]{:S(2)}, u32[]{:S(2)}) collective-permute-start(bf16[2,64,1408]{2,0,1:T(2,128)(2,1)} %get-tuple-element.174), channel_id=1, source_target_pairs={{0,2},{1,3},{2,0},{3,1},{4,6},{5,7},{6,4},{7,5},{8,10},{9,11},{10,... | collective-permute-start | bytes 1081352 | tf_op jit(solution)/shard_map/ppermute | solution.py:21
  19.4 94.3 %collective-permute-start.32 = (bf16[2,64,1408]{2,0,1:T(2,128)(2,1)S(1)}, bf16[2,64,1408]{2,0,1:T(2,128)(2,1)}, u32[]{:S(2)}, u32[]{:S(2)}) collective-permute-start(bf16[2,64,1408]{2,0,1:T(2,128)(2,1)S(1)} %get-tuple-element.170), channel_id=1, source_target_pairs={{0,2},{1,3},{2,0},{3,1},{4,6},{5,7},{6,4},{7,5},{8,10},{9,11},{10,... | collective-permute-start | bytes 1081352 | tf_op jit(solution)/shard_map/ppermute | solution.py:21
  125.6 309.3 %collective-permute-start.19 = (bf16[256,1408]{1,0:T(8,128)(2,1)}, bf16[256,1408]{1,0:T(8,128)(2,1)}, u32[]{:S(2)}, u32[]{:S(2)}) collective-permute-start(bf16[256,1408]{1,0:T(8,128)(2,1)} %bitcast.40), channel_id=1, source_target_pairs={{0,16},{8,24},{16,0},{24,8},{1,17},{9,25},{17,1},{25,9},{2,18},{10... | collective-permute-start | bytes 2162696 | tf_op jit(solution)/shard_map/ppermute | solution.py:21
  219.1 267.2 %collective-permute-start.25 = (bf16[256,1408]{1,0:T(8,128)(2,1)}, bf16[256,1408]{1,0:T(8,128)(2,1)}, u32[]{:S(2)}, u32[]{:S(2)}) collective-permute-start(bf16[256,1408]{1,0:T(8,128)(2,1)} %bitcast.54), channel_id=1, source_target_pairs={{0,4},{1,5},{2,6},{3,7},{4,0},{5,1},{6,2},{7,3},{8,12},{9,13},{10,... | collective-permute-start | bytes 2162696 | tf_op jit(solution)/shard_map/ppermute | solution.py:21
  300.6 208.1 %collective-permute-start.26 = (bf16[256,1408]{1,0:T(8,128)(2,1)}, bf16[256,1408]{1,0:T(8,128)(2,1)}, u32[]{:S(2)}, u32[]{:S(2)}) collective-permute-start(bf16[256,1408]{1,0:T(8,128)(2,1)} %bitcast.54), channel_id=1, source_target_pairs={{0,16},{8,24},{16,0},{24,8},{1,17},{9,25},{17,1},{25,9},{2,18},{10... | collective-permute-start | bytes 2162696 | tf_op jit(solution)/shard_map/ppermute | solution.py:21
  304.5 185.2 %collective-permute-start.7 = (bf16[256,2048]{1,0:T(8,128)(2,1)}, bf16[256,2048]{1,0:T(8,128)(2,1)}, u32[]{:S(2)}, u32[]{:S(2)}) collective-permute-start(bf16[256,2048]{1,0:T(8,128)(2,1)} %maximum_select_fusion.2), channel_id=1, source_target_pairs={{0,1},{1,0},{2,3},{3,2},{4,5},{5,4},{6,7},{7,6},{8,9},{9,8},{10,11... | collective-permute-start | bytes 3145736 | tf_op jit(solution)/shard_map/ppermute | solution.py:21
  320.0 108.8 %collective-permute-start.18 = (bf16[256,1408]{1,0:T(8,128)(2,1)}, bf16[256,1408]{1,0:T(8,128)(2,1)}, u32[]{:S(2)}, u32[]{:S(2)}) collective-permute-start(bf16[256,1408]{1,0:T(8,128)(2,1)} %collective-permute-done.16), channel_id=1, source_target_pairs={{0,8},{8,0},{16,24},{24,16},{1,9},{9,1},{17,25},{25,17},{2,10},{10... | collective-permute-start | bytes 2162696 | tf_op jit(solution)/shard_map/ppermute | solution.py:21
  807.4 123.6 %collective-permute-start.76 = (bf16[256,2048]{1,0:T(8,128)(2,1)}, bf16[256,2048]{1,0:T(8,128)(2,1)}, u32[]{:S(2)}, u32[]{:S(2)}) collective-permute-start(bf16[256,2048]{1,0:T(8,128)(2,1)} %get-tuple-element.80), channel_id=1, source_target_pairs={{0,1},{1,0},{2,3},{3,2},{4,5},{5,4},{6,7},{7,6},{8,9},{9,8},{10,11... | collective-permute-start | bytes 3145736 | tf_op jit(solution)/shard_map/ppermute | solution.py:21
  807.9 151.7 %collective-permute-start.75 = (bf16[256,2048]{1,0:T(8,128)(2,1)}, bf16[256,2048]{1,0:T(8,128)(2,1)}, u32[]{:S(2)}, u32[]{:S(2)}) collective-permute-start(bf16[256,2048]{1,0:T(8,128)(2,1)} %get-tuple-element.79), channel_id=1, source_target_pairs={{0,1},{1,0},{2,3},{3,2},{4,5},{5,4},{6,7},{7,6},{8,9},{9,8},{10,11... | collective-permute-start | bytes 3145736 | tf_op jit(solution)/shard_map/ppermute | solution.py:21
  845.3 91.3 %collective-permute-start.60 = (bf16[256,2048]{1,0:T(8,128)(2,1)}, bf16[256,2048]{1,0:T(8,128)(2,1)}, u32[]{:S(2)}, u32[]{:S(2)}) collective-permute-start(bf16[256,2048]{1,0:T(8,128)(2,1)} %get-tuple-element.69), channel_id=1, source_target_pairs={{0,1},{1,0},{2,3},{3,2},{4,5},{5,4},{6,7},{7,6},{8,9},{9,8},{10,11... | collective-permute-start | bytes 3145736 | tf_op jit(solution)/shard_map/ppermute | solution.py:21
  925.0 134.0 %collective-permute-start.114 = (bf16[2,2,256,1408]{3,2,1,0:T(8,128)(2,1)}, bf16[2,2,256,1408]{3,2,1,0:T(8,128)(2,1)}, u32[]{:S(2)}, u32[]{:S(2)}) collective-permute-start(bf16[2,2,256,1408]{3,2,1,0:T(8,128)(2,1)} %dynamic-slice_bitcast_fusion), channel_id=1, source_target_pairs={{0,16},{8,24},{16,0},{24,8},{1,17},{9,25},{17,1},{25,9},{2,18},{10... | collective-permute-start | bytes 8650760 | tf_op jit(solution)/shard_map/ppermute | solution.py:21
  936.6 129.8 %collective-permute-start.109 = (bf16[2,2,256,1408]{3,2,1,0:T(8,128)(2,1)}, bf16[2,2,256,1408]{3,2,1,0:T(8,128)(2,1)}, u32[]{:S(2)}, u32[]{:S(2)}) collective-permute-start(bf16[2,2,256,1408]{3,2,1,0:T(8,128)(2,1)} %dynamic-slice_bitcast_fusion.1), channel_id=1, source_target_pairs={{0,8},{8,0},{16,24},{24,16},{1,9},{9,1},{17,25},{25,17},{2,10},{10... | collective-permute-start | bytes 8650760 | tf_op jit(solution)/shard_map/ppermute | solution.py:21
  954.9 115.7 %collective-permute-start.104 = (bf16[2,2,256,1408]{3,2,1,0:T(8,128)(2,1)}, bf16[2,2,256,1408]{3,2,1,0:T(8,128)(2,1)}, u32[]{:S(2)}, u32[]{:S(2)}) collective-permute-start(bf16[2,2,256,1408]{3,2,1,0:T(8,128)(2,1)} %dynamic-slice_bitcast_fusion.2), channel_id=1, source_target_pairs={{0,16},{8,24},{16,0},{24,8},{1,17},{9,25},{17,1},{25,9},{2,18},{10... | collective-permute-start | bytes 8650760 | tf_op jit(solution)/shard_map/ppermute | solution.py:21
  1054.2 520.2 %collective-permute-start.94 = (bf16[2,2,2,2,64,2048]{5,4,2,3,0,1:T(8,128)(2,1)}, bf16[2,2,2,2,64,2048]{5,4,2,3,0,1:T(8,128)(2,1)}, u32[]{:S(2)}, u32[]{:S(2)}) collective-permute-start(bf16[2,2,2,2,64,2048]{5,4,2,3,0,1:T(8,128)(2,1)} %bitcast.687), channel_id=1, source_target_pairs={{0,1},{1,0},{2,3},{3,2},{4,5},{5,4},{6,7},{7,6},{8,9},{9,8},{10,11... | collective-permute-start | bytes 12582920 | tf_op jit(solution)/shard_map/ppermute | solution.py:21
  1057.4 235.9 %collective-permute-start.91 = (f32[2,2,64,128]{3,2,1,0:T(8,128)}, f32[2,2,64,128]{3,2,1,0:T(8,128)}, u32[]{:S(2)}, u32[]{:S(2)}) collective-permute-start(f32[2,2,64,128]{3,2,1,0:T(8,128)} %dynamic-slice_bitcast_fusion.28), channel_id=1, source_target_pairs={{0,16},{8,24},{16,0},{24,8},{1,17},{9,25},{17,1},{25,9},{2,18},{10... | collective-permute-start | bytes 393224 | tf_op jit(solution)/shard_map/ppermute | solution.py:21
  1065.3 239.5 %collective-permute-start.115 = (bf16[2,256,1408]{2,1,0:T(8,128)(2,1)}, bf16[2,256,1408]{2,1,0:T(8,128)(2,1)}, u32[]{:S(2)}, u32[]{:S(2)}) collective-permute-start(bf16[2,256,1408]{2,1,0:T(8,128)(2,1)} %dynamic-slice_bitcast_fusion.8), channel_id=1, source_target_pairs={{0,8},{8,0},{16,24},{24,16},{1,9},{9,1},{17,25},{25,17},{2,10},{10... | collective-permute-start | bytes 4325384 | tf_op jit(solution)/shard_map/ppermute | solution.py:21
  1070.3 237.0 %collective-permute-start.110 = (bf16[2,256,1408]{2,1,0:T(8,128)(2,1)}, bf16[2,256,1408]{2,1,0:T(8,128)(2,1)}, u32[]{:S(2)}, u32[]{:S(2)}) collective-permute-start(bf16[2,256,1408]{2,1,0:T(8,128)(2,1)} %dynamic-slice_bitcast_fusion.9), channel_id=1, source_target_pairs={{0,16},{8,24},{16,0},{24,8},{1,17},{9,25},{17,1},{25,9},{2,18},{10... | collective-permute-start | bytes 4325384 | tf_op jit(solution)/shard_map/ppermute | solution.py:21
  1304.6 132.9 %collective-permute-start.78 = (bf16[4,128,2048]{2,1,0:T(8,128)(2,1)S(1)}, bf16[4,128,2048]{2,1,0:T(8,128)(2,1)S(1)}, u32[]{:S(2)}, u32[]{:S(2)}) collective-permute-start(bf16[4,128,2048]{2,1,0:T(8,128)(2,1)S(1)} %dynamic-slice_bitcast_fusion.5), channel_id=1, source_target_pairs={{0,1},{1,0},{2,3},{3,2},{4,5},{5,4},{6,7},{7,6},{8,9},{9,8},{10,11... | collective-permute-start | bytes 6291464 | tf_op jit(solution)/shard_map/ppermute | solution.py:21
  1304.9 133.7 %collective-permute-start.81 = (bf16[4,128,2048]{2,1,0:T(8,128)(2,1)S(1)}, bf16[4,128,2048]{2,1,0:T(8,128)(2,1)S(1)}, u32[]{:S(2)}, u32[]{:S(2)}) collective-permute-start(bf16[4,128,2048]{2,1,0:T(8,128)(2,1)S(1)} %dynamic-slice_bitcast_fusion.4), channel_id=1, source_target_pairs={{0,1},{1,0},{2,3},{3,2},{4,5},{5,4},{6,7},{7,6},{8,9},{9,8},{10,11... | collective-permute-start | bytes 6291464 | tf_op jit(solution)/shard_map/ppermute | solution.py:21
  1437.5 208.4 %collective-permute-start.93 = (f32[64,128]{1,0:T(8,128)}, f32[64,128]{1,0:T(8,128)}, u32[]{:S(2)}, u32[]{:S(2)}) collective-permute-start(f32[64,128]{1,0:T(8,128)} %fusion.251), channel_id=1, source_target_pairs={{0,4},{1,5},{2,6},{3,7},{4,0},{5,1},{6,2},{7,3},{8,12},{9,13},{10,... | collective-permute-start | bytes 98312 | tf_op jit(solution)/shard_map/ppermute | solution.py:21
  1438.6 191.9 %collective-permute-start.88 = (f32[4,128,768]{2,1,0:T(8,128)}, f32[4,128,768]{2,1,0:T(8,128)}, u32[]{:S(2)}, u32[]{:S(2)}) collective-permute-start(f32[4,128,768]{2,1,0:T(8,128)} %maximum_select_fusion.1), channel_id=1, source_target_pairs={{0,4},{1,5},{2,6},{3,7},{4,0},{5,1},{6,2},{7,3},{8,12},{9,13},{10,... | collective-permute-start | bytes 4718600 | tf_op jit(solution)/shard_map/ppermute | solution.py:21
  (412 other events, 8280.4 us)

commit v2 on v1

v2 whole, which is shorter than its diff:
```python
import functools
import math

import jax
import jax.numpy as jnp
import numpy as np
from jax import lax
from jax.experimental import pallas as pl
from jax.experimental.pallas import tpu as pltpu
from jax.sharding import PartitionSpec as P

HEADS = 16
HEAD = 128


deep_alpha = math.sqrt(48.0)
epsilon = 1e-05
mask_token = 3
both = ("items", "seq")
bf16 = jnp.bfloat16
f32 = jnp.float32
score_scale = HEAD ** (-0.5)
exponent_scale = score_scale * math.log2(math.e)


class Lines:
    def __init__(self):
        self.last = {}

    def swap(self, part, axis, bit):
        if (axis, bit) in self.last:
            part, _ = lax.optimization_barrier((part, self.last[axis, bit]))
        size = lax.axis_size(axis)
        got = lax.ppermute(part, axis, [(j, j ^ bit) for j in range(size)])
        self.last[axis, bit] = got
        return got


def bits_of(axis):
    found = []
    bit = 1
    while bit < lax.axis_size(axis):
        found.append((axis, bit))
        bit *= 2
    return found


def my_bit(axis, bit):
    return (lax.axis_index(axis) // bit) % 2


def in_order(own, got, place, dim):
    return jnp.where(
        place == 0, jnp.concatenate([own, got], axis=dim), jnp.concatenate([got, own], axis=dim)
    )


def pick(whole, place, dim):
    return lax.dynamic_index_in_dim(whole, place, dim, keepdims=False)


def gather_merge(lines, own, steps):
    for axis, bit in steps:
        own = in_order(own, lines.swap(own, axis, bit), my_bit(axis, bit), 0)
    return own


def halve(lines, whole, dim, axis, bit):
    place = my_bit(axis, bit)
    mine = pick(whole, place, dim)
    got = lines.swap(pick(whole, 1 - place, dim), axis, bit)
    return (mine.astype(f32) + got.astype(f32)).astype(whole.dtype)


def moved(masks, axis, bit):
    return (masks[0] ^ (bit if axis == "items" else 0), masks[1] ^ (bit if axis == "seq" else 0))


def gather_four(lines, own):
    chip = jnp.concatenate([own, lines.swap(own, "seq", 2)], axis=0)
    return jnp.concatenate([chip, lines.swap(chip, "seq", 1)], axis=0)


def sum_four(lines, parts):
    mine, other = jnp.split(parts, 2, axis=0)
    mine = mine.astype(f32) + lines.swap(other, "seq", 1).astype(f32)
    own, far = jnp.split(mine, 2, axis=0)
    return own + lines.swap(far.astype(bf16), "seq", 2).astype(f32)


def contract_rows(left, right):
    return lax.dot_general(left, right, (((0,), (0,)), ((), ())), preferred_element_type=f32)


def contract_cols(left, right):
    return lax.dot_general(left, right, (((1,), (1,)), ((), ())), preferred_element_type=f32)


def dot(left, right):
    return jnp.dot(left, right, preferred_element_type=f32)


def turn(values, cosine, sine_part):
    return values * cosine + pltpu.roll(values, HEAD // 2, 1) * sine_part


def head_parts(onehot_ref, table_ref, cosine, sine_part):
    onehot = onehot_ref[...]
    mixed = dot(jnp.concatenate([onehot, onehot], axis=1), table_ref[...])
    query = turn(mixed[:, :HEAD], cosine, sine_part).astype(bf16)
    key = turn(mixed[:, HEAD : 2 * HEAD], cosine, sine_part).astype(bf16)
    return query, key, mixed[:, 2 * HEAD :].astype(bf16)


def visible_scores(key, query, offset, visible):
    scores = contract_cols(key, query)
    place = offset + lax.broadcasted_iota(jnp.int32, (1, query.shape[0]), 1)
    seen = lax.broadcasted_iota(jnp.int32, scores.shape, 0) < jnp.maximum(place + 1, visible)
    return jnp.where(seen, scores, -1e30)


def table_halves(mixed_table):
    vocab = mixed_table.shape[0]
    by_head = jnp.transpose(mixed_table.reshape(vocab, -1, 3 * HEAD), (1, 0, 2))
    high = lax.reduce_precision(by_head, 8, 7)
    return jnp.concatenate([high.astype(bf16), (by_head - high).astype(bf16)], axis=1)


MESH = pl.DeviceIdType.MESH


class Copies:
    def __init__(self, send_sems, recv_sems, local_sems):
        self.sems = send_sems, recv_sems, local_sems
        self.sent = {}
        self.moved = 0
        self.count = 0
        self.here = lax.axis_index("items"), lax.axis_index("seq")

    def send(self, source, target, masks):
        order = self.count
        self.count += 1
        copy = pltpu.make_async_remote_copy(
            src_ref=source,
            dst_ref=target,
            send_sem=self.sems[0].at[order],
            recv_sem=self.sems[1].at[order],
            device_id=(self.here[0] ^ masks[0], self.here[1] ^ masks[1]),
            device_id_type=MESH,
        )
        copy.start()
        self.sent[id(copy)] = copy
        return copy

    def move(self, source, target):
        copy = pltpu.make_async_copy(source, target, self.sems[2].at[self.moved])
        self.moved += 1
        copy.start()
        return copy

    def sent_now(self, copy):
        self.sent.pop(id(copy)).wait_send()

    def end(self):
        for copy in self.sent.values():
            copy.wait_send()


def wait_all(copies):
    for copy in copies:
        copy.wait_recv()


def mask_of(step):
    return moved((0, 0), *step)


def greet(masks):
    barrier = pltpu.get_barrier_semaphore()
    here = lax.axis_index("items"), lax.axis_index("seq")
    for mask_i, mask_s in masks:
        pl.semaphore_signal(
            barrier,
            inc=1,
            device_id=(here[0] ^ mask_i, here[1] ^ mask_s),
            device_id_type=MESH,
        )
    pl.semaphore_wait(barrier, len(masks))


def partners(seq_size, item_bits):
    return [(0, mask) for mask in range(1, seq_size)] + [mask_of(step) for step in item_bits]


def aligned(place, size):
    return pl.ds(place // size * size, size)


def first_kernel(
    item_bits,
    seq_bits,
    row_count,
    small_ref,
    heads_ref,
    dense_ref,
    in_ref,
    out_ref,
    everyone_ref,
    table_ref,
    block_ref,
    dense_all_ref,
    own_in_ref,
    own_out_ref,
    embed_scr,
    block_scr,
    sum_scr,
    got_scr,
    send_sems,
    recv_sems,
    local_sems,
):
    items_size, seq_size = everyone_ref.shape[:2]
    item_place, seq_place = lax.axis_index("items"), lax.axis_index("seq")
    core, chip = seq_place % 2, seq_place // 2
    member = seq_place % 4
    rows = dense_ref.shape[0]
    columns = block_scr.shape[2]
    greet(partners(seq_size, item_bits))
    copies = Copies(send_sems, recv_sems, local_sems)

    def head_columns(place):
        return heads_ref.at[:, pl.ds(pl.multiple_of(place * columns, 128), columns)]

    small = [copies.send(small_ref, everyone_ref.at[item_place, seq_place], mask_of(seq_bits[0]))]
    heads = [
        copies.send(head_columns(seq_place ^ mask), block_scr.at[seq_place], (0, mask))
        for mask in range(1, seq_size)
    ]
    dense = [
        copies.send(dense_ref, dense_all_ref.at[item_place, chip, core], mask_of(seq_bits[1]))
    ]
    shares = []
    for source, target in ((in_ref, own_in_ref), (out_ref, own_out_ref)):
        mine = pl.ds(pl.multiple_of(member * rows, rows), rows)
        for mask in range(1, 4):
            other = member ^ mask
            shares.append(
                copies.send(source.at[other // 2, other % 2], target.at[mine], (0, mask))
            )
    local = [
        copies.move(small_ref, everyone_ref.at[item_place, seq_place]),
        copies.move(dense_ref, dense_all_ref.at[item_place, chip, core]),
        copies.move(head_columns(seq_place), block_scr.at[seq_place]),
        copies.move(in_ref.at[member // 2, core], own_in_ref.at[mine]),
        copies.move(out_ref.at[member // 2, core], own_out_ref.at[mine]),
    ]
    for copy in local:
        copy.wait()

    for order in range(1, len(seq_bits)):
        wait_all(small[-1:])
        part = everyone_ref.at[item_place, aligned(seq_place, 2**order)]
        small.append(copies.send(part, part, mask_of(seq_bits[order])))
        if order > 1:
            wait_all(dense[-1:])
            part = dense_all_ref.at[item_place, aligned(chip, 2 ** (order - 1)), core]
            dense.append(copies.send(part, part, mask_of(seq_bits[order])))
    wait_all(small[-1:])
    embed = copies.move(everyone_ref.at[item_place, :, pl.ds(0, row_count)], embed_scr)
    part = everyone_ref.at[item_place]
    small.append(copies.send(part, part, mask_of(item_bits[0])))
    wait_all(dense[-1:])

    def dense_part(mask):
        return dense_all_ref.at[item_place ^ mask, :, core]

    known = [0]
    waves = []
    for step in item_bits[::-1]:
        waves.append([(mask, step) for mask in known])
        known = known + [mask ^ step[1] for mask in known]
    arrived = {}
    for wave in waves:
        part = dense_part(0)
        arrived[wave[0][1][1]] = copies.send(part, part, mask_of(wave[0][1]))
    near = [copies.send(dense_part(0), dense_part(0), mask_of(seq_bits[0]))]

    wait_all(heads)
    embed.wait()
    sum_scr[0] = lax.dot_general(
        embed_scr[...].reshape(seq_size * row_count, -1),
        block_scr[...].reshape(seq_size * row_count, columns),
        (((0,), (0,)), ((), ())),
        preferred_element_type=f32,
    )
    block_out = copies.move(block_scr, block_ref)
    for order, step in enumerate(item_bits):
        one = copies.send(sum_scr.at[order], got_scr.at[order], mask_of(step))
        if order + 1 < len(item_bits):
            wait_all(small[-1:])
            part = everyone_ref.at[aligned(item_place, 2 ** (order + 1))]
            small.append(copies.send(part, part, mask_of(item_bits[order + 1])))
        one.wait_recv()
        sum_scr[order + 1] = sum_scr[order] + got_scr[order]
    table_ref[...] = sum_scr[len(item_bits)]

    for wave in waves:
        for mask, step in wave:
            if mask:
                part = dense_part(mask)
                arrived[mask ^ step[1]] = copies.send(part, part, mask_of(step))
        for mask, step in wave:
            arrived[mask ^ step[1]].wait_recv()
            part = dense_part(mask ^ step[1])
            near.append(copies.send(part, part, mask_of(seq_bits[0])))
    wait_all(near)
    wait_all(shares)
    wait_all(small[-1:])
    block_out.wait()
    copies.end()


def first_call(item_bits, seq_bits, small, heads, dense, parts_in, parts_out):
    items_size, seq_size = 2 ** len(item_bits), 2 ** len(seq_bits)
    row_count = heads.shape[0]
    rows, width = dense.shape
    vocab = small.shape[1]
    columns = heads.shape[1] // seq_size
    any_space = pl.BlockSpec(memory_space=pl.ANY)
    spare = 8 * (len(item_bits) + len(seq_bits)) + 2 * seq_size + 2 ** (len(item_bits) + 1)
    return pl.pallas_call(
        functools.partial(first_kernel, item_bits, seq_bits, row_count),
        in_specs=[any_space] * 5,
        out_specs=[any_space, pl.BlockSpec(memory_space=pltpu.VMEM)] + [any_space] * 4,
        out_shape=[
            jax.ShapeDtypeStruct((items_size, seq_size) + small.shape, bf16),
            jax.ShapeDtypeStruct((vocab, columns), f32),
            jax.ShapeDtypeStruct((seq_size, row_count, columns), bf16),
            jax.ShapeDtypeStruct((items_size, seq_size // 2, 2, rows, width), bf16),
            jax.ShapeDtypeStruct((4 * rows, parts_in.shape[3]), bf16),
            jax.ShapeDtypeStruct((4 * rows, parts_out.shape[3]), bf16),
        ],
        scratch_shapes=[
            pltpu.VMEM((seq_size, row_count, vocab), bf16),
            pltpu.VMEM((seq_size, row_count, columns), bf16),
            pltpu.VMEM((len(item_bits) + 1, vocab, columns), f32),
            pltpu.VMEM((len(item_bits), vocab, columns), f32),
            pltpu.SemaphoreType.DMA((spare,)),
            pltpu.SemaphoreType.DMA((spare,)),
            pltpu.SemaphoreType.DMA((8,)),
        ],
        compiler_params=pltpu.CompilerParams(
            collective_id=0, has_side_effects=True, vmem_limit_bytes=24 * 2**20
        ),
        name="first",
    )(small, heads, dense, parts_in, parts_out)


class Spread:
    def __init__(self, copies, own, whole, outer_bits, item_bits):
        self.copies, self.own, self.whole = copies, own, whole
        self.outer_bits, self.item_bits = outer_bits, item_bits
        self.half = own.shape[0] // 2

    def part(self, masks):
        place = (self.copies.here[0] ^ masks[0]) * lax.axis_size("seq")
        return self.whole.at[(place + (self.copies.here[1] ^ masks[1])) // 4]

    def over(self, masks, step, rows=None):
        source = self.own if masks == (0, 0) else self.part(masks)
        target = self.part(masks)
        if rows is not None:
            source, target = source.at[rows], target.at[rows]
        return self.copies.send(source, target, mask_of(step))

    def start(self):
        self.local = self.copies.move(self.own, self.part((0, 0)))
        self.first = [self.over((0, 0), step) for step in self.item_bits]
        self.outer = self.over((0, 0), self.outer_bits[0])

    def cross(self, masks, first):
        one, two = self.item_bits
        first[0].wait_recv()
        found = [self.over(moved(masks, *one), two, pl.ds(0, self.half))]
        first[1].wait_recv()
        found.append(self.over(moved(masks, *two), one, pl.ds(self.half, self.half)))
        return found

    def cross_own(self):
        self.last = self.cross((0, 0), self.first)

    def spread_outer(self):
        self.outer.wait_recv()
        masks = mask_of(self.outer_bits[0])
        self.second = [self.over(masks, step) for step in self.item_bits]

    def cross_outer(self):
        self.last += self.cross(mask_of(self.outer_bits[0]), self.second)

    def plain(self):
        self.local = self.copies.move(self.own, self.part((0, 0)))
        known = [(0, 0)]
        for step in self.outer_bits + self.item_bits:
            wait_all([self.over(masks, step) for masks in known])
            known = known + [moved(masks, *step) for masks in known]
        self.last = []

    def end(self):
        wait_all(self.last)
        self.local.wait()


def attend_unit(block, visible, onehot_ref, table_ref, cosine_ref, sine_ref, context_ref, lse_ref):
    query, key, value = head_parts(onehot_ref, table_ref, cosine_ref[...], sine_ref[...])
    value_turned = value.T
    for offset in range(0, query.shape[0], block):
        scores = visible_scores(key, query[offset : offset + block], offset, visible)
        peak = jnp.max(scores, axis=0, keepdims=True)
        expos = jnp.exp2((scores - peak) * exponent_scale)
        total = jnp.sum(expos, axis=0, keepdims=True)
        context = dot(value_turned, expos.astype(bf16)) / total
        context_ref[offset : offset + block, :] = context.T.astype(bf16)
        lse_ref[:, offset : offset + block] = peak * exponent_scale + jnp.log2(total)


def second_kernel(
    item_bits,
    seq_bits,
    visible_ref,
    onehot_ref,
    table_ref,
    cosine_ref,
    sine_ref,
    own_in_ref,
    own_out_ref,
    context_ref,
    lse_ref,
    in_ref,
    out_ref,
    context_scr,
    send_sems,
    recv_sems,
    local_sems,
):
    seq_size = 2 ** len(seq_bits)
    items_here, length, features = context_scr.shape
    heads_here = features // HEAD
    span = length // seq_size
    seq_place = lax.axis_index("seq")
    outer_bits = seq_bits[2:]
    greet(partners(seq_size, item_bits))
    copies = Copies(send_sems, recv_sems, local_sems)
    spreads = [
        Spread(copies, own_in_ref, in_ref, outer_bits, item_bits),
        Spread(copies, own_out_ref, out_ref, outer_bits, item_bits),
    ]
    stepwise = len(outer_bits) == 1 and len(item_bits) == 2
    if stepwise:
        for one in spreads:
            one.start()
    arrivals, local = [], []
    for item in range(items_here):

        @pl.loop(0, heads_here)
        def _(head):
            place = pl.ds(pl.multiple_of(head * HEAD, HEAD), HEAD)
            attend_unit(
                min(256, length),
                visible_ref[item],
                onehot_ref.at[item],
                table_ref.at[head],
                cosine_ref,
                sine_ref,
                context_scr.at[item, :, place],
                lse_ref.at[item, head],
            )

        target = context_ref.at[
            item, :, pl.ds(pl.multiple_of(seq_place * features, HEAD), features)
        ]
        for mask in range(seq_size):
            rows = pl.ds(pl.multiple_of((seq_place ^ mask) * span, span), span)
            source = context_scr.at[item, rows]
            if mask:
                arrivals.append(copies.send(source, target, (0, mask)))
            else:
                local.append(copies.move(source, target))
    if stepwise:
        for one in spreads:
            one.cross_own()
        for one in spreads:
            one.spread_outer()
        for one in spreads:
            one.cross_outer()
    else:
        for one in spreads:
            one.plain()
    for one in spreads:
        one.end()
    wait_all(arrivals)
    for copy in local:
        copy.wait()
    copies.end()


def second_call(item_bits, seq_bits, visible, onehots, tables, cosine, sine_part, own_in, own_out):
    items_here, length, vocab = onehots.shape
    heads_here = tables.shape[0]
    features = heads_here * HEAD
    seq_size = 2 ** len(seq_bits)
    groups = 2 ** (len(item_bits) + len(seq_bits)) // 4
    any_space = pl.BlockSpec(memory_space=pl.ANY)
    near_space = pl.BlockSpec(memory_space=pltpu.VMEM)
    spare = 4 * groups + items_here * seq_size
    return pl.pallas_call(
        functools.partial(second_kernel, item_bits, seq_bits),
        in_specs=[pl.BlockSpec(memory_space=pltpu.SMEM)] + [near_space] * 4 + [any_space] * 2,
        out_specs=[any_space, near_space, any_space, any_space],
        out_shape=[
            jax.ShapeDtypeStruct((items_here, length // seq_size, features * seq_size), bf16),
            jax.ShapeDtypeStruct((items_here, heads_here, 1, length), f32),
            jax.ShapeDtypeStruct((groups,) + own_in.shape, bf16),
            jax.ShapeDtypeStruct((groups,) + own_out.shape, bf16),
        ],
        scratch_shapes=[
            pltpu.VMEM((items_here, length, features), bf16),
            pltpu.SemaphoreType.DMA((spare,)),
            pltpu.SemaphoreType.DMA((spare,)),
            pltpu.SemaphoreType.DMA((8,)),
        ],
        compiler_params=pltpu.CompilerParams(
            collective_id=1, has_side_effects=True, vmem_limit_bytes=48 * 2**20
        ),
        name="second",
    )(visible, onehots, tables, cosine, sine_part, own_in, own_out)


def leading(ref):
    return [index for index in np.ndindex(*ref.shape[:-2])]


def add_into(target, source):
    rows = target.shape[-2]
    for index in leading(target):

        @pl.loop(0, rows // 16)
        def _(order):
            place = index + (pl.ds(pl.multiple_of(order * 16, 16), 16),)
            total = target[place].astype(f32) + source[place].astype(f32)
            target[place] = total.astype(target.dtype)


def copy_into(target, source):
    @pl.loop(0, target.shape[0] // 16)
    def _(order):
        place = pl.ds(pl.multiple_of(order * 16, 16), 16)
        target[place] = source[place]


class Reduce:
    def __init__(self, copies, whole, rows, dims, steps, got, stage, stage_sems):
        self.copies, self.whole, self.rows = copies, whole, rows
        self.steps, self.got = steps, got
        self.place = dims.index(steps[0])
        self.stage, self.stage_sems = stage, stage_sems
        self.order = 0

    def first(self, bit, index=()):
        full = (slice(None),) * self.place
        if index:
            full = index[: self.place]
        rest = index[self.place :] if index else ()
        if index:
            return self.whole.at[full + (bit,) + rest + (self.rows,)]
        spare = len(self.whole.shape) - 3 - self.place
        return self.whole.at[full + (bit,) + (slice(None),) * spare + (self.rows,)]

    def start(self):
        step = self.steps[0]
        self.copy = self.copies.send(self.first(1 - my_bit(*step)), self.got[0], mask_of(step))

    def advance(self):
        step = self.steps[self.order]
        self.copy.wait_recv()
        if self.order == 0:
            self.kept = self.got[0]
            rows, columns = self.kept.shape[-2:]
            places = leading(self.kept)

            def load(order):
                return pltpu.make_async_copy(
                    self.first(my_bit(*step), places[order]),
                    self.stage.at[order % 2, pl.ds(0, rows), pl.ds(0, columns)],
                    self.stage_sems.at[order % 2],
                )

            load(0).start()
            for order, place in enumerate(places):
                if order + 1 < len(places):
                    load(order + 1).start()
                load(order).wait()
                add_into(
                    self.kept.at[place],
                    self.stage.at[order % 2, pl.ds(0, rows), pl.ds(0, columns)],
                )
        else:
            self.kept = self.kept.at[my_bit(*step)]
            add_into(self.kept, self.got[self.order])
        self.order += 1
        if self.order < len(self.steps):
            step = self.steps[self.order]
            self.copy = self.copies.send(
                self.kept.at[1 - my_bit(*step)], self.got[self.order], mask_of(step)
            )


def attend_back_unit(
    block,
    visible,
    onehot_ref,
    table_ref,
    cosine_ref,
    sine_ref,
    lse_ref,
    grad_ref,
    mixed_ref,
    sums_ref,
):
    cosine, sine_part = cosine_ref[...], sine_ref[...]
    query, key, value = head_parts(onehot_ref, table_ref, cosine, sine_part)
    key_turned = key.T
    length = query.shape[0]
    grad_key = jnp.zeros((length, HEAD), f32)
    grad_value = jnp.zeros((length, HEAD), f32)
    grad_query = []
    for offset in range(0, length, block):
        query_block = query[offset : offset + block]
        grad_block = grad_ref[offset : offset + block, :]
        scores = visible_scores(key, query_block, offset, visible)
        weights = jnp.exp2(scores * exponent_scale - lse_ref[:, offset : offset + block])
        grad_weights = contract_cols(value, grad_block)
        inner = jnp.sum(weights * grad_weights, axis=0, keepdims=True)
        grad_scores = (weights * (grad_weights - inner)).astype(bf16)
        grad_value = grad_value + dot(weights.astype(bf16), grad_block)
        grad_key = grad_key + dot(grad_scores, query_block)
        grad_query.append(dot(key_turned, grad_scores).T)
    grad_query = jnp.concatenate(grad_query, axis=0)

    def back(grad):
        return turn((grad * score_scale).astype(bf16).astype(f32), cosine, -sine_part).astype(bf16)

    mixed = jnp.concatenate([back(grad_query), back(grad_key), grad_value.astype(bf16)], axis=1)
    mixed_ref[...] = mixed.reshape(mixed_ref.shape)
    sums_ref[...] += dot(onehot_ref[...].T, mixed)


def third_kernel(
    item_bits,
    seq_bits,
    visible_ref,
    onehot_ref,
    table_ref,
    cosine_ref,
    sine_ref,
    lse_ref,
    slice_ref,
    grad_ref,
    in_ref,
    out_ref,
    dense_ref,
    bias_ref,
    spread_ref,
    sums_all_ref,
    in_part_ref,
    out_part_ref,
    dense_part_ref,
    bias_sum_ref,
    mixed_scr,
    other_scr,
    kept_scr,
    step_scrs,
    sums_scr,
    sums_got,
    bias_scr,
    bias_got,
    in_got,
    out_got,
    dense_got,
    in_final,
    out_final,
    stage_scr,
    stage_sems,
    send_sems,
    recv_sems,
    local_sems,
):
    seq_size = 2 ** len(seq_bits)
    items_here, length, features = grad_ref.shape
    heads_here = features // HEAD
    seq_place = lax.axis_index("seq")
    member = seq_place % 4
    outer_bits = seq_bits[2:]
    width = slice_ref.shape[1]
    greet(partners(seq_size, item_bits))
    copies = Copies(send_sems, recv_sems, local_sems)
    dims = item_bits[::-1] + outer_bits[::-1]

    def reducers(whole, got):
        rows = whole.shape[-2]
        if len(item_bits) == 2:
            one, two = item_bits
            ways = [
                (pl.ds(0, rows // 2), [two, one] + outer_bits[::-1]),
                (pl.ds(rows // 2, rows // 2), [one, two] + outer_bits[::-1]),
            ]
        else:
            ways = [(pl.ds(0, rows), dims)]
        return [
            Reduce(copies, whole, part, dims, steps, list(got[order]), stage_scr, stage_sems)
            for order, (part, steps) in enumerate(ways)
        ]

    in_sums = reducers(in_ref, in_got)
    out_sums = reducers(out_ref, out_got)
    dense_steps = item_bits[::-1] + seq_bits[:0:-1]
    dense_sum = Reduce(
        copies,
        dense_ref,
        pl.ds(0, dense_ref.shape[-2]),
        dense_steps,
        dense_steps,
        list(dense_got),
        stage_scr,
        stage_sems,
    )
    for one in in_sums:
        one.start()
    sums_scr[...] = jnp.zeros_like(sums_scr)
    tile = 256
    flying = {}
    for stage in range(items_here + len(seq_bits)):
        if stage < items_here:

            @pl.loop(0, heads_here)
            def _(head):
                place = pl.ds(pl.multiple_of(head * HEAD, HEAD), HEAD)
                packed = pl.ds(pl.multiple_of(head * 3 * HEAD, HEAD), 3 * HEAD)
                attend_back_unit(
                    min(256, length),
                    visible_ref[stage],
                    onehot_ref.at[stage],
                    table_ref.at[head],
                    cosine_ref,
                    sine_ref,
                    lse_ref.at[stage, head],
                    grad_ref.at[stage, :, place],
                    mixed_scr.at[:, :, :, packed],
                    sums_scr.at[0, head],
                )

        for order in range(len(seq_bits) - 1, -1, -1):
            item = stage - 1 - order
            if not 0 <= item < items_here:
                continue
            copy, kept = flying[item]
            copy.wait_recv()
            got = step_scrs[order].at[item % 2]
            if order:
                full = (slice(None),) * (len(kept.shape) - 3)
                kept = kept.at[full + (my_bit(*seq_bits[order]),)]
            if order + 1 < len(seq_bits):
                add_into(kept, got)
                step = seq_bits[order + 1]
                full = (slice(None),) * (len(kept.shape) - 3)
                copy = copies.send(
                    kept.at[full + (1 - my_bit(*step),)],
                    step_scrs[order + 1].at[item % 2],
                    mask_of(step),
                )
                flying[item] = copy, kept
                flying["later", item].append(copy)
            else:

                @pl.loop(0, kept.shape[0] // 16)
                def _(block):
                    place = (pl.ds(pl.multiple_of(block * 16, 16), 16),)
                    total = kept[place].astype(f32) + got[place].astype(f32)
                    spread_ref[(item,) + place] = total.astype(bf16)

        if stage < items_here:
            core = my_bit(*seq_bits[0])
            slot = stage % 2
            if stage >= 2:
                copies.sent_now(flying["first", stage - 2])
            kept_slot = stage % len(seq_bits)
            if stage >= len(seq_bits):
                for copy in flying["later", stage - len(seq_bits)]:
                    copies.sent_now(copy)
            half = mixed_scr.shape[0] * mixed_scr.shape[2]
            other = mixed_scr[:, 1 - core].reshape(half, -1)
            mine = mixed_scr[:, core].reshape(half, -1)

            @pl.loop(0, width // tile)
            def _(order):
                place = pl.ds(pl.multiple_of(order * tile, tile), tile)
                weights = slice_ref[:, place]
                target = other_scr.at[slot]
                target[..., place] = dot(other, weights).astype(bf16).reshape(
                    target.shape[:-1] + (tile,)
                )
                target = kept_scr.at[kept_slot]
                target[..., place] = dot(mine, weights).astype(bf16).reshape(
                    target.shape[:-1] + (tile,)
                )

            copy = copies.send(
                other_scr.at[slot], step_scrs[0].at[slot], mask_of(seq_bits[0])
            )
            flying[stage] = copy, kept_scr.at[kept_slot]
            flying["first", stage] = copy
            flying["later", stage] = []
        if stage == 0:
            for one in out_sums:
                one.start()
        if stage == 2:
            dense_sum.start()
        if stage == items_here:
            for one in in_sums:
                one.advance()

    for one in out_sums:
        one.advance()
    for order, step in enumerate(item_bits):
        copy = copies.send(sums_scr.at[order], sums_got.at[order], mask_of(step))
        copy.wait_recv()
        sums_scr[order + 1] = sums_scr[order] + sums_got[order]
    sums_all_ref[seq_place] = sums_scr[len(item_bits)].astype(bf16)
    for one in in_sums + out_sums:
        one.advance()
    known = [0]
    for axis, bit in seq_bits[::-1]:
        arrivals = []
        for mask in known:
            part = sums_all_ref.at[seq_place ^ mask]
            arrivals.append(copies.send(part, part, (0, bit)))
        if bit == seq_bits[-1][1]:
            dense_sum.advance()
        wait_all(arrivals)
        known = known + [mask ^ bit for mask in known]
    bias_scr[0] = bias_ref[...]
    for order, step in enumerate(seq_bits + item_bits):
        copy = copies.send(bias_scr.at[order], bias_got.at[order], mask_of(step))
        copy.wait_recv()
        bias_scr[order + 1] = bias_scr[order] + bias_got[order]
    bias_sum_ref[...] = bias_scr[len(seq_bits) + len(item_bits)]

    while in_sums[0].order < len(dims):
        for one in in_sums + out_sums:
            one.advance()
        if dense_sum.order < len(dense_steps):
            dense_sum.advance()
    shares, local = [], []
    for sums, final, target in (
        (in_sums, in_final, in_part_ref),
        (out_sums, out_final, out_part_ref),
    ):
        rows = target.shape[1]
        first = 0
        for one in sums:
            copy_into(final.at[pl.ds(first, one.kept.shape[0])], one.kept)
            first += one.kept.shape[0]
        for mask in range(4):
            source = final.at[pl.ds(pl.multiple_of((member ^ mask) * rows, 16), rows)]
            if mask:
                shares.append(copies.send(source, target.at[member], (0, mask)))
            else:
                local.append(copies.move(source, target.at[member]))
    while dense_sum.order < len(dense_steps):
        dense_sum.advance()
    dense_part_ref[...] = dense_sum.kept[...]
    wait_all(shares)
    for copy in local:
        copy.wait()
    copies.end()


def third_call(
    item_bits,
    seq_bits,
    visible,
    onehots,
    tables,
    cosine,
    sine_part,
    log_sums,
    w_slice,
    grad_context,
    grad_in,
    grad_out,
    by_rows,
    in_sum,
):
    items_here, length, vocab = onehots.shape
    heads_here = tables.shape[0]
    seq_size = 2 ** len(seq_bits)
    span = length // seq_size
    width = w_slice.shape[1]
    packed = heads_here * 3 * HEAD
    outer = len(seq_bits) - 2
    levels = len(item_bits) + outer
    any_space = pl.BlockSpec(memory_space=pl.ANY)
    near_space = pl.BlockSpec(memory_space=pltpu.VMEM)

    def got_shapes(whole, ways, depth):
        rows, columns = whole.shape[-2:]
        one = tuple(
            pltpu.VMEM((2,) * order + (rows // ways, columns), bf16)
            for order in range(depth - 1, -1, -1)
        )
        return one

    ways = 2 if len(item_bits) == 2 else 1
    group_rows = grad_in.shape[-2]
    rows = group_rows // 4
    dense_depth = len(item_bits) + len(seq_bits) - 1
    spread = (2,) * (len(seq_bits) - 1) + (span, width)
    all_bits = len(item_bits) + len(seq_bits)
    spare = 8 * items_here + 8 * levels + 16 * all_bits
    stage_rows = max(group_rows // ways, by_rows.shape[-2])
    return pl.pallas_call(
        functools.partial(third_kernel, item_bits, seq_bits),
        in_specs=[pl.BlockSpec(memory_space=pltpu.SMEM)]
        + [near_space] * 7
        + [any_space] * 3
        + [near_space],
        out_specs=[near_space, near_space, any_space, any_space, near_space, near_space],
        out_shape=[
            jax.ShapeDtypeStruct((items_here, span, width), bf16),
            jax.ShapeDtypeStruct((seq_size, heads_here, vocab, 3 * HEAD), bf16),
            jax.ShapeDtypeStruct((4, rows, grad_in.shape[-1]), bf16),
            jax.ShapeDtypeStruct((4, rows, grad_out.shape[-1]), bf16),
            jax.ShapeDtypeStruct(by_rows.shape[-2:], bf16),
            jax.ShapeDtypeStruct(in_sum.shape, f32),
        ],
        scratch_shapes=[
            pltpu.VMEM((seq_size // 2, 2, span, packed), bf16),
            pltpu.VMEM((2,) + spread, bf16),
            pltpu.VMEM((len(seq_bits),) + spread, bf16),
            tuple(pltpu.VMEM((2,) + spread[order:], bf16) for order in range(len(seq_bits))),
            pltpu.VMEM((len(item_bits) + 1, heads_here, vocab, 3 * HEAD), f32),
            pltpu.VMEM((len(item_bits), heads_here, vocab, 3 * HEAD), f32),
            pltpu.VMEM((all_bits + 1,) + in_sum.shape, f32),
            pltpu.VMEM((all_bits,) + in_sum.shape, f32),
            tuple(got_shapes(grad_in, ways, levels) for _ in range(ways)),
            tuple(got_shapes(grad_out, ways, levels) for _ in range(ways)),
            got_shapes(by_rows, 1, dense_depth),
            pltpu.VMEM((group_rows, grad_in.shape[-1]), bf16),
            pltpu.VMEM((group_rows, grad_out.shape[-1]), bf16),
            pltpu.VMEM((2, stage_rows, grad_in.shape[-1]), bf16),
            pltpu.SemaphoreType.DMA((2,)),
            pltpu.SemaphoreType.DMA((spare,)),
            pltpu.SemaphoreType.DMA((spare,)),
            pltpu.SemaphoreType.DMA((8,)),
        ],
        compiler_params=pltpu.CompilerParams(
            collective_id=2, has_side_effects=True, vmem_limit_bytes=60 * 2**20
        ),
        name="third",
    )(
        visible,
        onehots,
        tables,
        cosine,
        sine_part,
        log_sums,
        w_slice,
        grad_context,
        grad_in,
        grad_out,
        by_rows,
        in_sum,
    )


def norm_forward(residual, gain_vec, bias_vec):
    center = residual - jnp.mean(residual, axis=-1, keepdims=True)
    inverse = lax.rsqrt(jnp.mean(center * center, axis=-1, keepdims=True) + epsilon)
    normed = center * inverse
    return (normed * gain_vec + bias_vec, normed, inverse)


def norm_backward(grad_out, normed, inverse, gain_vec):
    scaled = grad_out * gain_vec
    grad_in = inverse * (
        scaled
        - jnp.mean(scaled, axis=-1, keepdims=True)
        - normed * jnp.mean(scaled * normed, axis=-1, keepdims=True)
    )
    return (grad_in, jnp.sum(grad_out * normed, axis=0), jnp.sum(grad_out, axis=0))


def on_device(
    token_ids,
    masked,
    item_flag,
    prefix,
    cotangent,
    embedding,
    heads_weight,
    heads_bias,
    dense_weight,
    dense_bias,
    first_gain,
    first_bias,
    up_weight,
    up_bias,
    down_weight,
    down_bias,
    second_gain,
    second_bias,
):
    lines = Lines()
    items_here, span = token_ids.shape
    items_size, seq_size = lax.axis_size("items"), lax.axis_size("seq")
    item_place, seq_place = lax.axis_index("items"), lax.axis_index("seq")
    count = items_size * seq_size
    length = span * seq_size
    width = embedding.shape[0] * count
    vocab = embedding.shape[1]
    heads_here = HEADS // seq_size
    packed_width = heads_here * 3 * HEAD
    rows_here = up_weight.shape[0]
    ff_width = down_weight.shape[0]
    members = 4
    groups = count // members
    member = seq_place % members
    ff_part = -(-ff_width // (members * 128)) * 128
    ff_all = members * ff_part

    item_bits, seq_bits = bits_of("items"), bits_of("seq")
    outer_bits = seq_bits[2:]

    input_ids = jnp.where(masked == 1, mask_token, token_ids)
    flat_place = item_place * seq_size + seq_place
    row_count = rows_here + 16
    bias_row = lax.dynamic_update_slice(
        jnp.zeros((16, heads_weight.shape[1]), bf16),
        heads_bias[None],
        (0, flat_place * heads_bias.shape[0]),
    )
    ones_row = jnp.zeros((16, vocab), bf16).at[0].set(1.0)
    small = [
        embedding.reshape(-1),
        ones_row.reshape(-1),
        input_ids.astype(bf16).reshape(-1),
        dense_bias,
        first_gain,
        first_bias,
        down_bias,
        second_gain,
        second_bias,
    ]
    ends = [0]
    for part in small:
        ends.append(ends[-1] + part.shape[0])
    flat = jnp.concatenate(small)
    flat = jnp.pad(flat, (0, -flat.shape[0] % 2048)).reshape(-1, 128)

    def by_member(part):
        padded = jnp.pad(part, ((0, 0), (0, ff_all - ff_width)))
        return jnp.transpose(padded.reshape(rows_here, 2, 2, ff_part), (1, 2, 0, 3))

    parts_in = jnp.concatenate(
        [by_member(up_weight[:, :ff_width]), by_member(up_weight[:, ff_width:])], axis=3
    )
    parts_out = by_member(down_weight.T)
    everyone, mixed_table, w_block, w_dense, own_in, own_out = first_call(
        item_bits,
        seq_bits,
        flat,
        jnp.concatenate([heads_weight, bias_row], axis=0),
        dense_weight,
        parts_in,
        parts_out,
    )
    w_dense = w_dense.reshape(width, width)
    w_block = w_block[:, :rows_here].reshape(seq_size * rows_here, packed_width)
    everyone = everyone.reshape(count, -1)
    pieces = [everyone[:, a:b] for a, b in zip(ends[:-1], ends[1:])]
    table = pieces[0].reshape(width, vocab)
    b_dense, gain_one, shift_one, b_down, gain_two, shift_two = (
        part.reshape(-1).astype(f32) for part in pieces[3:]
    )
    ids_here = pick(pieces[2].reshape(items_size, seq_size, items_here, span), item_place, 0)
    ids_here = jnp.transpose(ids_here, (1, 0, 2)).reshape(items_here, length).astype(jnp.int32)
    in_bias = jnp.pad(
        up_bias.astype(f32).reshape(2, ff_width), ((0, 0), (0, ff_all - ff_width))
    )
    in_bias = lax.dynamic_slice(in_bias, (0, member * ff_part), (2, ff_part)).reshape(-1)

    vocab_index = jnp.arange(vocab, dtype=jnp.int32)
    positions = jnp.arange(length, dtype=f32)
    frequency = jnp.exp(jnp.arange(HEAD // 2, dtype=f32) * (-2.0 * math.log(10000.0) / HEAD))
    angles = positions[:, None] * frequency[None, :]
    cosine = jnp.cos(angles)
    sine_part = jnp.sin(angles)
    cosine = jnp.concatenate([cosine, cosine], axis=1)
    sine_part = jnp.concatenate([-sine_part, sine_part], axis=1)
    visible = jnp.where(item_flag == 1, length, prefix)
    tables = table_halves(mixed_table)
    onehots = (ids_here[:, :, None] == vocab_index).astype(bf16)
    halves = 2 if items_here % 2 == 0 else 1
    per_half = items_here // halves
    chosen = [slice(half * per_half, (half + 1) * per_half) for half in range(halves)]
    context_rows, log_sums, w_in, w_out = second_call(
        item_bits, seq_bits, visible, onehots, tables, cosine, sine_part, own_in, own_out
    )
    w_in = w_in.reshape(width, 2 * ff_part)
    w_out = w_out.reshape(width, ff_part)
    contexts = [context_rows[part].reshape(per_half * span, width) for part in chosen]

    kept = []
    for half, part in enumerate(chosen):
        own_ids = input_ids[part].reshape(-1)
        onehot = (own_ids[:, None] == vocab_index[None, :]).astype(bf16)
        inputs = contract_cols(onehot, table)
        branch = dot(contexts[half], w_dense) + b_dense
        hidden, normed_one, inverse_one = norm_forward(
            deep_alpha * inputs + branch, gain_one, shift_one
        )
        kept.append(
            dict(
                onehot=onehot,
                hidden=hidden,
                normed_one=normed_one,
                inverse_one=inverse_one,
                shared=gather_four(lines, hidden.astype(bf16)),
            )
        )
    for half, part in enumerate(chosen):
        one = kept[half]
        gate_up = dot(one["shared"], w_in) + in_bias
        up_part, gate = gate_up[:, :ff_part], gate_up[:, ff_part:]
        below = 0.5 * (1.0 + lax.erf(gate * (0.5**0.5)))
        activated = gate * below
        slope = below + gate * jnp.exp(-0.5 * gate * gate) * (1.0 / math.sqrt(2.0 * math.pi))
        product_low = (up_part * activated).astype(bf16)
        one["act"] = activated.astype(bf16)
        one["slope"] = (up_part * slope).astype(bf16)
        one["product"] = product_low
        mlp_branch = sum_four(lines, contract_cols(product_low, w_out).astype(bf16)) + b_down
        layer_out, normed_two, inverse_two = norm_forward(
            deep_alpha * one["hidden"] + mlp_branch, gain_two, shift_two
        )
        one["layer_out"] = layer_out.astype(bf16)
        grad_top = cotangent[part].reshape(per_half * span, width).astype(f32)
        grad_resid_two, one["gain_two"], one["shift_two"] = norm_backward(
            grad_top, normed_two, inverse_two, gain_two
        )
        grad_mlp_low = grad_resid_two.astype(bf16)
        one["grad_resid_two"] = grad_resid_two
        one["down_sum"] = jnp.sum(grad_mlp_low.astype(f32), axis=0)
        one["grad_shared"] = gather_four(lines, grad_mlp_low)

    def total(function):
        result = function(kept[0])
        for one in kept[1:]:
            result = result + function(one)
        return result

    for one in kept:
        grad_product = dot(one["grad_shared"], w_out)
        one["grad_in"] = jnp.concatenate(
            [
                grad_product * one["act"].astype(f32),
                grad_product * one["slope"].astype(f32),
            ],
            axis=1,
        ).astype(bf16)
        one["in_sum"] = jnp.sum(one["grad_in"].astype(f32), axis=0)
        grad_hidden = (
            sum_four(lines, contract_cols(one["grad_in"], w_in).astype(bf16))
            + deep_alpha * one["grad_resid_two"]
        )
        grad_resid_one, one["gain_one"], one["shift_one"] = norm_backward(
            grad_hidden, one["normed_one"], one["inverse_one"], gain_one
        )
        grad_branch_low = grad_resid_one.astype(bf16)
        one["grad_branch"] = grad_branch_low
        one["grad_resid_one"] = grad_resid_one
        one["branch_sum"] = jnp.sum(grad_branch_low.astype(f32), axis=0)
        grad_context = contract_cols(grad_branch_low, w_dense).astype(bf16)
        grad_context = lax.all_to_all(
            jnp.transpose(
                grad_context.reshape(per_half, span, seq_size, heads_here * HEAD), (0, 2, 1, 3)
            ),
            "seq",
            split_axis=1,
            concat_axis=1,
            tiled=True,
        )
        one["grad_context"] = grad_context.reshape(per_half, length, heads_here * HEAD)

    vectors = jnp.stack(
        [
            total(lambda one: one[name])
            for name in ("gain_one", "shift_one", "branch_sum", "gain_two", "shift_two", "down_sum")
        ],
        axis=1,
    )
    token_sum = total(
        lambda one: lax.dot_general(
            one["grad_resid_one"],
            one["onehot"].astype(f32),
            (((0,), (0,)), ((), ())),
            precision=lax.Precision.HIGHEST,
            preferred_element_type=f32,
        )
    )
    grad_dense = sum(
        contract_rows(contexts[half], one["grad_branch"]) for half, one in enumerate(kept)
    )
    by_rows = jnp.concatenate(
        [grad_dense, token_sum, jnp.pad(vectors, ((0, 0), (0, 128 - vectors.shape[1])))], axis=1
    ).astype(bf16)
    row_dims = item_bits[::-1] + seq_bits[::-1]
    by_rows = by_rows.reshape((2,) * len(row_dims) + (rows_here, -1))
    by_rows = halve(lines, by_rows, len(row_dims) - 1, *seq_bits[0])
    grad_out_weight = total(lambda one: contract_rows(one["grad_shared"], one["product"]))
    grad_in_weight = total(lambda one: contract_rows(one["shared"], one["grad_in"]))
    group_dims = (2,) * (len(item_bits) + len(outer_bits)) + (members * rows_here, -1)
    in_sum = total(lambda one: one["in_sum"]).reshape(2, ff_part)
    in_all = lax.dynamic_update_slice(
        jnp.zeros((2, ff_all), f32), in_sum, (0, member * ff_part)
    ).reshape(-1, 128)
    w_slice = gather_merge(lines, w_block[None], item_bits).reshape(width, packed_width)
    spread, token_all, in_part, out_part, by_rows, in_all = third_call(
        item_bits,
        seq_bits,
        visible,
        onehots,
        tables,
        cosine,
        sine_part,
        log_sums,
        w_slice.T,
        jnp.concatenate([one["grad_context"] for one in kept], axis=0),
        grad_in_weight.astype(bf16).reshape(group_dims),
        grad_out_weight.astype(bf16).reshape(group_dims),
        by_rows,
        in_all,
    )
    grad_resid_one = jnp.concatenate([one["grad_resid_one"] for one in kept], axis=0)
    input_grads = spread.astype(f32) + deep_alpha * grad_resid_one.reshape(spread.shape)
    token_all = jnp.transpose(token_all, (2, 0, 1, 3)).reshape(vocab, -1)

    def from_members(part):
        taken = jnp.transpose(part, (1, 0, 2)).reshape(rows_here, ff_all)
        return taken[:, :ff_width].astype(f32)

    grad_up = from_members(in_part[..., :ff_part])
    grad_gate = from_members(in_part[..., ff_part:])
    grad_down = from_members(out_part)
    by_rows = by_rows.astype(f32)
    grad_dense = by_rows[:, :width]
    token_sum = by_rows[:, width : width + vocab]
    own_vectors = by_rows[:, width + vocab :].T
    in_all = in_all.reshape(2, ff_all)
    grad_up_bias = in_all[:, :ff_width].reshape(-1)

    grad_heads = dot(embedding, token_all)
    grad_heads_bias = lax.dynamic_slice_in_dim(
        jnp.sum(token_all.astype(f32), axis=0),
        (item_place * seq_size + seq_place) * heads_bias.shape[0],
        heads_bias.shape[0],
        0,
    )
    embed_grad = 0.1 * (contract_cols(heads_weight, token_all) + deep_alpha * token_sum)
    return (
        jnp.concatenate([one["layer_out"] for one in kept], axis=0).reshape(
            items_here, span, width
        ),
        input_grads,
        embed_grad,
        grad_heads,
        grad_heads_bias,
        grad_dense,
        own_vectors[2],
        own_vectors[0],
        own_vectors[1],
        jnp.concatenate([grad_up, grad_gate], axis=1),
        grad_up_bias,
        grad_down.T,
        own_vectors[5],
        own_vectors[3],
        own_vectors[4],
    )


def solution(mesh):
    in_specs = (
        P("items", "seq"),
        P("items", "seq"),
        P("items"),
        P("items"),
        P("items", "seq", None),
        P(("items", "seq"), None),
        P(("items", "seq"), None),
        P(("items", "seq")),
        P(("items", "seq"), None),
        P(("items", "seq")),
        P(("items", "seq")),
        P(("items", "seq")),
        P(("items", "seq"), None),
        P(),
        P(None, ("items", "seq")),
        P(("items", "seq")),
        P(("items", "seq")),
        P(("items", "seq")),
    )
    out_specs = (
        P("items", "seq", None),
        P("items", "seq", None),
        P(("items", "seq"), None),
        P(("items", "seq"), None),
        P(("items", "seq")),
        P(("items", "seq"), None),
        P(("items", "seq")),
        P(("items", "seq")),
        P(("items", "seq")),
        P(("items", "seq"), None),
        P(),
        P(None, ("items", "seq")),
        P(("items", "seq")),
        P(("items", "seq")),
        P(("items", "seq")),
    )
    return jax.shard_map(
        on_device, mesh=mesh, in_specs=in_specs, out_specs=out_specs, check_vma=False
    )
```

time: 1730 us -> 1280 us (0.74)
  Pallas kernels: 0 us -> 702 us
  waiting for transfers between devices: 636 us -> 169 us
  local copies, waits for them, and re-layouts: 333 us -> 73.1 us
  matrix products: 373 us -> 228 us
  starting transfers between devices: 137 us -> 12.6 us
  other arithmetic: 178 us -> 81.2 us
  blocking collectives: 63.2 us -> 0 us
    pallas_call x0 -> x3, Pallas kernels: none -> 702 us  [the longest x1 374 us: third_call(): pl.pallas_call(functools.partial(third_kernel, item_bits, seq_bits), in_s...]
    ppermute x119 -> x19, waiting for transfers between devices: 615 us -> 156 us  [swap(): got = lax.ppermute(part, axis, [(j, j ^ bit) for j in range(size)])]
    dot_general x56 -> x2, matrix products: 110 us -> 3.82 us  [on_device(): lax.dot_general(one['grad_resid_one'], one['onehot'].astype(f32), (((0,),...]
    ppermute x119 -> x19, starting transfers between devices: 97.8 us -> 3.87 us  [swap(): got = lax.ppermute(part, axis, [(j, j ^ bit) for j in range(size)])]
    unnamed x645 -> x212, local copies, waits for them, and re-layouts: 89 us -> 22.5 us
    all_gather x1 -> x0, blocking collectives: 63.2 us -> none  [on_device(): everyone = lax.all_gather(flat, both, axis=0, tiled=True).reshape(count, -1)]
    dynamic_update_slice x45 -> x2, local copies, waits for them, and re-layouts: 62.7 us -> 0.26 us  [the longest x1 0.24 us: on_device(): lax.dynamic_update_slice(jnp.zeros((16, heads_weight.shape[1]), bf16), he...]
    slice x37 -> x6, local copies, waits for them, and re-layouts: 54.6 us -> 4.53 us  [the longest x1 2.76 us: on_device(): context_rows[part].reshape(per_half * span, width)]
  transfers between devices with their start and end apart: 128 -> 21, of which waited for: 46 -> 12; matrix products, arithmetic and copies ran while one was open for 48% -> 19% of each run, Pallas kernels for 0% -> 0%
where the time goes in v2:
time: 1280 us; the launch traced here: 1270 us
  Pallas kernels  702 us (55%)
  matrix products  228 us (18%)
  waiting for transfers between devices  169 us (13%)
  other arithmetic  81.2 us (6%)
  local copies, waits for them, and re-layouts  73.1 us (6%)
    pallas_call x1, Pallas kernels, third_call(): pl.pallas_call(functools.partial(third_kernel, item_bits, seq_bits), in_s...  374 us
    pallas_call x1, Pallas kernels, second_call(): pl.pallas_call(functools.partial(second_kernel, item_bits, seq_bits), in_...  182 us
    ppermute x19, waiting for transfers between devices, swap(): got = lax.ppermute(part, axis, [(j, j ^ bit) for j in range(size)])  156 us
    pallas_call x1, Pallas kernels, first_call(): pl.pallas_call(functools.partial(first_kernel, item_bits, seq_bits, row_c...  146 us
    dot_general x6, matrix products, contract_rows(): lax.dot_general(left, right, (((0,), (0,)), ((), ())), preferred_element_...  83.5 us
    dot_general x7, matrix products, dot(): return jnp.dot(left, right, preferred_element_type=f32)  81 us
    dot_general x9, matrix products, contract_cols(): lax.dot_general(left, right, (((1,), (1,)), ((), ())), preferred_element_...  59.4 us
  transfers between devices with their start and end apart: 21, of which 12 were waited for; matrix products, arithmetic and copies ran while one was open for 19% of the time, Pallas kernels for 0%

profile of v2, /device:TPU:0, one launch (start us, length us, event | category | flops | bytes accessed | tf_op | source)
XLA Modules:
  0.0 1268.5 jit_solution(1736212527935384053)
XLA Ops:
  8.8 145.8 %first.1 = (bf16[4,8,96,128]{3,2,1,0:T(8,128)(2,1)S(1)}, f32[128,768]{1,0:T(8,128)S(1)}, bf16[8,80,768]{2,1,0:T(8,128)(2,1)S(1)}, bf16[4,4,2,64,2048]{4,3,2,1,0:...) custom-call(bf16[96,128]{1,0:T(8,128)(2,1)S(1)} %pad_bitcast_fusion.small_ref, ...), custom_call_target="tpu_custom_call" | custom-call | tf_op jit(solution)/shard_map/first/pallas_call | solution.py:331
  165.2 181.9 %second.1 = (bf16[4,128,2048]{2,1,0:T(8,128)(2,1)}, f32[4,2,1,1024]{3,2,1,0:T(1,128)S(1)}, bf16[8,256,2816]{2,1,0:T(8,128)(2,1)}, bf16[8,256,1408]{2,1,0:T(8,128)(2,1)}) custom-call(s32[4]{0:T(128)S(1)} %compare_select_fusion.visible_ref, bf16[4,1024,128]{2,1,0:T(8,128)(2,1)S(1)} %fusion.36.onehot_ref, ...), custom_call_target="tpu_custom_call" | custom-call | tf_op jit(solution)/shard_map/second/pallas_call | solution.py:515
  369.3 24.3 %collective-permute-done = bf16[256,2048]{1,0:T(8,128)(2,1)S(1)} collective-permute-done((bf16[256,2048]{1,0:T(8,128)(2,1)S(1)}, bf16[256,2048]{1,0:T(8,128)(2,1)S(1)}, u32[]{:S(2)}, u32[]{:S(2)}) %collective-permute-start) | collective-permute-done | bytes 1048608 | tf_op jit(solution)/shard_map/ppermute | solution.py:34
  396.6 25.4 %collective-permute-done.2 = bf16[256,2048]{1,0:T(8,128)(2,1)} collective-permute-done((bf16[256,2048]{1,0:T(8,128)(2,1)}, bf16[256,2048]{1,0:T(8,128)(2,1)}, u32[]{:S(2)}, u32[]{:S(2)}) %collective-permute-start.2) | collective-permute-done | bytes 1048608 | tf_op jit(solution)/shard_map/ppermute | solution.py:34
  424.0 17.2 %convolution_add_fusion.1 = f32[1024,2816]{1,0:T(8,128)S(1)} fusion(bf16[2048,2816]{1,0:T(8,128)(2,1)} %bitcast.218, f32[2816]{0:T(1024)S(1)} %add.327, bf16[512,2048]{1,0:T(8,128)(2,1)} %collective-permute-done.1, bf16[256,2048]{1,0:T(8,128)(2,1)S(1)} %copy-done.39, bf16[256,2048]{1,0:T(8,128)(2,1)S(1)} %get-tuple-element.147), kind=kOutput, calls=%fused_computation.12 | convolution fusion | flops 11826626560 | bytes 27274240 | tf_op jit(solution)/shard_map/dot_general | solution.py:100
  463.4 23.0 %collective-permute-done.5 = bf16[256,2048]{1,0:T(8,128)(2,1)S(1)} collective-permute-done((bf16[256,2048]{1,0:T(8,128)(2,1)}, bf16[256,2048]{1,0:T(8,128)(2,1)S(1)}, u32[]{:S(2)}, u32[]{:S(2)}) %collective-permute-start.5) | collective-permute-done | bytes 1048608 | tf_op jit(solution)/shard_map/ppermute | solution.py:34
  491.3 18.5 %convolution_add_fusion = f32[1024,2816]{1,0:T(8,128)S(1)} fusion(bf16[2048,2816]{1,0:T(8,128)(2,1)} %bitcast.219, f32[2816]{0:T(1024)S(1)} %add.327, bf16[512,2048]{1,0:T(8,128)(2,1)} %collective-permute-done.3, bf16[256,2048]{1,0:T(8,128)(2,1)} %collective-permute-done.2, bf16[256,2048]{1,0:T(8,128)(2,1)} %get-tuple-element.66), kind=kOutput, calls=%fused_computation.11 | convolution fusion | flops 11826626560 | bytes 27274240 | tf_op jit(solution)/shard_map/dot_general | solution.py:100
  529.9 18.1 %collective-permute-done.10 = bf16[1,512,768]{2,1,0:T(8,128)(2,1)} collective-permute-done((bf16[1,512,768]{2,1,0:T(8,128)(2,1)S(1)}, bf16[1,512,768]{2,1,0:T(8,128)(2,1)}, u32[]{:S(2)}, u32[]{:S(2)}) %collective-permute-start.10) | collective-permute-done | bytes 786464 | tf_op jit(solution)/shard_map/ppermute | solution.py:34
  557.8 27.4 %collective-permute-done.11 = bf16[2,512,768]{2,1,0:T(8,128)(2,1)} collective-permute-done((bf16[2,512,768]{2,1,0:T(8,128)(2,1)S(1)}, bf16[2,512,768]{2,1,0:T(8,128)(2,1)}, u32[]{:S(2)}, u32[]{:S(2)}) %collective-permute-start.11) | collective-permute-done | bytes 1572896 | tf_op jit(solution)/shard_map/ppermute | solution.py:34
  600.1 15.9 %multiply_convert_fusion.3 = (bf16[1024,1408]{1,0:T(8,128)(2,1)S(1)}, bf16[1024,1408]{1,0:T(8,128)(2,1)}) fusion(f32[1024,2816]{1,0:T(8,128)} %copy-done.26, bf16[2048,1408]{1,0:T(8,128)(2,1)} %bitcast.222, bf16[512,2048]{1,0:T(8,128)(2,1)S(1)} %copy-done.94, bf16[256,2048]{1,0:T(8,128)(2,1)S(1)} %copy-done.59, bf16[256,2048]{1,0:T(8,128)(2,1)S(1)} %get-tuple-element.70), kind=kOutput, calls=%fused_computation.30 | convolution fusion | flops 5944115200 | bytes 27262976 | tf_op jit(solution)/shard_map/dot_general | solution.py:100
  623.0 17.3 %convolution_convert_fusion.1 = bf16[1024,2048]{1,0:T(8,128)(2,1)} fusion(bf16[2048,2816]{1,0:T(8,128)(2,1)} %bitcast.220, bf16[1024,1408]{1,0:T(8,128)(2,1)} %get-tuple-element.130, bf16[1024,1408]{1,0:T(8,128)(2,1)S(1)} %get-tuple-element.129), kind=kOutput, calls=%fused_computation.49 | convolution fusion | flops 11824791552 | bytes 21495808 | tf_op jit(solution)/shard_map/dot_general | solution.py:96
  645.1 16.1 %multiply_convert_fusion.1 = (bf16[1024,1408]{1,0:T(8,128)(2,1)}, bf16[1024,1408]{1,0:T(8,128)(2,1)}) fusion(f32[1024,2816]{1,0:T(8,128)} %copy-done.27, bf16[2048,1408]{1,0:T(8,128)(2,1)} %bitcast.223, bf16[512,2048]{1,0:T(8,128)(2,1)} %collective-permute-done.13, bf16[256,2048]{1,0:T(8,128)(2,1)S(1)} %collective-permute-done.12, ...), kind=kOutput, calls=%fused_computation.28 | convolution fusion | flops 5944115200 | bytes 27262976 | tf_op jit(solution)/shard_map/dot_general | solution.py:100
  661.1 18.0 %convolution_convert_fusion = bf16[1024,2048]{1,0:T(8,128)(2,1)} fusion(bf16[2048,2816]{1,0:T(8,128)(2,1)} %bitcast.221, bf16[1024,1408]{1,0:T(8,128)(2,1)} %get-tuple-element.132, bf16[1024,1408]{1,0:T(8,128)(2,1)} %get-tuple-element.131), kind=kOutput, calls=%fused_computation.48 | convolution fusion | flops 11824791552 | bytes 21495808 | tf_op jit(solution)/shard_map/dot_general | solution.py:96
  682.2 20.3 %fusion.42 = f32[2048,2816]{1,0:T(8,128)} fusion(bf16[512,2048]{1,0:T(8,128)(2,1)} %collective-permute-done.3, bf16[256,2048]{1,0:T(8,128)(2,1)} %collective-permute-done.2, bf16[256,2048]{1,0:T(8,128)(2,1)} %get-tuple-element.66, bf16[1024,1408]{1,0:T(8,128)(2,1)} %get-tuple-element.132, bf16[1024,1408]{1,0:T(8,128)(2,1)} %get-tuple-element.131), kind=kOutput, calls=%fused_computation.137 | convolution fusion | flops 11835277312 | bytes 33030144 | tf_op jit(solution)/shard_map/dot_general | solution.py:92
  707.1 19.1 %add_convert_fusion = bf16[2048,2816]{1,0:T(8,128)(2,1)} fusion(f32[2048,2816]{1,0:T(8,128)} %fusion.42, bf16[512,2048]{1,0:T(8,128)(2,1)} %collective-permute-done.1, bf16[256,2048]{1,0:T(8,128)(2,1)S(1)} %copy-done.40, bf16[256,2048]{1,0:T(8,128)(2,1)S(1)} %copy-done.30, bf16[1024,1408]{1,0:T(8,128)(2,1)} %get-tuple-element.130, ...), kind=kOutput, calls=%fused_computation | convolution fusion | flops 11846811648 | bytes 44564480 | tf_op jit(solution)/shard_map/dot_general | solution.py:92
  736.6 19.9 %collective-permute-done.17 = bf16[256,2048]{1,0:T(8,128)(2,1)S(1)} collective-permute-done((bf16[256,2048]{1,0:T(8,128)(2,1)S(1)}, bf16[256,2048]{1,0:T(8,128)(2,1)S(1)}, u32[]{:S(2)}, u32[]{:S(2)}) %collective-permute-start.17) | collective-permute-done | bytes 1048608 | tf_op jit(solution)/shard_map/ppermute | solution.py:34
  761.5 8.3 fusion.67
  774.1 11.5 add_convert_fusion.1
  788.2 8.0 pad_maximum_fusion
  807.0 11.7 fusion.39
  838.1 12.6 add_convert_fusion.2
  856.9 7.7 all-to-all-done.1
  867.4 7.3 fusion.dense_ref
  874.7 374.3 %third.1 = (bf16[4,128,2048]{2,1,0:T(8,128)(2,1)}, bf16[8,2,128,384]{3,2,1,0:T(8,128)(2,1)}, bf16[4,64,2816]{2,1,0:T(8,128)(2,1)}, bf16[4,64,1408]{2,1,0:T(8,128...) custom-call(s32[4]{0:T(128)} %copy-done.8, bf16[4,1024,128]{2,1,0:T(8,128)(2,1)} %copy-done, ...), custom_call_target="tpu_custom_call" | custom-call | tf_op jit(solution)/shard_map/third/pallas_call | solution.py:930
  (405 shorter events, 216.3 us)
Async XLA Ops:
  162.7 184.3 %copy-start = (bf16[4,1024,128]{2,1,0:T(8,128)(2,1)}, bf16[4,1024,128]{2,1,0:T(8,128)(2,1)S(1)}, u32[]{:S(2)}) copy-start(bf16[4,1024,128]{2,1,0:T(8,128)(2,1)S(1)} %fusion.36.onehot_ref) | copy-start | bytes 3145732
  165.2 185.3 %copy-start.1 = (f32[1024,128]{1,0:T(8,128)}, f32[1024,128]{1,0:T(8,128)S(1)}, u32[]{:S(2)}) copy-start(f32[1024,128]{1,0:T(8,128)S(1)} %get-tuple-element.162.cosine_ref) | copy-start | bytes 1572868
  165.2 185.3 %copy-start.2 = (f32[1024,128]{1,0:T(8,128)}, f32[1024,128]{1,0:T(8,128)S(1)}, u32[]{:S(2)}) copy-start(f32[1024,128]{1,0:T(8,128)S(1)} %get-tuple-element.163.sine_ref) | copy-start | bytes 1572868
  369.3 24.3 %collective-permute-start = (bf16[256,2048]{1,0:T(8,128)(2,1)S(1)}, bf16[256,2048]{1,0:T(8,128)(2,1)S(1)}, u32[]{:S(2)}, u32[]{:S(2)}) collective-permute-start(bf16[256,2048]{1,0:T(8,128)(2,1)S(1)} %get-tuple-element.147), channel_id=1, source_target_pairs={{0,2},{1,3},{2,0},{3,1},{4,6},{5,7},{6,4},{7,5},{8,10},{9,11},{10,... | collective-permute-start | bytes 3145736 | tf_op jit(solution)/shard_map/ppermute | solution.py:34
  396.2 27.7 %collective-permute-start.1 = (bf16[512,2048]{1,0:T(8,128)(2,1)}, bf16[512,2048]{1,0:T(8,128)(2,1)}, u32[]{:S(2)}, u32[]{:S(2)}) collective-permute-start(bf16[512,2048]{1,0:T(8,128)(2,1)} %pad_maximum_fusion.7), channel_id=1, source_target_pairs={{0,1},{1,0},{2,3},{3,2},{4,5},{5,4},{6,7},{7,6},{8,9},{9,8},{10,11... | collective-permute-start | bytes 6291464 | tf_op jit(solution)/shard_map/ppermute | solution.py:34
  396.2 25.9 %collective-permute-start.2 = (bf16[256,2048]{1,0:T(8,128)(2,1)}, bf16[256,2048]{1,0:T(8,128)(2,1)}, u32[]{:S(2)}, u32[]{:S(2)}) collective-permute-start(bf16[256,2048]{1,0:T(8,128)(2,1)} %get-tuple-element.66), channel_id=1, source_target_pairs={{0,2},{1,3},{2,0},{3,1},{4,6},{5,7},{6,4},{7,5},{8,10},{9,11},{10,... | collective-permute-start | bytes 3145736 | tf_op jit(solution)/shard_map/ppermute | solution.py:34
  423.9 28.6 %collective-permute-start.3 = (bf16[512,2048]{1,0:T(8,128)(2,1)S(1)}, bf16[512,2048]{1,0:T(8,128)(2,1)}, u32[]{:S(2)}, u32[]{:S(2)}) collective-permute-start(bf16[512,2048]{1,0:T(8,128)(2,1)S(1)} %pad_maximum_fusion.8), channel_id=1, source_target_pairs={{0,1},{1,0},{2,3},{3,2},{4,5},{5,4},{6,7},{7,6},{8,9},{9,8},{10,11... | collective-permute-start | bytes 6291464 | tf_op jit(solution)/shard_map/ppermute | solution.py:34
  452.5 4.3 collective-permute-start.4
  460.8 25.6 %collective-permute-start.5 = (bf16[256,2048]{1,0:T(8,128)(2,1)}, bf16[256,2048]{1,0:T(8,128)(2,1)S(1)}, u32[]{:S(2)}, u32[]{:S(2)}) collective-permute-start(bf16[256,2048]{1,0:T(8,128)(2,1)} %split.111), channel_id=1, source_target_pairs={{0,2},{1,3},{2,0},{3,1},{4,6},{5,7},{6,4},{7,5},{8,10},{9,11},{10,... | collective-permute-start | bytes 3145736 | tf_op jit(solution)/shard_map/ppermute | solution.py:34
  490.9 24.7 %collective-permute-start.6 = (bf16[256,2048]{1,0:T(8,128)(2,1)S(1)}, bf16[256,2048]{1,0:T(8,128)(2,1)S(1)}, u32[]{:S(2)}, u32[]{:S(2)}) collective-permute-start(bf16[256,2048]{1,0:T(8,128)(2,1)S(1)} %get-tuple-element.70), channel_id=1, source_target_pairs={{0,2},{1,3},{2,0},{3,1},{4,6},{5,7},{6,4},{7,5},{8,10},{9,11},{10,... | collective-permute-start | bytes 3145736 | tf_op jit(solution)/shard_map/ppermute | solution.py:34
  515.9 11.2 collective-permute-start.7
  527.1 23.5 %collective-permute-start.8 = (bf16[512,2048]{1,0:T(8,128)(2,1)}, bf16[512,2048]{1,0:T(8,128)(2,1)}, u32[]{:S(2)}, u32[]{:S(2)}) collective-permute-start(bf16[512,2048]{1,0:T(8,128)(2,1)} %split.73), channel_id=1, source_target_pairs={{0,1},{1,0},{2,3},{3,2},{4,5},{5,4},{6,7},{7,6},{8,9},{9,8},{10,11... | collective-permute-start | bytes 6291464 | tf_op jit(solution)/shard_map/ppermute | solution.py:34
  529.1 19.0 %collective-permute-start.10 = (bf16[1,512,768]{2,1,0:T(8,128)(2,1)S(1)}, bf16[1,512,768]{2,1,0:T(8,128)(2,1)}, u32[]{:S(2)}, u32[]{:S(2)}) collective-permute-start(bf16[1,512,768]{2,1,0:T(8,128)(2,1)S(1)} %bitcast.200), channel_id=1, source_target_pairs={{0,8},{8,0},{16,24},{24,16},{1,9},{9,1},{17,25},{25,17},{2,10},{10... | collective-permute-start | bytes 2359304 | tf_op jit(solution)/shard_map/ppermute | solution.py:34
  550.2 34.9 %collective-permute-start.11 = (bf16[2,512,768]{2,1,0:T(8,128)(2,1)S(1)}, bf16[2,512,768]{2,1,0:T(8,128)(2,1)}, u32[]{:S(2)}, u32[]{:S(2)}) collective-permute-start(bf16[2,512,768]{2,1,0:T(8,128)(2,1)S(1)} %maximum_select_fusion.1), channel_id=1, source_target_pairs={{0,16},{8,24},{16,0},{24,8},{1,17},{9,25},{17,1},{25,9},{2,18},{10... | collective-permute-start | bytes 4718600 | tf_op jit(solution)/shard_map/ppermute | solution.py:34
  556.8 36.9 %collective-permute-start.9 = (bf16[256,2048]{1,0:T(8,128)(2,1)}, bf16[256,2048]{1,0:T(8,128)(2,1)}, u32[]{:S(2)}, u32[]{:S(2)}) collective-permute-start(bf16[256,2048]{1,0:T(8,128)(2,1)} %split.110), channel_id=1, source_target_pairs={{0,2},{1,3},{2,0},{3,1},{4,6},{5,7},{6,4},{7,5},{8,10},{9,11},{10,... | collective-permute-start | bytes 3145736 | tf_op jit(solution)/shard_map/ppermute | solution.py:34
  598.7 22.7 %collective-permute-start.12 = (bf16[256,2048]{1,0:T(8,128)(2,1)S(1)}, bf16[256,2048]{1,0:T(8,128)(2,1)S(1)}, u32[]{:S(2)}, u32[]{:S(2)}) collective-permute-start(bf16[256,2048]{1,0:T(8,128)(2,1)S(1)} %get-tuple-element.76), channel_id=1, source_target_pairs={{0,2},{1,3},{2,0},{3,1},{4,6},{5,7},{6,4},{7,5},{8,10},{9,11},{10,... | collective-permute-start | bytes 3145736 | tf_op jit(solution)/shard_map/ppermute | solution.py:34
  623.0 21.5 %collective-permute-start.13 = (bf16[512,2048]{1,0:T(8,128)(2,1)}, bf16[512,2048]{1,0:T(8,128)(2,1)}, u32[]{:S(2)}, u32[]{:S(2)}) collective-permute-start(bf16[512,2048]{1,0:T(8,128)(2,1)} %pad_maximum_fusion.11), channel_id=1, source_target_pairs={{0,1},{1,0},{2,3},{3,2},{4,5},{5,4},{6,7},{7,6},{8,9},{9,8},{10,11... | collective-permute-start | bytes 6291464 | tf_op jit(solution)/shard_map/ppermute | solution.py:34
  644.5 58.0 %collective-permute-start.14 = (bf16[512,2048]{1,0:T(8,128)(2,1)}, bf16[512,2048]{1,0:T(8,128)(2,1)}, u32[]{:S(2)}, u32[]{:S(2)}) collective-permute-start(bf16[512,2048]{1,0:T(8,128)(2,1)} %split.77), channel_id=1, source_target_pairs={{0,1},{1,0},{2,3},{3,2},{4,5},{5,4},{6,7},{7,6},{8,9},{9,8},{10,11... | collective-permute-start | bytes 6291464 | tf_op jit(solution)/shard_map/ppermute | solution.py:34
  706.8 25.4 %collective-permute-start.15 = (bf16[256,2048]{1,0:T(8,128)(2,1)}, bf16[256,2048]{1,0:T(8,128)(2,1)}, u32[]{:S(2)}, u32[]{:S(2)}) collective-permute-start(bf16[256,2048]{1,0:T(8,128)(2,1)} %split.109), channel_id=1, source_target_pairs={{0,2},{1,3},{2,0},{3,1},{4,6},{5,7},{6,4},{7,5},{8,10},{9,11},{10,... | collective-permute-start | bytes 3145736 | tf_op jit(solution)/shard_map/ppermute | solution.py:34
  707.1 19.2 %collective-permute-start.16 = (bf16[512,2048]{1,0:T(8,128)(2,1)}, bf16[512,2048]{1,0:T(8,128)(2,1)}, u32[]{:S(2)}, u32[]{:S(2)}) collective-permute-start(bf16[512,2048]{1,0:T(8,128)(2,1)} %split.81), channel_id=1, source_target_pairs={{0,1},{1,0},{2,3},{3,2},{4,5},{5,4},{6,7},{7,6},{8,9},{9,8},{10,11... | collective-permute-start | bytes 6291464 | tf_op jit(solution)/shard_map/ppermute | solution.py:34
  732.2 24.3 %collective-permute-start.17 = (bf16[256,2048]{1,0:T(8,128)(2,1)S(1)}, bf16[256,2048]{1,0:T(8,128)(2,1)S(1)}, u32[]{:S(2)}, u32[]{:S(2)}) collective-permute-start(bf16[256,2048]{1,0:T(8,128)(2,1)S(1)} %split.108), channel_id=1, source_target_pairs={{0,2},{1,3},{2,0},{3,1},{4,6},{5,7},{6,4},{7,5},{8,10},{9,11},{10,... | collective-permute-start | bytes 3145736 | tf_op jit(solution)/shard_map/ppermute | solution.py:34
  801.2 66.2 %collective-permute-start.18 = (bf16[2,2,2,2,64,2304]{5,4,3,2,1,0:T(8,128)(2,1)}, bf16[2,2,2,2,64,2304]{5,4,3,2,1,0:T(8,128)(2,1)}, u32[]{:S(2)}, u32[]{:S(2)}) collective-permute-start(bf16[2,2,2,2,64,2304]{5,4,3,2,1,0:T(8,128)(2,1)} %dynamic-slice_bitcast_fusion), channel_id=1, source_target_pairs={{0,1},{1,0},{2,3},{3,2},{4,5},{5,4},{6,7},{7,6},{8,9},{9,8},{10,11... | collective-permute-start | bytes 14155784 | tf_op jit(solution)/shard_map/ppermute | solution.py:34
  802.7 30.8 %all-to-all-start = ((bf16[2,8,128,256]{3,2,0,1:T(8,128)(2,1)}), bf16[2,8,128,256]{3,2,0,1:T(8,128)(2,1)}, u32[]{:S(2)}, u32[]{:S(2)}) async-start(bf16[2,8,128,256]{3,2,0,1:T(8,128)(2,1)} %bitcast.171), calls=%async_computation | async-start | bytes 2097152 | tf_op jit(solution)/shard_map/all_to_all | solution.py:1193
  833.6 31.1 %all-to-all-start.1 = ((bf16[2,8,128,256]{3,2,0,1:T(8,128)(2,1)}), bf16[2,8,128,256]{3,2,0,1:T(8,128)(2,1)}, u32[]{:S(2)}, u32[]{:S(2)}) async-start(bf16[2,8,128,256]{3,2,0,1:T(8,128)(2,1)} %bitcast.195), calls=%async_computation.1 | async-start | bytes 2097152 | tf_op jit(solution)/shard_map/all_to_all | solution.py:1193
  (100 other events, 1552.7 us)

commit v3 on v2

--- a/solution.py
+++ b/solution.py
@@ -76,18 +76,6 @@
     return (masks[0] ^ (bit if axis == "items" else 0), masks[1] ^ (bit if axis == "seq" else 0))
 
 
-def gather_four(lines, own):
-    chip = jnp.concatenate([own, lines.swap(own, "seq", 2)], axis=0)
-    return jnp.concatenate([chip, lines.swap(chip, "seq", 1)], axis=0)
-
-
-def sum_four(lines, parts):
-    mine, other = jnp.split(parts, 2, axis=0)
-    mine = mine.astype(f32) + lines.swap(other, "seq", 1).astype(f32)
-    own, far = jnp.split(mine, 2, axis=0)
-    return own + lines.swap(far.astype(bf16), "seq", 2).astype(f32)
-
-
 def contract_rows(left, right):
     return lax.dot_general(left, right, (((0,), (0,)), ((), ())), preferred_element_type=f32)
 
@@ -124,6 +112,21 @@
     by_head = jnp.transpose(mixed_table.reshape(vocab, -1, 3 * HEAD), (1, 0, 2))
     high = lax.reduce_precision(by_head, 8, 7)
     return jnp.concatenate([high.astype(bf16), (by_head - high).astype(bf16)], axis=1)
+
+
+def norm_rows(rows):
+    center = rows - jnp.mean(rows, axis=-1, keepdims=True)
+    inverse = lax.rsqrt(jnp.mean(center * center, axis=-1, keepdims=True) + epsilon)
+    return center * inverse, inverse
+
+
+def norm_rows_back(grad, normed, inverse, gain):
+    scaled = grad * gain
+    return inverse * (
+        scaled
+        - jnp.mean(scaled, axis=-1, keepdims=True)
+        - normed * jnp.mean(scaled * normed, axis=-1, keepdims=True)
+    )
 
 
 MESH = pl.DeviceIdType.MESH
@@ -431,13 +434,23 @@
     table_ref,
     cosine_ref,
     sine_ref,
+    own_onehot_ref,
+    embed_ref,
+    vector_ref,
+    dense_ref,
     own_in_ref,
     own_out_ref,
     context_ref,
     lse_ref,
     in_ref,
     out_ref,
+    shared_ref,
+    normed_ref,
+    inverse_ref,
     context_scr,
+    dense_scr,
+    resid_scr,
+    low_scr,
     send_sems,
     recv_sems,
     local_sems,
@@ -446,10 +459,12 @@
     items_here, length, features = context_scr.shape
     heads_here = features // HEAD
     span = length // seq_size
+    width = dense_ref.shape[0]
     seq_place = lax.axis_index("seq")
     outer_bits = seq_bits[2:]
     greet(partners(seq_size, item_bits))
     copies = Copies(send_sems, recv_sems, local_sems)
+    dense_copy = copies.move(dense_ref, dense_scr)
     spreads = [
         Spread(copies, own_in_ref, in_ref, outer_bits, item_bits),
         Spread(copies, own_out_ref, out_ref, outer_bits, item_bits),
@@ -485,11 +500,57 @@
                 arrivals.append(copies.send(source, target, (0, mask)))
             else:
                 local.append(copies.move(source, target))
+    wait_all(arrivals)
+    for copy in local:
+        copy.wait()
     if stepwise:
         for one in spreads:
             one.cross_own()
-        for one in spreads:
-            one.spread_outer()
+
+    dense_copy.wait()
+    rows_all = items_here * span
+    tile = 256
+
+    @pl.loop(0, width // tile)
+    def _(order):
+        place = pl.ds(pl.multiple_of(order * tile, tile), tile)
+        branch = dot(context_ref[...].reshape(rows_all, width), dense_scr[:, place])
+        inputs = contract_cols(own_onehot_ref[...], embed_ref[place, :])
+        resid_scr[:, place] = deep_alpha * inputs + (branch + vector_ref[5:6, place])
+
+    block = 32
+    near, far = ("seq", 1), ("seq", 2)
+    far_copies, near_copies, own_copies = [], [], []
+    for item in range(items_here):
+
+        @pl.loop(0, span // block)
+        def _(order):
+            start = pl.multiple_of(order * block, block)
+            rows = pl.ds(pl.multiple_of(item * span + start, block), block)
+            normed, inverse = norm_rows(resid_scr[rows, :])
+            normed_ref[rows, :] = normed
+            inverse_ref[rows, :] = jnp.broadcast_to(inverse, (block, 128))
+            hidden = normed * vector_ref[0:1, :] + vector_ref[1:2, :]
+            low_scr[item, pl.ds(start, block), :] = hidden.astype(bf16)
+
+        source = low_scr.at[item]
+        far_copies.append(copies.send(source, shared_ref.at[item, 1], mask_of(far)))
+        near_copies.append(copies.send(source, shared_ref.at[item, 2], mask_of(near)))
+        own_copies.append(copies.move(source, shared_ref.at[item, 0]))
+
+    def pass_on(item):
+        far_copies[item].wait_recv()
+        part = shared_ref.at[item, 1]
+        near_copies.append(copies.send(part, shared_ref.at[item, 3], mask_of(near)))
+
+    if stepwise:
+        spreads[0].spread_outer()
+    pass_on(0)
+    if stepwise:
+        spreads[1].spread_outer()
+    for item in range(1, items_here):
+        pass_on(item)
+    if stepwise:
         for one in spreads:
             one.cross_outer()
     else:
@@ -497,42 +558,76 @@
             one.plain()
     for one in spreads:
         one.end()
-    wait_all(arrivals)
-    for copy in local:
+    wait_all(near_copies)
+    for copy in own_copies:
         copy.wait()
     copies.end()
 
 
-def second_call(item_bits, seq_bits, visible, onehots, tables, cosine, sine_part, own_in, own_out):
+def second_call(
+    item_bits,
+    seq_bits,
+    visible,
+    onehots,
+    tables,
+    cosine,
+    sine_part,
+    own_onehot,
+    embed,
+    vectors,
+    w_dense,
+    own_in,
+    own_out,
+):
     items_here, length, vocab = onehots.shape
     heads_here = tables.shape[0]
     features = heads_here * HEAD
     seq_size = 2 ** len(seq_bits)
+    span = length // seq_size
+    width = w_dense.shape[0]
     groups = 2 ** (len(item_bits) + len(seq_bits)) // 4
     any_space = pl.BlockSpec(memory_space=pl.ANY)
     near_space = pl.BlockSpec(memory_space=pltpu.VMEM)
-    spare = 4 * groups + items_here * seq_size
+    spare = 4 * groups + items_here * (seq_size + 4)
     return pl.pallas_call(
         functools.partial(second_kernel, item_bits, seq_bits),
-        in_specs=[pl.BlockSpec(memory_space=pltpu.SMEM)] + [near_space] * 4 + [any_space] * 2,
-        out_specs=[any_space, near_space, any_space, any_space],
+        in_specs=[pl.BlockSpec(memory_space=pltpu.SMEM)] + [near_space] * 7 + [any_space] * 3,
+        out_specs=[near_space] * 2 + [any_space] * 3 + [near_space] * 2,
         out_shape=[
-            jax.ShapeDtypeStruct((items_here, length // seq_size, features * seq_size), bf16),
+            jax.ShapeDtypeStruct((items_here, span, width), bf16),
             jax.ShapeDtypeStruct((items_here, heads_here, 1, length), f32),
             jax.ShapeDtypeStruct((groups,) + own_in.shape, bf16),
             jax.ShapeDtypeStruct((groups,) + own_out.shape, bf16),
+            jax.ShapeDtypeStruct((items_here, 4, span, width), bf16),
+            jax.ShapeDtypeStruct((items_here * span, width), f32),
+            jax.ShapeDtypeStruct((items_here * span, 128), f32),
         ],
         scratch_shapes=[
             pltpu.VMEM((items_here, length, features), bf16),
+            pltpu.VMEM((width, width), bf16),
+            pltpu.VMEM((items_here * span, width), f32),
+            pltpu.VMEM((items_here, span, width), bf16),
             pltpu.SemaphoreType.DMA((spare,)),
             pltpu.SemaphoreType.DMA((spare,)),
-            pltpu.SemaphoreType.DMA((8,)),
+            pltpu.SemaphoreType.DMA((16,)),
         ],
         compiler_params=pltpu.CompilerParams(
-            collective_id=1, has_side_effects=True, vmem_limit_bytes=48 * 2**20
+            collective_id=1, has_side_effects=True, vmem_limit_bytes=56 * 2**20
         ),
         name="second",
-    )(visible, onehots, tables, cosine, sine_part, own_in, own_out)
+    )(
+        visible,
+        onehots,
+        tables,
+        cosine,
+        sine_part,
+        own_onehot,
+        embed,
+        vectors,
+        w_dense,
+        own_in,
+        own_out,
+    )
 
 
 def leading(ref):
@@ -738,6 +833,9 @@
     sums_scr[...] = jnp.zeros_like(sums_scr)
     tile = 256
     flying = {}
+    bias_scr[0] = bias_ref[...]
+    bias_steps = seq_bits + item_bits
+    bias_copies = [copies.send(bias_scr.at[0], bias_got.at[0], mask_of(bias_steps[0]))]
     for stage in range(items_here + len(seq_bits)):
         if stage < items_here:
 
@@ -822,43 +920,66 @@
         if stage == 0:
             for one in out_sums:
                 one.start()
-        if stage == 2:
-            dense_sum.start()
         if stage == items_here:
             for one in in_sums:
                 one.advance()
-
-    for one in out_sums:
-        one.advance()
+            dense_sum.start()
+            sums_copy = copies.send(sums_scr.at[0], sums_got.at[0], mask_of(item_bits[0]))
+        if stage == items_here + 1:
+            for one in out_sums:
+                one.advance()
+        if stage == items_here + 2:
+            for one in in_sums:
+                one.advance()
+        bias_done = len(bias_copies)
+        if bias_done <= len(bias_steps):
+            bias_copies[-1].wait_recv()
+            bias_scr[bias_done] = bias_scr[bias_done - 1] + bias_got[bias_done - 1]
+            if bias_done < len(bias_steps):
+                bias_copies.append(
+                    copies.send(
+                        bias_scr.at[bias_done],
+                        bias_got.at[bias_done],
+                        mask_of(bias_steps[bias_done]),
+                    )
+                )
+            else:
+                bias_copies.append(None)
+                bias_sum_ref[...] = bias_scr[bias_done]
+
     for order, step in enumerate(item_bits):
-        copy = copies.send(sums_scr.at[order], sums_got.at[order], mask_of(step))
-        copy.wait_recv()
+        sums_copy.wait_recv()
         sums_scr[order + 1] = sums_scr[order] + sums_got[order]
+        if order + 1 < len(item_bits):
+            sums_copy = copies.send(
+                sums_scr.at[order + 1], sums_got.at[order + 1], mask_of(item_bits[order + 1])
+            )
     sums_all_ref[seq_place] = sums_scr[len(item_bits)].astype(bf16)
-    for one in in_sums + out_sums:
-        one.advance()
     known = [0]
+    arrivals = []
     for axis, bit in seq_bits[::-1]:
+        wait_all(arrivals)
         arrivals = []
         for mask in known:
             part = sums_all_ref.at[seq_place ^ mask]
             arrivals.append(copies.send(part, part, (0, bit)))
-        if bit == seq_bits[-1][1]:
+        known = known + [mask ^ bit for mask in known]
+        for one in out_sums:
+            if one.order < 2:
+                one.advance()
+        if dense_sum.order == 0:
             dense_sum.advance()
-        wait_all(arrivals)
-        known = known + [mask ^ bit for mask in known]
-    bias_scr[0] = bias_ref[...]
-    for order, step in enumerate(seq_bits + item_bits):
-        copy = copies.send(bias_scr.at[order], bias_got.at[order], mask_of(step))
-        copy.wait_recv()
-        bias_scr[order + 1] = bias_scr[order] + bias_got[order]
-    bias_sum_ref[...] = bias_scr[len(seq_bits) + len(item_bits)]
 
     while in_sums[0].order < len(dims):
         for one in in_sums + out_sums:
-            one.advance()
+            if one.order < len(dims):
+                one.advance()
         if dense_sum.order < len(dense_steps):
             dense_sum.advance()
+    while out_sums[0].order < len(dims):
+        for one in out_sums:
+            one.advance()
+    wait_all(arrivals)
     shares, local = [], []
     for sums, final, target in (
         (in_sums, in_final, in_part_ref),
@@ -982,21 +1103,360 @@
     )
 
 
-def norm_forward(residual, gain_vec, bias_vec):
-    center = residual - jnp.mean(residual, axis=-1, keepdims=True)
-    inverse = lax.rsqrt(jnp.mean(center * center, axis=-1, keepdims=True) + epsilon)
-    normed = center * inverse
-    return (normed * gain_vec + bias_vec, normed, inverse)
-
-
-def norm_backward(grad_out, normed, inverse, gain_vec):
-    scaled = grad_out * gain_vec
-    grad_in = inverse * (
-        scaled
-        - jnp.mean(scaled, axis=-1, keepdims=True)
-        - normed * jnp.mean(scaled * normed, axis=-1, keepdims=True)
-    )
-    return (grad_in, jnp.sum(grad_out * normed, axis=0), jnp.sum(grad_out, axis=0))
+def ff_kernel(
+    shared_ref,
+    normed_ref,
+    inverse_ref,
+    cotangent_ref,
+    in_ref,
+    out_ref,
+    vector_ref,
+    bias_ref,
+    product_ref,
+    saved_ref,
+    grad_shared_ref,
+    grad_in_ref,
+    layer_ref,
+    resid_ref,
+    sums_ref,
+    in_sum_ref,
+    rows_scr,
+    product_scr,
+    save_scr,
+    parts_scr,
+    near_got,
+    far_got,
+    low_scr,
+    grad_in_scr,
+    resid_scr,
+    normed_scr,
+    gate_scr,
+    send_sems,
+    recv_sems,
+    load_sems,
+    keep_sems,
+):
+    chunks, blocks, span, width = shared_ref.shape
+    group_rows = blocks * span
+    tiles = product_scr.shape[-1] // 128
+    tile = 256
+    near, far = ("seq", 1), ("seq", 2)
+    greet([mask_of(near), mask_of(far)])
+    copies = Copies(send_sems, recv_sems, None)
+    keeps, loads = {}, {}
+    state = {}
+    gain_one, shift_one, b_down, gain_two, shift_two = range(5)
+    for line in range(sums_ref.shape[0]):
+        sums_ref[line : line + 1, :] = jnp.zeros((1, width), f32)
+    in_sum_ref[...] = jnp.zeros_like(in_sum_ref)
+
+    def load(name, slot, source, target):
+        copy = pltpu.make_async_copy(source, target, load_sems.at[slot])
+        copy.start()
+        loads[name] = copy
+
+    def loaded(name):
+        loads.pop(name).wait()
+
+    def keep(name, slot, source, target):
+        copy = pltpu.make_async_copy(source, target, keep_sems.at[slot])
+        copy.start()
+        keeps[name] = copy
+
+    def keep_done(name):
+        if name in keeps:
+            keeps.pop(name).wait()
+
+    def load_shared(chunk):
+        slot = chunk % 2
+        load(("rows", slot), slot, shared_ref.at[chunk], rows_scr.at[slot])
+
+    def load_normed(chunk):
+        slot = chunk % 2
+        rows = pl.ds(chunk * span, span)
+        load(("normed", slot), 2 + slot, normed_ref.at[rows], normed_scr.at[slot])
+
+    def forward_gate(chunk):
+        slot = chunk % 2
+        loaded(("rows", slot))
+        if chunk + 1 < chunks:
+            load_shared(chunk + 1)
+        keep_done(("product", slot))
+        keep_done(("save", slot))
+        rows = rows_scr.at[slot]
+
+        def multiply(order, place):
+            columns = pl.ds(pl.multiple_of(order * tile, tile), tile)
+            gate_scr[place] = (
+                dot(rows[...].reshape(group_rows, width), in_ref[:, columns])
+                + bias_ref[:, columns]
+            )
+
+        def finish(order, place):
+            gate_up = gate_scr[place]
+            up_part, gate = gate_up[:, :128], gate_up[:, 128:]
+            below = 0.5 * (1.0 + lax.erf(gate * (0.5**0.5)))
+            activated = gate * below
+            slope = below + gate * jnp.exp(-0.5 * gate * gate) * (1.0 / math.sqrt(2.0 * math.pi))
+            columns = pl.ds(pl.multiple_of(order * 128, 128), 128)
+            product_scr[slot, :, columns] = (up_part * activated).astype(bf16)
+            save_scr[slot, 0, :, columns] = activated.astype(bf16)
+            save_scr[slot, 1, :, columns] = (up_part * slope).astype(bf16)
+
+        multiply(0, 0)
+
+        @pl.loop(0, (tiles - 1) // 2)
+        def _(pair):
+            finish(2 * pair, 0)
+            multiply(2 * pair + 1, 1)
+            finish(2 * pair + 1, 1)
+            multiply(2 * pair + 2, 0)
+
+        if tiles % 2 == 0:
+            multiply(tiles - 1, 1)
+            finish(tiles - 2, 0)
+            finish(tiles - 1, 1)
+        else:
+            finish(tiles - 1, 0)
+        keep(("product", slot), slot, product_scr.at[slot], product_ref.at[chunk])
+        keep(("save", slot), 2 + slot, save_scr.at[slot], saved_ref.at[chunk])
+
+    def send_near(name, slot):
+        source = parts_scr.at[slot, pl.ds(2, 2)]
+        state["near", name] = copies.send(source, near_got.at[slot], mask_of(near))
+
+    def free_parts(slot):
+        for key in ("near", "far"):
+            copy = state.pop((key, "of", slot), None)
+            if copy is not None:
+                copies.sent_now(copy)
+
+    def times_turned(name, slot, left, weights_ref):
+        free_parts(slot)
+
+        @pl.loop(0, width // tile)
+        def _(order):
+            place = pl.ds(pl.multiple_of(order * tile, tile), tile)
+            total = contract_cols(left[...], weights_ref[place, :])
+            parts_scr[slot, :, :, place] = total.astype(bf16).reshape(blocks, span, tile)
+
+        send_near(name, slot)
+        state["near", "of", slot] = state["near", name]
+
+    def forward_out(chunk):
+        times_turned(chunk, chunk % 2, product_scr.at[chunk % 2], out_ref)
+
+    def sum_near(name, chunk):
+        slot = chunk % 2
+        state["near", name].wait_recv()
+        add_into(parts_scr.at[slot, pl.ds(0, 2)], near_got.at[slot])
+        copy = copies.send(parts_scr.at[slot, 1], far_got.at[chunk], mask_of(far))
+        state["far", name] = copy
+        state["far", "of", slot] = copy
+
+    block = 32
+
+    def row_blocks(function):
+        @pl.loop(0, span // block)
+        def _(order):
+            function(pl.ds(pl.multiple_of(order * block, block), block))
+
+    def line(index):
+        return vector_ref[index : index + 1, :]
+
+    def add_sum(index, rows):
+        sums_ref[index : index + 1, :] += jnp.sum(rows, axis=0, keepdims=True)
+
+    def second_norm(chunk):
+        slot = chunk % 2
+        state["far", chunk].wait_recv()
+        loaded(("normed", slot))
+        for key in ("low near", "low far"):
+            copy = state.pop((key, slot), None)
+            if copy is not None:
+                copies.sent_now(copy)
+        keep_done(("low", slot))
+
+        def body(rows):
+            hidden = normed_scr[slot, rows] * line(gain_one) + line(shift_one)
+            mlp_branch = parts_scr[slot, 0, rows].astype(f32) + far_got[chunk, rows].astype(f32)
+            normed, inverse = norm_rows(deep_alpha * hidden + mlp_branch + line(b_down))
+            layer_ref[chunk, rows] = (normed * line(gain_two) + line(shift_two)).astype(bf16)
+            grad = cotangent_ref[chunk, rows].astype(f32)
+            resid = norm_rows_back(grad, normed, inverse, line(gain_two))
+            low = resid.astype(bf16)
+            resid_scr[chunk, rows] = resid
+            low_scr[slot, rows] = low
+            add_sum(3, grad * normed)
+            add_sum(4, grad)
+            add_sum(5, low.astype(f32))
+
+        row_blocks(body)
+        if chunk + 2 < chunks:
+            load_normed(chunk + 2)
+        source = low_scr.at[slot]
+        keep(("low", slot), 4 + slot, source, grad_shared_ref.at[chunk, 0])
+        state["low far", slot] = copies.send(source, grad_shared_ref.at[chunk, 1], mask_of(far))
+        state["low near", slot] = copies.send(source, grad_shared_ref.at[chunk, 2], mask_of(near))
+        state["grad far", chunk] = state["low far", slot]
+        state["grad near", chunk] = state["low near", slot]
+
+    def pass_on(chunk):
+        state["grad far", chunk].wait_recv()
+        part = grad_shared_ref.at[chunk, 1]
+        state["grad cross", chunk] = copies.send(
+            part, grad_shared_ref.at[chunk, 3], mask_of(near)
+        )
+
+    def load_grads(chunk):
+        slot = chunk % 2
+        keep_done(("low", slot))
+        state["grad near", chunk].wait_recv()
+        state["grad cross", chunk].wait_recv()
+        load(("rows", slot), slot, grad_shared_ref.at[chunk], rows_scr.at[slot])
+        keep_done(("save", slot))
+        load(("save", slot), 4 + slot, saved_ref.at[chunk], save_scr.at[slot])
+
+    def backward_gate(chunk):
+        slot = chunk % 2
+        loaded(("rows", slot))
+        loaded(("save", slot))
+        keep_done("grad in")
+        rows = rows_scr.at[slot]
+
+        def columns_of(first, count):
+            columns = pl.ds(pl.multiple_of(first * 128, 128), count * 128)
+            grad = dot(rows[...].reshape(group_rows, width), out_ref[:, columns])
+            for order in range(count):
+                part = grad[:, order * 128 : (order + 1) * 128]
+                saved = pl.ds(pl.multiple_of((first + order) * 128, 128), 128)
+                for which in range(2):
+                    low = (part * save_scr[slot, which, :, saved].astype(f32)).astype(bf16)
+                    place = pl.ds(
+                        pl.multiple_of((2 * (first + order) + which) * 128, 128), 128
+                    )
+                    grad_in_scr[:, place] = low
+                    in_sum_ref[:, place] += jnp.sum(low.astype(f32), axis=0, keepdims=True)
+
+        @pl.loop(0, tiles // 2)
+        def _(pair):
+            columns_of(2 * pair, 2)
+
+        if tiles % 2:
+            columns_of(tiles - 1, 1)
+        keep("grad in", 6, grad_in_scr, grad_in_ref.at[chunk])
+
+    def backward_in(chunk):
+        times_turned(("back", chunk), chunk % 2, grad_in_scr, in_ref)
+
+    def first_norm(chunk):
+        slot = chunk % 2
+        state["far", ("back", chunk)].wait_recv()
+        loaded(("normed", slot))
+
+        def body(rows):
+            grad = parts_scr[slot, 0, rows].astype(f32) + far_got[chunk, rows].astype(f32)
+            grad = grad + deep_alpha * resid_scr[chunk, rows]
+            normed = normed_scr[slot, rows]
+            place = pl.ds(pl.multiple_of(chunk * span + rows.start, block), block)
+            resid = norm_rows_back(grad, normed, inverse_ref[place, 0:1], line(gain_one))
+            resid_scr[chunk, rows] = resid
+            add_sum(0, grad * normed)
+            add_sum(1, grad)
+            add_sum(2, resid.astype(bf16).astype(f32))
+
+        row_blocks(body)
+        if chunk + 2 < chunks:
+            load_normed(chunk + 2)
+        keep(("resid", chunk), 7 + chunk, resid_scr.at[chunk], resid_ref.at[chunk])
+
+    load_shared(0)
+    load_normed(0)
+    load_normed(1)
+    last = chunks - 1
+    for chunk in range(chunks):
+        forward_gate(chunk)
+        if chunk >= 1:
+            sum_near(chunk - 1, chunk - 1)
+        if chunk >= 2:
+            second_norm(chunk - 2)
+        if chunk >= 3:
+            pass_on(chunk - 3)
+        forward_out(chunk)
+    sum_near(last, last)
+    second_norm(last - 1)
+    pass_on(last - 2)
+    waiting = [("norm", last), ("pass", last - 1), ("pass", last)]
+    for chunk in range(chunks):
+        if chunk == 0:
+            load_grads(0)
+        backward_gate(chunk)
+        if waiting and waiting[0][0] == "norm":
+            second_norm(waiting.pop(0)[1])
+            load_normed(0)
+            load_normed(1)
+        if waiting:
+            pass_on(waiting.pop(0)[1])
+        if chunk >= 1:
+            sum_near(("back", chunk - 1), chunk - 1)
+        if chunk >= 2:
+            first_norm(chunk - 2)
+        if chunk + 1 < chunks:
+            if chunk + 1 == last and waiting:
+                pass_on(waiting.pop(0)[1])
+            load_grads(chunk + 1)
+        backward_in(chunk)
+    sum_near(("back", last), last)
+    first_norm(last - 1)
+    first_norm(last)
+    for name in list(keeps):
+        keep_done(name)
+    copies.end()
+
+
+def ff_call(shared, normed, inverse, cotangent, w_in, w_out, vectors, in_bias):
+    chunks, blocks, span, width = shared.shape
+    group_rows = blocks * span
+    ff_part = w_out.shape[1]
+    any_space = pl.BlockSpec(memory_space=pl.ANY)
+    near_space = pl.BlockSpec(memory_space=pltpu.VMEM)
+    spare = 8 * chunks
+    return pl.pallas_call(
+        ff_kernel,
+        in_specs=[any_space, any_space] + [near_space] * 6,
+        out_specs=[any_space] * 4 + [near_space, any_space, near_space, near_space],
+        out_shape=[
+            jax.ShapeDtypeStruct((chunks, group_rows, ff_part), bf16),
+            jax.ShapeDtypeStruct((chunks, 2, group_rows, ff_part), bf16),
+            jax.ShapeDtypeStruct((chunks, blocks, span, width), bf16),
+            jax.ShapeDtypeStruct((chunks, group_rows, 2 * ff_part), bf16),
+            jax.ShapeDtypeStruct((chunks, span, width), bf16),
+            jax.ShapeDtypeStruct((chunks, span, width), f32),
+            jax.ShapeDtypeStruct((8, width), f32),
+            jax.ShapeDtypeStruct((1, 2 * ff_part), f32),
+        ],
+        scratch_shapes=[
+            pltpu.VMEM((2, blocks, span, width), bf16),
+            pltpu.VMEM((2, group_rows, ff_part), bf16),
+            pltpu.VMEM((2, 2, group_rows, ff_part), bf16),
+            pltpu.VMEM((2, blocks, span, width), bf16),
+            pltpu.VMEM((2, 2, span, width), bf16),
+            pltpu.VMEM((chunks, span, width), bf16),
+            pltpu.VMEM((2, span, width), bf16),
+            pltpu.VMEM((group_rows, 2 * ff_part), bf16),
+            pltpu.VMEM((chunks, span, width), f32),
+            pltpu.VMEM((2, span, width), f32),
+            pltpu.VMEM((2, group_rows, 256), f32),
+            pltpu.SemaphoreType.DMA((spare,)),
+            pltpu.SemaphoreType.DMA((spare,)),
+            pltpu.SemaphoreType.DMA((6,)),
+            pltpu.SemaphoreType.DMA((7 + chunks,)),
+        ],
+        compiler_params=pltpu.CompilerParams(
+            collective_id=3, has_side_effects=True, vmem_limit_bytes=60 * 2**20
+        ),
+        name="feed_forward",
+    )(shared, normed, inverse, cotangent, w_in, w_out, vectors, in_bias)
 
 
 def on_device(
@@ -1070,9 +1530,20 @@
         padded = jnp.pad(part, ((0, 0), (0, ff_all - ff_width)))
         return jnp.transpose(padded.reshape(rows_here, 2, 2, ff_part), (1, 2, 0, 3))
 
-    parts_in = jnp.concatenate(
-        [by_member(up_weight[:, :ff_width]), by_member(up_weight[:, ff_width:])], axis=3
-    )
+    tiles = ff_part // 128
+
+    def woven(up, gate):
+        shape = up.shape[:-1] + (tiles, 128)
+        return jnp.stack([up.reshape(shape), gate.reshape(shape)], axis=-2).reshape(
+            up.shape[:-1] + (2 * ff_part,)
+        )
+
+    def unwoven(both_parts):
+        parts = both_parts.reshape(both_parts.shape[:-1] + (tiles, 2, 128))
+        shape = both_parts.shape[:-1] + (ff_part,)
+        return parts[..., 0, :].reshape(shape), parts[..., 1, :].reshape(shape)
+
+    parts_in = woven(by_member(up_weight[:, :ff_width]), by_member(up_weight[:, ff_width:]))
     parts_out = by_member(down_weight.T)
     everyone, mixed_table, w_block, w_dense, own_in, own_out = first_call(
         item_bits,
@@ -1096,7 +1567,8 @@
     in_bias = jnp.pad(
         up_bias.astype(f32).reshape(2, ff_width), ((0, 0), (0, ff_all - ff_width))
     )
-    in_bias = lax.dynamic_slice(in_bias, (0, member * ff_part), (2, ff_part)).reshape(-1)
+    in_bias = lax.dynamic_slice(in_bias, (0, member * ff_part), (2, ff_part))
+    in_bias = woven(in_bias[:1], in_bias[1:])
 
     vocab_index = jnp.arange(vocab, dtype=jnp.int32)
     positions = jnp.arange(length, dtype=f32)
@@ -1109,127 +1581,73 @@
     visible = jnp.where(item_flag == 1, length, prefix)
     tables = table_halves(mixed_table)
     onehots = (ids_here[:, :, None] == vocab_index).astype(bf16)
-    halves = 2 if items_here % 2 == 0 else 1
-    per_half = items_here // halves
-    chosen = [slice(half * per_half, (half + 1) * per_half) for half in range(halves)]
-    context_rows, log_sums, w_in, w_out = second_call(
-        item_bits, seq_bits, visible, onehots, tables, cosine, sine_part, own_in, own_out
-    )
-    w_in = w_in.reshape(width, 2 * ff_part)
-    w_out = w_out.reshape(width, ff_part)
-    contexts = [context_rows[part].reshape(per_half * span, width) for part in chosen]
-
-    kept = []
-    for half, part in enumerate(chosen):
-        own_ids = input_ids[part].reshape(-1)
-        onehot = (own_ids[:, None] == vocab_index[None, :]).astype(bf16)
-        inputs = contract_cols(onehot, table)
-        branch = dot(contexts[half], w_dense) + b_dense
-        hidden, normed_one, inverse_one = norm_forward(
-            deep_alpha * inputs + branch, gain_one, shift_one
-        )
-        kept.append(
-            dict(
-                onehot=onehot,
-                hidden=hidden,
-                normed_one=normed_one,
-                inverse_one=inverse_one,
-                shared=gather_four(lines, hidden.astype(bf16)),
-            )
-        )
-    for half, part in enumerate(chosen):
-        one = kept[half]
-        gate_up = dot(one["shared"], w_in) + in_bias
-        up_part, gate = gate_up[:, :ff_part], gate_up[:, ff_part:]
-        below = 0.5 * (1.0 + lax.erf(gate * (0.5**0.5)))
-        activated = gate * below
-        slope = below + gate * jnp.exp(-0.5 * gate * gate) * (1.0 / math.sqrt(2.0 * math.pi))
-        product_low = (up_part * activated).astype(bf16)
-        one["act"] = activated.astype(bf16)
-        one["slope"] = (up_part * slope).astype(bf16)
-        one["product"] = product_low
-        mlp_branch = sum_four(lines, contract_cols(product_low, w_out).astype(bf16)) + b_down
-        layer_out, normed_two, inverse_two = norm_forward(
-            deep_alpha * one["hidden"] + mlp_branch, gain_two, shift_two
-        )
-        one["layer_out"] = layer_out.astype(bf16)
-        grad_top = cotangent[part].reshape(per_half * span, width).astype(f32)
-        grad_resid_two, one["gain_two"], one["shift_two"] = norm_backward(
-            grad_top, normed_two, inverse_two, gain_two
-        )
-        grad_mlp_low = grad_resid_two.astype(bf16)
-        one["grad_resid_two"] = grad_resid_two
-        one["down_sum"] = jnp.sum(grad_mlp_low.astype(f32), axis=0)
-        one["grad_shared"] = gather_four(lines, grad_mlp_low)
-
-    def total(function):
-        result = function(kept[0])
-        for one in kept[1:]:
-            result = result + function(one)
-        return result
-
-    for one in kept:
-        grad_product = dot(one["grad_shared"], w_out)
-        one["grad_in"] = jnp.concatenate(
-            [
-                grad_product * one["act"].astype(f32),
-                grad_product * one["slope"].astype(f32),
-            ],
-            axis=1,
-        ).astype(bf16)
-        one["in_sum"] = jnp.sum(one["grad_in"].astype(f32), axis=0)
-        grad_hidden = (
-            sum_four(lines, contract_cols(one["grad_in"], w_in).astype(bf16))
-            + deep_alpha * one["grad_resid_two"]
-        )
-        grad_resid_one, one["gain_one"], one["shift_one"] = norm_backward(
-            grad_hidden, one["normed_one"], one["inverse_one"], gain_one
-        )
-        grad_branch_low = grad_resid_one.astype(bf16)
-        one["grad_branch"] = grad_branch_low
-        one["grad_resid_one"] = grad_resid_one
-        one["branch_sum"] = jnp.sum(grad_branch_low.astype(f32), axis=0)
-        grad_context = contract_cols(grad_branch_low, w_dense).astype(bf16)
-        grad_context = lax.all_to_all(
-            jnp.transpose(
-                grad_context.reshape(per_half, span, seq_size, heads_here * HEAD), (0, 2, 1, 3)
-            ),
-            "seq",
-            split_axis=1,
-            concat_axis=1,
-            tiled=True,
-        )
-        one["grad_context"] = grad_context.reshape(per_half, length, heads_here * HEAD)
-
-    vectors = jnp.stack(
-        [
-            total(lambda one: one[name])
-            for name in ("gain_one", "shift_one", "branch_sum", "gain_two", "shift_two", "down_sum")
-        ],
-        axis=1,
-    )
-    token_sum = total(
-        lambda one: lax.dot_general(
-            one["grad_resid_one"],
-            one["onehot"].astype(f32),
-            (((0,), (0,)), ((), ())),
-            precision=lax.Precision.HIGHEST,
-            preferred_element_type=f32,
-        )
-    )
-    grad_dense = sum(
-        contract_rows(contexts[half], one["grad_branch"]) for half, one in enumerate(kept)
-    )
+    own_onehot = (input_ids.reshape(-1)[:, None] == vocab_index[None, :]).astype(bf16)
+    vectors = jnp.stack([gain_one, shift_one, b_down, gain_two, shift_two, b_dense])
+    vectors = jnp.pad(vectors, ((0, 2), (0, 0)))
+    context, log_sums, w_in, w_out, shared, normed, inverse = second_call(
+        item_bits,
+        seq_bits,
+        visible,
+        onehots,
+        tables,
+        cosine,
+        sine_part,
+        own_onehot,
+        table,
+        vectors,
+        w_dense,
+        own_in,
+        own_out,
+    )
+    product, _, grad_shared, grad_in, layer_out, grad_resid, sums, in_sum = ff_call(
+        shared,
+        normed,
+        inverse,
+        cotangent,
+        w_in.reshape(width, 2 * ff_part),
+        w_out.reshape(width, ff_part),
+        vectors,
+        in_bias,
+    )
+    rows_all = items_here * span
+    group_all = members * rows_all
+    context = context.reshape(rows_all, width)
+    grad_resid = grad_resid.reshape(rows_all, width)
+    grad_branch = grad_resid.astype(bf16)
+    grad_context = contract_cols(grad_branch, w_dense).astype(bf16)
+    grad_context = lax.all_to_all(
+        jnp.transpose(
+            grad_context.reshape(items_here, span, seq_size, heads_here * HEAD), (0, 2, 1, 3)
+        ),
+        "seq",
+        split_axis=1,
+        concat_axis=1,
+        tiled=True,
+    ).reshape(items_here, length, heads_here * HEAD)
+
+    vector_sums = sums[:6].T
+    token_sum = lax.dot_general(
+        grad_resid,
+        own_onehot.astype(f32),
+        (((0,), (0,)), ((), ())),
+        precision=lax.Precision.HIGHEST,
+        preferred_element_type=f32,
+    )
+    grad_dense = contract_rows(context, grad_branch)
     by_rows = jnp.concatenate(
-        [grad_dense, token_sum, jnp.pad(vectors, ((0, 0), (0, 128 - vectors.shape[1])))], axis=1
+        [grad_dense, token_sum, jnp.pad(vector_sums, ((0, 0), (0, 122)))], axis=1
     ).astype(bf16)
     row_dims = item_bits[::-1] + seq_bits[::-1]
     by_rows = by_rows.reshape((2,) * len(row_dims) + (rows_here, -1))
     by_rows = halve(lines, by_rows, len(row_dims) - 1, *seq_bits[0])
-    grad_out_weight = total(lambda one: contract_rows(one["grad_shared"], one["product"]))
-    grad_in_weight = total(lambda one: contract_rows(one["shared"], one["grad_in"]))
+    grad_out_weight = contract_rows(
+        grad_shared.reshape(group_all, width), product.reshape(group_all, ff_part)
+    )
+    grad_in_weight = contract_rows(
+        shared.reshape(group_all, width), grad_in.reshape(group_all, 2 * ff_part)
+    )
     group_dims = (2,) * (len(item_bits) + len(outer_bits)) + (members * rows_here, -1)
-    in_sum = total(lambda one: one["in_sum"]).reshape(2, ff_part)
+    in_sum = jnp.concatenate(unwoven(in_sum), axis=0)
     in_all = lax.dynamic_update_slice(
         jnp.zeros((2, ff_all), f32), in_sum, (0, member * ff_part)
     ).reshape(-1, 128)
@@ -1244,22 +1662,20 @@
         sine_part,
         log_sums,
         w_slice.T,
-        jnp.concatenate([one["grad_context"] for one in kept], axis=0),
+        grad_context,
         grad_in_weight.astype(bf16).reshape(group_dims),
         grad_out_weight.astype(bf16).reshape(group_dims),
         by_rows,
         in_all,
     )
-    grad_resid_one = jnp.concatenate([one["grad_resid_one"] for one in kept], axis=0)
-    input_grads = spread.astype(f32) + deep_alpha * grad_resid_one.reshape(spread.shape)
+    input_grads = spread.astype(f32) + deep_alpha * grad_resid.reshape(spread.shape)
     token_all = jnp.transpose(token_all, (2, 0, 1, 3)).reshape(vocab, -1)
 
     def from_members(part):
         taken = jnp.transpose(part, (1, 0, 2)).reshape(rows_here, ff_all)
         return taken[:, :ff_width].astype(f32)
 
-    grad_up = from_members(in_part[..., :ff_part])
-    grad_gate = from_members(in_part[..., ff_part:])
+    grad_up, grad_gate = (from_members(part) for part in unwoven(in_part))
     grad_down = from_members(out_part)
     by_rows = by_rows.astype(f32)
     grad_dense = by_rows[:, :width]
@@ -1277,9 +1693,7 @@
     )
     embed_grad = 0.1 * (contract_cols(heads_weight, token_all) + deep_alpha * token_sum)
     return (
-        jnp.concatenate([one["layer_out"] for one in kept], axis=0).reshape(
-            items_here, span, width
-        ),
+        layer_out,
         input_grads,
         embed_grad,
         grad_heads,

time: 1280 us -> 1120 us (0.88)
  Pallas kernels: 702 us -> 900 us
  waiting for transfers between devices: 169 us -> 15.4 us
  matrix products: 228 us -> 75.6 us
  other arithmetic: 81.2 us -> 34.4 us
    pallas_call x0 -> x1, Pallas kernels: none -> 182 us  [ff_call(): pl.pallas_call(ff_kernel, in_specs=[any_space, any_space] + [near_space]...]
    ppermute x19 -> x3, waiting for transfers between devices: 156 us -> 15.4 us  [swap(): got = lax.ppermute(part, axis, [(j, j ^ bit) for j in range(size)])]
    dot_general x7 -> x1, matrix products: 81 us -> 1.8 us  [dot(): return jnp.dot(left, right, preferred_element_type=f32)]
    pallas_call x1, Pallas kernels: 182 us -> 244 us  [second_call(): pl.pallas_call(functools.partial(second_kernel, item_bits, seq_bits), in_...]
    dot_general x9 -> x2, matrix products: 59.4 us -> 9.16 us  [contract_cols(): lax.dot_general(left, right, (((1,), (1,)), ((), ())), preferred_element_...]
    pallas_call x1, Pallas kernels: 374 us -> 327 us  [third_call(): pl.pallas_call(functools.partial(third_kernel, item_bits, seq_bits), in_s...]
    dot_general x6 -> x3, matrix products: 83.5 us -> 59.5 us  [contract_rows(): lax.dot_general(left, right, (((0,), (0,)), ((), ())), preferred_element_...]
    reduce_sum x16 -> x0, other arithmetic: 22.8 us -> none  [the longest x4 8.58 us: norm_backward(): jnp.sum(grad_out * normed, axis=0)]
  transfers between devices with their start and end apart: 21 -> 4, of which waited for: 12 -> 1; matrix products, arithmetic and copies ran while one was open for 19% -> 6% of each run, Pallas kernels for 0% -> 0%
where the time goes in v3:
time: 1120 us; the launch traced here: 1110 us
  Pallas kernels  900 us (80%)
  matrix products  75.6 us (7%)
  local copies, waits for them, and re-layouts  75.3 us (7%)
  other arithmetic  34.4 us (3%)
  waiting for transfers between devices  15.4 us (1%)
    pallas_call x1, Pallas kernels, third_call(): pl.pallas_call(functools.partial(third_kernel, item_bits, seq_bits), in_s...  327 us
    pallas_call x1, Pallas kernels, second_call(): pl.pallas_call(functools.partial(second_kernel, item_bits, seq_bits), in_...  244 us
    pallas_call x1, Pallas kernels, ff_call(): pl.pallas_call(ff_kernel, in_specs=[any_space, any_space] + [near_space]...  182 us
    pallas_call x1, Pallas kernels, first_call(): pl.pallas_call(functools.partial(first_kernel, item_bits, seq_bits, row_c...  146 us
    dot_general x3, matrix products, contract_rows(): lax.dot_general(left, right, (((0,), (0,)), ((), ())), preferred_element_...  59.5 us
  transfers between devices with their start and end apart: 4, of which 1 were waited for; matrix products, arithmetic and copies ran while one was open for 6% of the time, Pallas kernels for 0%

profile of v3, /device:TPU:0, one launch (start us, length us, event | category | flops | bytes accessed | tf_op | source)
XLA Modules:
  0.0 1110.2 jit_solution(14059346271322160720)
XLA Ops:
  2.0 5.5 concatenate.47
  12.0 3.3 copy.88
  15.4 3.8 reshape.273.in_ref
  24.6 146.0 %first.1 = (bf16[4,8,96,128]{3,2,1,0:T(8,128)(2,1)S(1)}, f32[128,768]{1,0:T(8,128)S(1)}, bf16[8,80,768]{2,1,0:T(8,128)(2,1)S(1)}, bf16[4,4,2,64,2048]{4,3,2,1,0:...) custom-call(bf16[96,128]{1,0:T(8,128)(2,1)S(1)} %copy-done.4, ...), custom_call_target="tpu_custom_call" | custom-call | tf_op jit(solution)/shard_map/first/pallas_call | solution.py:334
  170.7 3.3 copy-done
  187.0 244.3 %second.1 = (bf16[4,128,2048]{2,1,0:T(8,128)(2,1)}, f32[4,2,1,1024]{3,2,1,0:T(1,128)}, bf16[8,256,2816]{2,1,0:T(8,128)(2,1)}, bf16[8,256,1408]{2,1,0:T(8,128)(2,...) custom-call(s32[4]{0:T(128)} %compare_select_fusion.1.visible_ref, ...), custom_call_target="tpu_custom_call" | custom-call | tf_op jit(solution)/shard_map/second/pallas_call | solution.py:592
  431.3 182.4 %feed_forward.1 = (bf16[4,512,1408]{2,1,0:T(8,128)(2,1)}, bf16[4,2,512,1408]{3,2,1,0:T(8,128)(2,1)}, bf16[4,4,128,2048]{3,2,1,0:T(8,128)(2,1)}, bf16[4,512,2816]...) custom-call(bf16[4,4,128,2048]{3,2,1,0:T(8,128)(2,1)} %get-tuple-ele, ...), custom_call_target="tpu_custom_call" | custom-call | tf_op jit(solution)/shard_map/feed_forward/pallas_call | solution.py:1424
  616.2 5.3 copy.96
  621.6 5.1 fusion.4
  629.7 8.6 bitcast_convert_fusion
  638.3 4.6 pad_maximum_fusion
  649.3 8.1 convolution_convert_fusion.2
  659.9 4.6 all-to-all-start
  664.8 31.4 %convolution_convert_fusion = bf16[2048,2816]{1,0:T(8,128)(2,1)} fusion(bf16[2048,2048]{1,0:T(8,128)(2,1)} %bitcast.141, bf16[2048,2816]{1,0:T(8,128)(2,1)} %bitcast.167), kind=kOutput, calls=%fused_computation.1 | convolution fusion | flops 23628087296 | bytes 31457280 | tf_op jit(solution)/shard_map/dot_general | solution.py:80
  698.9 19.5 %convolution_convert_fusion.1 = bf16[2048,1408]{1,0:T(8,128)(2,1)} fusion(bf16[2048,2048]{1,0:T(8,128)(2,1)} %bitcast.168, bf16[2048,1408]{1,0:T(8,128)(2,1)} %bitcast.169), kind=kOutput, calls=%fused_computation.5 | convolution fusion | flops 11814043648 | bytes 19922944 | tf_op jit(solution)/shard_map/dot_general | solution.py:80
  718.4 15.4 %collective-permute-done.1 = bf16[2,512,768]{2,1,0:T(8,128)(2,1)S(1)} collective-permute-done((bf16[2,512,768]{2,1,0:T(8,128)(2,1)S(1)}, bf16[2,512,768]{2,1,0:T(8,128)(2,1)S(1)}, u32[]{:S(2)}, u32[]{:S(2)}) %collective-permute-start.1) | collective-permute-done | bytes 1572896 | tf_op jit(solution)/shard_map/ppermute | solution.py:34
  734.4 2.9 copy.111
  737.2 3.1 copy.94
  740.4 7.4 fusion.dense_ref
  747.8 327.2 %third.1 = (bf16[4,128,2048]{2,1,0:T(8,128)(2,1)}, bf16[8,2,128,384]{3,2,1,0:T(8,128)(2,1)}, bf16[4,64,2816]{2,1,0:T(8,128)(2,1)}, bf16[4,64,1408]{2,1,0:T(8,128...) custom-call(s32[4]{0:T(128)} %compare_select_fusion.1.visible_ref, bf16[4,1024,128]{2,1,0:T(8,128)(2,1)} %fusion.3.onehot_ref, ...), custom_call_target="tpu_custom_call" | custom-call | tf_op jit(solution)/shard_map/third/pallas_call | solution.py:1051
  1082.5 3.1 reshape.296
  1085.6 7.8 slice_reduce_fusion.1
  1096.0 5.2 multiply_add_fusion
  1106.6 3.2 copy.144
  (135 shorter events, 57.2 us)
Async XLA Ops:
  9.5 1.4 copy-start.12
  9.5 1.3 copy-start.20
  15.4 7.5 copy-start.7
  170.7 3.3 copy-start
  174.0 1.1 copy-start.1
  177.4 6.2 copy-start.17
  177.5 7.0 copy-start.21
  177.6 7.0 copy-start.22
  621.6 5.1 copy-start.18
  642.9 5.0 copy-start.5
  647.9 92.5 %collective-permute-start.2 = (bf16[2,2,2,2,64,2304]{5,4,3,2,1,0:T(8,128)(2,1)}, bf16[2,2,2,2,64,2304]{5,4,3,2,1,0:T(8,128)(2,1)}, u32[]{:S(2)}, u32[]{:S(2)}) collective-permute-start(bf16[2,2,2,2,64,2304]{5,4,3,2,1,0:T(8,128)(2,1)} %dynamic-slice_bitcast_fusion), channel_id=1, source_target_pairs={{0,1},{1,0},{2,3},{3,2},{4,5},{5,4},{6,7},{7,6},{8,9},{9,8},{10,11... | collective-permute-start | bytes 14155784 | tf_op jit(solution)/shard_map/ppermute | solution.py:34
  659.9 77.4 %all-to-all-start = ((bf16[4,8,128,256]{3,2,0,1:T(8,128)(2,1)}), bf16[4,8,128,256]{3,2,0,1:T(8,128)(2,1)}, u32[]{:S(2)}, u32[]{:S(2)}) async-start(bf16[4,8,128,256]{3,2,0,1:T(8,128)(2,1)} %bitcast.121), calls=%async_computation | async-start | bytes 4194304 | tf_op jit(solution)/shard_map/all_to_all | solution.py:1618
  664.6 32.4 %collective-permute-start = (bf16[1,512,768]{2,1,0:T(8,128)(2,1)S(1)}, bf16[1,512,768]{2,1,0:T(8,128)(2,1)S(1)}, u32[]{:S(2)}, u32[]{:S(2)}) collective-permute-start(bf16[1,512,768]{2,1,0:T(8,128)(2,1)S(1)} %bitcast.145), channel_id=1, source_target_pairs={{0,8},{8,0},{16,24},{24,16},{1,9},{9,1},{17,25},{25,17},{2,10},{10... | collective-permute-start | bytes 2359304 | tf_op jit(solution)/shard_map/ppermute | solution.py:34
  664.8 31.4 %copy-start.19 = (f32[1,2816]{1,0:T(1,128)S(1)}, f32[1,2816]{1,0:T(1,128)}, u32[]{:S(2)}) copy-start(f32[1,2816]{1,0:T(1,128)} %get-tuple-element.72) | copy-start | bytes 33796
  697.2 36.6 %collective-permute-start.1 = (bf16[2,512,768]{2,1,0:T(8,128)(2,1)S(1)}, bf16[2,512,768]{2,1,0:T(8,128)(2,1)S(1)}, u32[]{:S(2)}, u32[]{:S(2)}) collective-permute-start(bf16[2,512,768]{2,1,0:T(8,128)(2,1)S(1)} %maximum_select_fusion.1), channel_id=1, source_target_pairs={{0,16},{8,24},{16,0},{24,8},{1,17},{9,25},{17,1},{25,9},{2,18},{10... | collective-permute-start | bytes 4718600 | tf_op jit(solution)/shard_map/ppermute | solution.py:34
  1075.0 2.3 copy-start.9
  1075.0 2.3 copy-start.15
  1075.0 4.2 copy-start.8
  1077.3 4.3 copy-start.6
  1094.4 1.6 copy-start.10
  1096.0 5.2 copy-start.13
  1101.2 1.3 copy-start.11
  1101.2 2.1 copy-start.16
  1101.2 2.8 copy-start.14
  (3 other events, 2.5 us)

commit v4 on v3

--- a/solution.py
+++ b/solution.py
@@ -49,20 +49,8 @@
     return (lax.axis_index(axis) // bit) % 2
 
 
-def in_order(own, got, place, dim):
-    return jnp.where(
-        place == 0, jnp.concatenate([own, got], axis=dim), jnp.concatenate([got, own], axis=dim)
-    )
-
-
 def pick(whole, place, dim):
     return lax.dynamic_index_in_dim(whole, place, dim, keepdims=False)
-
-
-def gather_merge(lines, own, steps):
-    for axis, bit in steps:
-        own = in_order(own, lines.swap(own, axis, bit), my_bit(axis, bit), 0)
-    return own
 
 
 def halve(lines, whole, dim, axis, bit):
@@ -205,6 +193,7 @@
     row_count,
     small_ref,
     heads_ref,
+    head_bias_ref,
     dense_ref,
     in_ref,
     out_ref,
@@ -231,47 +220,74 @@
     greet(partners(seq_size, item_bits))
     copies = Copies(send_sems, recv_sems, local_sems)
 
-    def head_columns(place):
-        return heads_ref.at[:, pl.ds(pl.multiple_of(place * columns, 128), columns)]
+    def head_columns(place, source):
+        return source.at[:, pl.ds(pl.multiple_of(place * columns, 128), columns)]
+
+    head_rows = [
+        (heads_ref, pl.ds(0, rows)),
+        (head_bias_ref, pl.ds(rows, row_count - rows)),
+    ]
 
     small = [copies.send(small_ref, everyone_ref.at[item_place, seq_place], mask_of(seq_bits[0]))]
     heads = [
-        copies.send(head_columns(seq_place ^ mask), block_scr.at[seq_place], (0, mask))
+        copies.send(
+            head_columns(seq_place ^ mask, source), block_scr.at[seq_place, place], (0, mask)
+        )
         for mask in range(1, seq_size)
+        for source, place in head_rows
     ]
     dense = [
         copies.send(dense_ref, dense_all_ref.at[item_place, chip, core], mask_of(seq_bits[1]))
     ]
+    mine = pl.ds(pl.multiple_of(member * rows, rows), rows)
     shares = []
-    for source, target in ((in_ref, own_in_ref), (out_ref, own_out_ref)):
-        mine = pl.ds(pl.multiple_of(member * rows, rows), rows)
+
+    def share(source, target):
         for mask in range(1, 4):
             other = member ^ mask
             shares.append(
                 copies.send(source.at[other // 2, other % 2], target.at[mine], (0, mask))
             )
+
     local = [
         copies.move(small_ref, everyone_ref.at[item_place, seq_place]),
         copies.move(dense_ref, dense_all_ref.at[item_place, chip, core]),
-        copies.move(head_columns(seq_place), block_scr.at[seq_place]),
-        copies.move(in_ref.at[member // 2, core], own_in_ref.at[mine]),
+        copies.move(head_columns(seq_place, heads_ref), block_scr.at[seq_place, head_rows[0][1]]),
+        copies.move(
+            head_columns(seq_place, head_bias_ref), block_scr.at[seq_place, head_rows[1][1]]
+        ),
+        copies.move(in_ref.at[member // 2, core], own_in_ref.at[0, mine]),
         copies.move(out_ref.at[member // 2, core], own_out_ref.at[mine]),
     ]
     for copy in local:
         copy.wait()
 
     for order in range(1, len(seq_bits)):
-        wait_all(small[-1:])
-        part = everyone_ref.at[item_place, aligned(seq_place, 2**order)]
-        small.append(copies.send(part, part, mask_of(seq_bits[order])))
         if order > 1:
             wait_all(dense[-1:])
             part = dense_all_ref.at[item_place, aligned(chip, 2 ** (order - 1)), core]
             dense.append(copies.send(part, part, mask_of(seq_bits[order])))
+        wait_all(small[-1:])
+        part = everyone_ref.at[item_place, aligned(seq_place, 2**order)]
+        small.append(copies.send(part, part, mask_of(seq_bits[order])))
+        if order == 1:
+            share(in_ref, own_in_ref.at[0])
     wait_all(small[-1:])
     embed = copies.move(everyone_ref.at[item_place, :, pl.ds(0, row_count)], embed_scr)
+
+    wait_all(heads)
+    embed.wait()
+    sum_scr[0] = lax.dot_general(
+        embed_scr[...].reshape(seq_size * row_count, -1),
+        block_scr[...].reshape(seq_size * row_count, columns),
+        (((0,), (0,)), ((), ())),
+        preferred_element_type=f32,
+    )
+    sums = copies.send(sum_scr.at[0], got_scr.at[0], mask_of(item_bits[0]))
+    block_out = copies.move(block_scr, block_ref)
     part = everyone_ref.at[item_place]
     small.append(copies.send(part, part, mask_of(item_bits[0])))
+    share(out_ref, own_out_ref)
     wait_all(dense[-1:])
 
     def dense_part(mask):
@@ -287,60 +303,65 @@
         part = dense_part(0)
         arrived[wave[0][1][1]] = copies.send(part, part, mask_of(wave[0][1]))
     near = [copies.send(dense_part(0), dense_part(0), mask_of(seq_bits[0]))]
-
-    wait_all(heads)
-    embed.wait()
-    sum_scr[0] = lax.dot_general(
-        embed_scr[...].reshape(seq_size * row_count, -1),
-        block_scr[...].reshape(seq_size * row_count, columns),
-        (((0,), (0,)), ((), ())),
-        preferred_element_type=f32,
-    )
-    block_out = copies.move(block_scr, block_ref)
+    wait_all(shares[:3])
+    outer = []
+    if len(seq_bits) == 3:
+        first = pl.ds(0, 2 * rows)
+        outer.append(
+            copies.send(own_in_ref.at[0, first], own_in_ref.at[1, first], mask_of(seq_bits[2]))
+        )
     for order, step in enumerate(item_bits):
-        one = copies.send(sum_scr.at[order], got_scr.at[order], mask_of(step))
+        sums.wait_recv()
+        sum_scr[order + 1] = sum_scr[order] + got_scr[order]
         if order + 1 < len(item_bits):
+            sums = copies.send(
+                sum_scr.at[order + 1], got_scr.at[order + 1], mask_of(item_bits[order + 1])
+            )
             wait_all(small[-1:])
             part = everyone_ref.at[aligned(item_place, 2 ** (order + 1))]
             small.append(copies.send(part, part, mask_of(item_bits[order + 1])))
-        one.wait_recv()
-        sum_scr[order + 1] = sum_scr[order] + got_scr[order]
+        if order < len(waves) and order + 1 < len(item_bits):
+            wave = waves[order]
+            for mask, step in wave:
+                arrived[mask ^ step[1]].wait_recv()
+                part = dense_part(mask ^ step[1])
+                for later in waves[order + 1 :]:
+                    arrived[mask ^ step[1] ^ later[0][1][1]] = copies.send(
+                        part, part, mask_of(later[0][1])
+                    )
+                near.append(copies.send(part, part, mask_of(seq_bits[0])))
     table_ref[...] = sum_scr[len(item_bits)]
 
-    for wave in waves:
-        for mask, step in wave:
-            if mask:
-                part = dense_part(mask)
-                arrived[mask ^ step[1]] = copies.send(part, part, mask_of(step))
-        for mask, step in wave:
-            arrived[mask ^ step[1]].wait_recv()
-            part = dense_part(mask ^ step[1])
-            near.append(copies.send(part, part, mask_of(seq_bits[0])))
+    for mask, step in waves[-1]:
+        arrived[mask ^ step[1]].wait_recv()
+        part = dense_part(mask ^ step[1])
+        near.append(copies.send(part, part, mask_of(seq_bits[0])))
     wait_all(near)
-    wait_all(shares)
+    wait_all(shares[3:])
+    wait_all(outer)
     wait_all(small[-1:])
     block_out.wait()
     copies.end()
 
 
-def first_call(item_bits, seq_bits, small, heads, dense, parts_in, parts_out):
+def first_call(item_bits, seq_bits, small, heads, head_bias, dense, parts_in, parts_out):
     items_size, seq_size = 2 ** len(item_bits), 2 ** len(seq_bits)
-    row_count = heads.shape[0]
+    row_count = heads.shape[0] + head_bias.shape[0]
     rows, width = dense.shape
     vocab = small.shape[1]
     columns = heads.shape[1] // seq_size
     any_space = pl.BlockSpec(memory_space=pl.ANY)
-    spare = 8 * (len(item_bits) + len(seq_bits)) + 2 * seq_size + 2 ** (len(item_bits) + 1)
+    spare = 8 * (len(item_bits) + len(seq_bits)) + 4 * seq_size + 2 ** (len(item_bits) + 2)
     return pl.pallas_call(
         functools.partial(first_kernel, item_bits, seq_bits, row_count),
-        in_specs=[any_space] * 5,
+        in_specs=[any_space] * 6,
         out_specs=[any_space, pl.BlockSpec(memory_space=pltpu.VMEM)] + [any_space] * 4,
         out_shape=[
             jax.ShapeDtypeStruct((items_size, seq_size) + small.shape, bf16),
             jax.ShapeDtypeStruct((vocab, columns), f32),
             jax.ShapeDtypeStruct((seq_size, row_count, columns), bf16),
             jax.ShapeDtypeStruct((items_size, seq_size // 2, 2, rows, width), bf16),
-            jax.ShapeDtypeStruct((4 * rows, parts_in.shape[3]), bf16),
+            jax.ShapeDtypeStruct((2, 4 * rows, parts_in.shape[3]), bf16),
             jax.ShapeDtypeStruct((4 * rows, parts_out.shape[3]), bf16),
         ],
         scratch_shapes=[
@@ -356,14 +377,16 @@
             collective_id=0, has_side_effects=True, vmem_limit_bytes=24 * 2**20
         ),
         name="first",
-    )(small, heads, dense, parts_in, parts_out)
+    )(small, heads, head_bias, dense, parts_in, parts_out)
 
 
 class Spread:
-    def __init__(self, copies, own, whole, outer_bits, item_bits):
-        self.copies, self.own, self.whole = copies, own, whole
+    def __init__(self, copies, own, whole, outer_bits, item_bits, given=None):
+        self.copies, self.own, self.whole, self.given = copies, own, whole, given
         self.outer_bits, self.item_bits = outer_bits, item_bits
-        self.half = own.shape[0] // 2
+        half = own.shape[0] // 2
+        self.halves = pl.ds(0, half), pl.ds(half, half)
+        self.last = []
 
     def part(self, masks):
         place = (self.copies.here[0] ^ masks[0]) * lax.axis_size("seq")
@@ -379,26 +402,42 @@
     def start(self):
         self.local = self.copies.move(self.own, self.part((0, 0)))
         self.first = [self.over((0, 0), step) for step in self.item_bits]
-        self.outer = self.over((0, 0), self.outer_bits[0])
-
-    def cross(self, masks, first):
+
+    def start_given(self):
+        masks = mask_of(self.outer_bits[0])
+        target = self.part(masks).at[self.halves[0]]
+        self.local_given = self.copies.move(self.given, target)
+        self.second = [
+            [self.copies.send(self.given, target, mask_of(step)) for step in self.item_bits],
+            [],
+        ]
+        self.outer = [None, self.over((0, 0), self.outer_bits[0], self.halves[1])]
+
+    def start_outer(self):
+        self.outer = [self.over((0, 0), self.outer_bits[0], rows) for rows in self.halves]
+        self.second = [[], []]
+
+    def cross_own(self):
         one, two = self.item_bits
-        first[0].wait_recv()
-        found = [self.over(moved(masks, *one), two, pl.ds(0, self.half))]
-        first[1].wait_recv()
-        found.append(self.over(moved(masks, *two), one, pl.ds(self.half, self.half)))
-        return found
-
-    def cross_own(self):
-        self.last = self.cross((0, 0), self.first)
-
-    def spread_outer(self):
-        self.outer.wait_recv()
+        self.first[0].wait_recv()
+        self.last.append(self.over(moved((0, 0), *one), two, self.halves[0]))
+        self.first[1].wait_recv()
+        self.last.append(self.over(moved((0, 0), *two), one, self.halves[1]))
+
+    def spread_outer(self, which):
+        self.outer[which].wait_recv()
         masks = mask_of(self.outer_bits[0])
-        self.second = [self.over(masks, step) for step in self.item_bits]
-
-    def cross_outer(self):
-        self.last += self.cross(mask_of(self.outer_bits[0]), self.second)
+        self.second[which] = [
+            self.over(masks, step, self.halves[which]) for step in self.item_bits
+        ]
+
+    def cross_outer(self, which):
+        masks = mask_of(self.outer_bits[0])
+        steps = self.item_bits if which == 0 else self.item_bits[::-1]
+        copies = self.second[which] if which == 0 else self.second[which][::-1]
+        copies[0].wait_recv()
+        self.last.append(self.over(moved(masks, *steps[0]), steps[1], self.halves[which]))
+        self.last.append(copies[1])
 
     def plain(self):
         self.local = self.copies.move(self.own, self.part((0, 0)))
@@ -406,11 +445,12 @@
         for step in self.outer_bits + self.item_bits:
             wait_all([self.over(masks, step) for masks in known])
             known = known + [moved(masks, *step) for masks in known]
-        self.last = []
 
     def end(self):
         wait_all(self.last)
         self.local.wait()
+        if self.given is not None:
+            self.local_given.wait()
 
 
 def attend_unit(block, visible, onehot_ref, table_ref, cosine_ref, sine_ref, context_ref, lse_ref):
@@ -465,14 +505,15 @@
     greet(partners(seq_size, item_bits))
     copies = Copies(send_sems, recv_sems, local_sems)
     dense_copy = copies.move(dense_ref, dense_scr)
+    stepwise = len(outer_bits) == 1 and len(item_bits) == 2
+    given = own_in_ref.at[1, pl.ds(0, own_in_ref.shape[1] // 2)] if stepwise else None
     spreads = [
-        Spread(copies, own_in_ref, in_ref, outer_bits, item_bits),
+        Spread(copies, own_in_ref.at[0], in_ref, outer_bits, item_bits, given),
         Spread(copies, own_out_ref, out_ref, outer_bits, item_bits),
     ]
-    stepwise = len(outer_bits) == 1 and len(item_bits) == 2
     if stepwise:
-        for one in spreads:
-            one.start()
+        spreads[0].start()
+        spreads[0].start_given()
     arrivals, local = [], []
     for item in range(items_here):
 
@@ -500,12 +541,17 @@
                 arrivals.append(copies.send(source, target, (0, mask)))
             else:
                 local.append(copies.move(source, target))
+    if stepwise:
+        spreads[0].cross_own()
+        spreads[0].cross_outer(0)
+        spreads[1].start()
+        spreads[0].spread_outer(1)
     wait_all(arrivals)
     for copy in local:
         copy.wait()
+
     if stepwise:
-        for one in spreads:
-            one.cross_own()
+        spreads[1].start_outer()
 
     dense_copy.wait()
     rows_all = items_here * span
@@ -544,15 +590,19 @@
         near_copies.append(copies.send(part, shared_ref.at[item, 3], mask_of(near)))
 
     if stepwise:
-        spreads[0].spread_outer()
+        spreads[1].cross_own()
+        spreads[0].cross_outer(1)
     pass_on(0)
     if stepwise:
-        spreads[1].spread_outer()
-    for item in range(1, items_here):
+        spreads[1].spread_outer(0)
+    pass_on(1)
+    if stepwise:
+        spreads[1].spread_outer(1)
+        spreads[1].cross_outer(0)
+    for item in range(2, items_here):
         pass_on(item)
     if stepwise:
-        for one in spreads:
-            one.cross_outer()
+        spreads[1].cross_outer(1)
     else:
         for one in spreads:
             one.plain()
@@ -596,7 +646,7 @@
         out_shape=[
             jax.ShapeDtypeStruct((items_here, span, width), bf16),
             jax.ShapeDtypeStruct((items_here, heads_here, 1, length), f32),
-            jax.ShapeDtypeStruct((groups,) + own_in.shape, bf16),
+            jax.ShapeDtypeStruct((groups,) + own_in.shape[1:], bf16),
             jax.ShapeDtypeStruct((groups,) + own_out.shape, bf16),
             jax.ShapeDtypeStruct((items_here, 4, span, width), bf16),
             jax.ShapeDtypeStruct((items_here * span, width), f32),
@@ -817,7 +867,7 @@
 
     in_sums = reducers(in_ref, in_got)
     out_sums = reducers(out_ref, out_got)
-    dense_steps = item_bits[::-1] + seq_bits[:0:-1]
+    dense_steps = (item_bits[::-1] + seq_bits[:0:-1])[1:]
     dense_sum = Reduce(
         copies,
         dense_ref,
@@ -828,11 +878,22 @@
         stage_scr,
         stage_sems,
     )
-    for one in in_sums:
+    for one in in_sums + out_sums:
         one.start()
     sums_scr[...] = jnp.zeros_like(sums_scr)
     tile = 256
     flying = {}
+    sums_copy = None
+
+    def next_sum(order):
+        nonlocal sums_copy
+        sums_copy.wait_recv()
+        sums_scr[order + 1] = sums_scr[order] + sums_got[order]
+        if order + 1 < len(item_bits):
+            sums_copy = copies.send(
+                sums_scr.at[order + 1], sums_got.at[order + 1], mask_of(item_bits[order + 1])
+            )
+
     bias_scr[0] = bias_ref[...]
     bias_steps = seq_bits + item_bits
     bias_copies = [copies.send(bias_scr.at[0], bias_got.at[0], mask_of(bias_steps[0]))]
@@ -917,20 +978,25 @@
             flying[stage] = copy, kept_scr.at[kept_slot]
             flying["first", stage] = copy
             flying["later", stage] = []
-        if stage == 0:
-            for one in out_sums:
-                one.start()
+        if stage == 1:
+            dense_sum.start()
+        if stage == items_here - 1:
+            sums_copy = copies.send(sums_scr.at[0], sums_got.at[0], mask_of(item_bits[0]))
         if stage == items_here:
             for one in in_sums:
                 one.advance()
-            dense_sum.start()
-            sums_copy = copies.send(sums_scr.at[0], sums_got.at[0], mask_of(item_bits[0]))
         if stage == items_here + 1:
+            next_sum(0)
+            for one in in_sums:
+                one.advance()
             for one in out_sums:
                 one.advance()
         if stage == items_here + 2:
-            for one in in_sums:
+            for order in range(1, len(item_bits)):
+                next_sum(order)
+            for one in out_sums:
                 one.advance()
+
         bias_done = len(bias_copies)
         if bias_done <= len(bias_steps):
             bias_copies[-1].wait_recv()
@@ -947,13 +1013,6 @@
                 bias_copies.append(None)
                 bias_sum_ref[...] = bias_scr[bias_done]
 
-    for order, step in enumerate(item_bits):
-        sums_copy.wait_recv()
-        sums_scr[order + 1] = sums_scr[order] + sums_got[order]
-        if order + 1 < len(item_bits):
-            sums_copy = copies.send(
-                sums_scr.at[order + 1], sums_got.at[order + 1], mask_of(item_bits[order + 1])
-            )
     sums_all_ref[seq_place] = sums_scr[len(item_bits)].astype(bf16)
     known = [0]
     arrivals = []
@@ -964,10 +1023,7 @@
             part = sums_all_ref.at[seq_place ^ mask]
             arrivals.append(copies.send(part, part, (0, bit)))
         known = known + [mask ^ bit for mask in known]
-        for one in out_sums:
-            if one.order < 2:
-                one.advance()
-        if dense_sum.order == 0:
+        if dense_sum.order < len(dense_steps):
             dense_sum.advance()
 
     while in_sums[0].order < len(dims):
@@ -1043,7 +1099,7 @@
     ways = 2 if len(item_bits) == 2 else 1
     group_rows = grad_in.shape[-2]
     rows = group_rows // 4
-    dense_depth = len(item_bits) + len(seq_bits) - 1
+    dense_depth = len(item_bits) + len(seq_bits) - 2
     spread = (2,) * (len(seq_bits) - 1) + (span, width)
     all_bits = len(item_bits) + len(seq_bits)
     spare = 8 * items_here + 8 * levels + 16 * all_bits
@@ -1104,6 +1160,7 @@
 
 
 def ff_kernel(
+    item_bits,
     shared_ref,
     normed_ref,
     inverse_ref,
@@ -1112,6 +1169,7 @@
     out_ref,
     vector_ref,
     bias_ref,
+    block_ref,
     product_ref,
     saved_ref,
     grad_shared_ref,
@@ -1120,6 +1178,7 @@
     resid_ref,
     sums_ref,
     in_sum_ref,
+    slices_ref,
     rows_scr,
     product_scr,
     save_scr,
@@ -1141,8 +1200,21 @@
     tiles = product_scr.shape[-1] // 128
     tile = 256
     near, far = ("seq", 1), ("seq", 2)
-    greet([mask_of(near), mask_of(far)])
-    copies = Copies(send_sems, recv_sems, None)
+    greet([mask_of(near), mask_of(far)] + [mask_of(step) for step in item_bits])
+    copies = Copies(send_sems, recv_sems, keep_sems)
+    item_place = copies.here[0]
+    slices = copies.move(block_ref, slices_ref.at[item_place])
+    slices.wait()
+    spread = []
+
+    def spread_block():
+        order = len(spread)
+        if order < len(item_bits):
+            wait_all(spread[-1:])
+            part = slices_ref.at[aligned(item_place, 2**order)]
+            spread.append(copies.send(part, part, mask_of(item_bits[order])))
+
+    spread_block()
     keeps, loads = {}, {}
     state = {}
     gain_one, shift_one, b_down, gain_two, shift_two = range(5)
@@ -1159,7 +1231,7 @@
         loads.pop(name).wait()
 
     def keep(name, slot, source, target):
-        copy = pltpu.make_async_copy(source, target, keep_sems.at[slot])
+        copy = pltpu.make_async_copy(source, target, keep_sems.at[1 + slot])
         copy.start()
         keeps[name] = copy
 
@@ -1391,6 +1463,7 @@
         if chunk == 0:
             load_grads(0)
         backward_gate(chunk)
+        spread_block()
         if waiting and waiting[0][0] == "norm":
             second_norm(waiting.pop(0)[1])
             load_normed(0)
@@ -1409,12 +1482,15 @@
     sum_near(("back", last), last)
     first_norm(last - 1)
     first_norm(last)
+    wait_all(spread[-1:])
     for name in list(keeps):
         keep_done(name)
     copies.end()
 
 
-def ff_call(shared, normed, inverse, cotangent, w_in, w_out, vectors, in_bias):
+def ff_call(
+    item_bits, shared, normed, inverse, cotangent, w_in, w_out, vectors, in_bias, block
+):
     chunks, blocks, span, width = shared.shape
     group_rows = blocks * span
     ff_part = w_out.shape[1]
@@ -1422,9 +1498,9 @@
     near_space = pl.BlockSpec(memory_space=pltpu.VMEM)
     spare = 8 * chunks
     return pl.pallas_call(
-        ff_kernel,
-        in_specs=[any_space, any_space] + [near_space] * 6,
-        out_specs=[any_space] * 4 + [near_space, any_space, near_space, near_space],
+        functools.partial(ff_kernel, item_bits),
+        in_specs=[any_space, any_space] + [near_space] * 6 + [any_space],
+        out_specs=[any_space] * 4 + [near_space, any_space, near_space, near_space, any_space],
         out_shape=[
             jax.ShapeDtypeStruct((chunks, group_rows, ff_part), bf16),
             jax.ShapeDtypeStruct((chunks, 2, group_rows, ff_part), bf16),
@@ -1434,6 +1510,7 @@
             jax.ShapeDtypeStruct((chunks, span, width), f32),
             jax.ShapeDtypeStruct((8, width), f32),
             jax.ShapeDtypeStruct((1, 2 * ff_part), f32),
+            jax.ShapeDtypeStruct((2 ** len(item_bits),) + block.shape, bf16),
         ],
         scratch_shapes=[
             pltpu.VMEM((2, blocks, span, width), bf16),
@@ -1450,13 +1527,13 @@
             pltpu.SemaphoreType.DMA((spare,)),
             pltpu.SemaphoreType.DMA((spare,)),
             pltpu.SemaphoreType.DMA((6,)),
-            pltpu.SemaphoreType.DMA((7 + chunks,)),
+            pltpu.SemaphoreType.DMA((8 + chunks,)),
         ],
         compiler_params=pltpu.CompilerParams(
             collective_id=3, has_side_effects=True, vmem_limit_bytes=60 * 2**20
         ),
         name="feed_forward",
-    )(shared, normed, inverse, cotangent, w_in, w_out, vectors, in_bias)
+    )(shared, normed, inverse, cotangent, w_in, w_out, vectors, in_bias, block)
 
 
 def on_device(
@@ -1549,7 +1626,8 @@
         item_bits,
         seq_bits,
         flat,
-        jnp.concatenate([heads_weight, bias_row], axis=0),
+        heads_weight,
+        bias_row,
         dense_weight,
         parts_in,
         parts_out,
@@ -1599,7 +1677,8 @@
         own_in,
         own_out,
     )
-    product, _, grad_shared, grad_in, layer_out, grad_resid, sums, in_sum = ff_call(
+    product, _, grad_shared, grad_in, layer_out, grad_resid, sums, in_sum, w_slice = ff_call(
+        item_bits,
         shared,
         normed,
         inverse,
@@ -1608,6 +1687,7 @@
         w_out.reshape(width, ff_part),
         vectors,
         in_bias,
+        w_block,
     )
     rows_all = items_here * span
     group_all = members * rows_all
@@ -1626,13 +1706,7 @@
     ).reshape(items_here, length, heads_here * HEAD)
 
     vector_sums = sums[:6].T
-    token_sum = lax.dot_general(
-        grad_resid,
-        own_onehot.astype(f32),
-        (((0,), (0,)), ((), ())),
-        precision=lax.Precision.HIGHEST,
-        preferred_element_type=f32,
-    )
+    token_sum = contract_rows(grad_branch, own_onehot)
     grad_dense = contract_rows(context, grad_branch)
     by_rows = jnp.concatenate(
         [grad_dense, token_sum, jnp.pad(vector_sums, ((0, 0), (0, 122)))], axis=1
@@ -1640,6 +1714,7 @@
     row_dims = item_bits[::-1] + seq_bits[::-1]
     by_rows = by_rows.reshape((2,) * len(row_dims) + (rows_here, -1))
     by_rows = halve(lines, by_rows, len(row_dims) - 1, *seq_bits[0])
+    by_rows = halve(lines, by_rows, 0, *row_dims[0])
     grad_out_weight = contract_rows(
         grad_shared.reshape(group_all, width), product.reshape(group_all, ff_part)
     )
@@ -1651,7 +1726,7 @@
     in_all = lax.dynamic_update_slice(
         jnp.zeros((2, ff_all), f32), in_sum, (0, member * ff_part)
     ).reshape(-1, 128)
-    w_slice = gather_merge(lines, w_block[None], item_bits).reshape(width, packed_width)
+    w_slice = w_slice.reshape(width, packed_width)
     spread, token_all, in_part, out_part, by_rows, in_all = third_call(
         item_bits,
         seq_bits,

time: 1120 us -> 1070 us (0.955)
  Pallas kernels: 900 us -> 835 us
  waiting for transfers between devices: 15.4 us -> 30.3 us
    pallas_call x1, Pallas kernels: 244 us -> 184 us  [second_call(): pl.pallas_call(functools.partial(second_kernel, item_bits, seq_bits), in_...]
    pallas_call x1, Pallas kernels: 146 us -> 104 us  [first_call(): pl.pallas_call(functools.partial(first_kernel, item_bits, seq_bits, row_c...]
    pallas_call x1, Pallas kernels: 182 us -> 204 us  [ff_call(): pl.pallas_call(functools.partial(ff_kernel, item_bits), in_specs=[any_spa...]
    pallas_call x1, Pallas kernels: 327 us -> 343 us  [third_call(): pl.pallas_call(functools.partial(third_kernel, item_bits, seq_bits), in_s...]
    ppermute x3 -> x2, waiting for transfers between devices: 15.4 us -> 30.3 us  [swap(): got = lax.ppermute(part, axis, [(j, j ^ bit) for j in range(size)])]
    dot_general x3 -> x4, matrix products: 59.5 us -> 60.7 us  [contract_rows(): lax.dot_general(left, right, (((0,), (0,)), ((), ())), preferred_element_...]
  transfers between devices with their start and end apart: 4 -> 3, of which waited for: 1 -> 1; matrix products, arithmetic and copies ran while one was open for 6% -> 7% of each run, Pallas kernels for 0% -> 0%
where the time goes in v4:
time: 1070 us; the launch traced here: 1060 us
  Pallas kernels  835 us (78%)
  local copies, waits for them, and re-layouts  81.2 us (8%)
  matrix products  71.9 us (7%)
  other arithmetic  35.6 us (3%)
  waiting for transfers between devices  30.3 us (3%)
    pallas_call x1, Pallas kernels, third_call(): pl.pallas_call(functools.partial(third_kernel, item_bits, seq_bits), in_s...  343 us
    pallas_call x1, Pallas kernels, ff_call(): pl.pallas_call(functools.partial(ff_kernel, item_bits), in_specs=[any_spa...  204 us
    pallas_call x1, Pallas kernels, second_call(): pl.pallas_call(functools.partial(second_kernel, item_bits, seq_bits), in_...  184 us
    pallas_call x1, Pallas kernels, first_call(): pl.pallas_call(functools.partial(first_kernel, item_bits, seq_bits, row_c...  104 us
    dot_general x4, matrix products, contract_rows(): lax.dot_general(left, right, (((0,), (0,)), ((), ())), preferred_element_...  60.7 us
    ppermute x2, waiting for transfers between devices, swap(): got = lax.ppermute(part, axis, [(j, j ^ bit) for j in range(size)])  30.3 us
  transfers between devices with their start and end apart: 3, of which 1 were waited for; matrix products, arithmetic and copies ran while one was open for 7% of the time, Pallas kernels for 0%

profile of v4, /device:TPU:0, one launch (start us, length us, event | category | flops | bytes accessed | tf_op | source)
XLA Modules:
  0.0 1062.7 jit_solution(8552289014146934097)
XLA Ops:
  2.0 5.5 concatenate.32
  12.0 3.3 copy.82
  15.4 4.1 reshape.275.in_ref
  24.8 104.2 %first.1 = (bf16[4,8,96,128]{3,2,1,0:T(8,128)(2,1)S(1)}, f32[128,768]{1,0:T(8,128)S(1)}, bf16[8,80,768]{2,1,0:T(8,128)(2,1)S(1)}, bf16[4,4,2,64,2048]{4,3,2,1,0:...) custom-call(bf16[96,128]{1,0:T(8,128)(2,1)S(1)} %copy-done.7, ...), custom_call_target="tpu_custom_call" | custom-call | tf_op jit(solution)/shard_map/first/pallas_call | solution.py:355
  129.1 3.2 copy-done
  150.3 183.6 %second.1 = (bf16[4,128,2048]{2,1,0:T(8,128)(2,1)}, f32[4,2,1,1024]{3,2,1,0:T(1,128)}, bf16[8,256,2816]{2,1,0:T(8,128)(2,1)}, bf16[8,256,1408]{2,1,0:T(8,128)(2,...) custom-call(s32[4]{0:T(128)} %compare_select_fusion.1.visible_ref, ...), custom_call_target="tpu_custom_call" | custom-call | tf_op jit(solution)/shard_map/second/pallas_call | solution.py:642
  333.9 204.5 %feed_forward.1 = (bf16[4,512,1408]{2,1,0:T(8,128)(2,1)}, bf16[4,2,512,1408]{3,2,1,0:T(8,128)(2,1)}, bf16[4,4,128,2048]{3,2,1,0:T(8,128)(2,1)}, bf16[4,512,2816]...) custom-call(bf16[4,4,128,2048]{3,2,1,0:T(8,128)(2,1)} %get-tuple-ele, ...), custom_call_target="tpu_custom_call" | custom-call | tf_op jit(solution)/shard_map/feed_forward/pallas_call | solution.py:1500
  541.2 6.7 bitcast_convert_fusion
  550.5 3.2 fusion.5
  555.9 4.6 pad_maximum_fusion
  567.4 8.3 convolution_convert_fusion.2
  578.1 4.5 all-to-all-start
  583.4 4.7 copy.105
  588.1 31.5 %convolution_convert_fusion = bf16[2048,2816]{1,0:T(8,128)(2,1)} fusion(bf16[2048,2048]{1,0:T(8,128)(2,1)} %bitcast.146, bf16[2048,2816]{1,0:T(8,128)(2,1)} %bitcast.172), kind=kOutput, calls=%fused_computation.1 | convolution fusion | flops 23628087296 | bytes 31457280 | tf_op jit(solution)/shard_map/dot_general | solution.py:68
  619.7 3.7 fusion
  628.1 19.3 %convolution_convert_fusion.1 = bf16[2048,1408]{1,0:T(8,128)(2,1)} fusion(bf16[2048,2048]{1,0:T(8,128)(2,1)} %bitcast.173, bf16[2048,1408]{1,0:T(8,128)(2,1)} %bitcast.174), kind=kOutput, calls=%fused_computation.5 | convolution fusion | flops 11814043648 | bytes 19922944 | tf_op jit(solution)/shard_map/dot_general | solution.py:68
  647.4 3.1 copy.88
  650.5 30.3 %collective-permute-done.1 = bf16[2,2,2,64,2304]{4,3,2,1,0:T(8,128)(2,1)S(1)} collective-permute-done((bf16[2,2,2,64,2304]{4,3,2,1,0:T(8,128)(2,1)}, bf16[2,2,2,64,2304]{4,3,2,1,0:T(8,128)(2,1)S(1)}, u32[]{:S(2)}, u32[]{:S(2)}) %collective-permute-start.1) | collective-permute-done | bytes 2359328 | tf_op jit(solution)/shard_map/ppermute | solution.py:34
  680.8 3.6 fusion.1.dense_ref
  684.4 342.6 %third.1 = (bf16[4,128,2048]{2,1,0:T(8,128)(2,1)}, bf16[8,2,128,384]{3,2,1,0:T(8,128)(2,1)}, bf16[4,64,2816]{2,1,0:T(8,128)(2,1)}, bf16[4,64,1408]{2,1,0:T(8,128...) custom-call(s32[4]{0:T(128)} %compare_select_fusion.1.visible_ref, bf16[4,1024,128]{2,1,0:T(8,128)(2,1)} %fusion.4.onehot_ref, ...), custom_call_target="tpu_custom_call" | custom-call | tf_op jit(solution)/shard_map/third/pallas_call | solution.py:1107
  1033.0 3.3 reshape.299
  1036.3 8.6 slice_reduce_fusion.1
  1048.8 5.2 multiply_add_fusion
  1059.3 3.2 copy.138
  (143 shorter events, 66.3 us)
Async XLA Ops:
  15.4 7.8 copy-start.1
  129.1 3.2 copy-start
  137.1 7.6 copy-start.18
  137.1 7.8 copy-start.5
  138.2 7.6 copy-start.14
  138.2 8.4 copy-start.23
  138.2 8.4 copy-start.24
  538.4 2.9 copy-start.22
  548.0 5.7 copy-start.19
  560.5 5.1 copy-start.8
  565.5 54.2 %collective-permute-start = (bf16[2,2,2,2,64,2304]{5,4,3,2,1,0:T(8,128)(2,1)}, bf16[2,2,2,2,64,2304]{5,4,3,2,1,0:T(8,128)(2,1)}, u32[]{:S(2)}, u32[]{:S(2)}) collective-permute-start(bf16[2,2,2,2,64,2304]{5,4,3,2,1,0:T(8,128)(2,1)} %dynamic-slice_bitcast_fusion), channel_id=1, source_target_pairs={{0,1},{1,0},{2,3},{3,2},{4,5},{5,4},{6,7},{7,6},{8,9},{9,8},{10,11... | collective-permute-start | bytes 14155784 | tf_op jit(solution)/shard_map/ppermute | solution.py:34
  578.1 4.5 copy-start.20
  578.1 69.3 %all-to-all-start = ((bf16[4,8,128,256]{3,2,0,1:T(8,128)(2,1)}), bf16[4,8,128,256]{3,2,0,1:T(8,128)(2,1)}, u32[]{:S(2)}, u32[]{:S(2)}) async-start(bf16[4,8,128,256]{3,2,0,1:T(8,128)(2,1)} %bitcast.125), calls=%async_computation | async-start | bytes 4194304 | tf_op jit(solution)/shard_map/all_to_all | solution.py:1698
  583.4 36.2 %slice-start = ((s8[9437184]{0:T(1024)(128)(4,1)}), s8[1048576]{0:T(1024)(128)(4,1)S(1)}, s32[]{:S(2)}) async-start(s8[9437184]{0:T(1024)(128)(4,1)} %bitcast.134), calls=%async_computation.1 | async-start | bytes 2097152
  588.1 31.5 %slice-start.1 = ((s8[9437184]{0:T(1024)(128)(4,1)}), s8[4194304]{0:T(1024)(128)(4,1)S(1)}, s32[]{:S(2)}) async-start(s8[9437184]{0:T(1024)(128)(4,1)} %bitcast.134), calls=%async_computation.2 | async-start | bytes 8388608
  588.1 31.5 %slice-start.2 = ((s8[9437184]{0:T(1024)(128)(4,1)}), s8[4194304]{0:T(1024)(128)(4,1)S(1)}, s32[]{:S(2)}) async-start(s8[9437184]{0:T(1024)(128)(4,1)} %bitcast.134), calls=%async_computation.3 | async-start | bytes 8388608
  623.4 2.2 copy-start.9
  627.1 53.7 %collective-permute-start.1 = (bf16[2,2,2,64,2304]{4,3,2,1,0:T(8,128)(2,1)}, bf16[2,2,2,64,2304]{4,3,2,1,0:T(8,128)(2,1)S(1)}, u32[]{:S(2)}, u32[]{:S(2)}) collective-permute-start(bf16[2,2,2,64,2304]{4,3,2,1,0:T(8,128)(2,1)} %dynamic-slice_bitcast_fusion.1), channel_id=1, source_target_pairs={{0,16},{8,24},{16,0},{24,8},{1,17},{9,25},{17,1},{25,9},{2,18},{10... | collective-permute-start | bytes 7077896 | tf_op jit(solution)/shard_map/ppermute | solution.py:34
  1027.0 2.0 copy-start.11
  1027.0 2.0 copy-start.16
  1029.0 3.7 copy-start.10
  1047.2 1.6 copy-start.12
  1048.8 5.2 copy-start.15
  1054.0 2.0 copy-start.17
  (7 other events, 7.8 us)

commit v5 on v4

--- a/solution.py
+++ b/solution.py
@@ -51,13 +51,6 @@
 
 def pick(whole, place, dim):
     return lax.dynamic_index_in_dim(whole, place, dim, keepdims=False)
-
-
-def halve(lines, whole, dim, axis, bit):
-    place = my_bit(axis, bit)
-    mine = pick(whole, place, dim)
-    got = lines.swap(pick(whole, 1 - place, dim), axis, bit)
-    return (mine.astype(f32) + got.astype(f32)).astype(whole.dtype)
 
 
 def moved(masks, axis, bit):
@@ -867,7 +860,7 @@
 
     in_sums = reducers(in_ref, in_got)
     out_sums = reducers(out_ref, out_got)
-    dense_steps = (item_bits[::-1] + seq_bits[:0:-1])[1:]
+    dense_steps = item_bits[::-1] + seq_bits[:0:-1]
     dense_sum = Reduce(
         copies,
         dense_ref,
@@ -1099,7 +1092,7 @@
     ways = 2 if len(item_bits) == 2 else 1
     group_rows = grad_in.shape[-2]
     rows = group_rows // 4
-    dense_depth = len(item_bits) + len(seq_bits) - 2
+    dense_depth = len(item_bits) + len(seq_bits) - 1
     spread = (2,) * (len(seq_bits) - 1) + (span, width)
     all_bits = len(item_bits) + len(seq_bits)
     spare = 8 * items_here + 8 * levels + 16 * all_bits
@@ -1159,6 +1152,512 @@
     )
 
 
+def merged_kernel(
+    item_bits,
+    seq_bits,
+    visible_ref,
+    onehot_ref,
+    table_ref,
+    cosine_ref,
+    sine_ref,
+    lse_ref,
+    slice_ref,
+    grad_ref,
+    shared_ref,
+    grad_in_ref,
+    grad_shared_ref,
+    product_ref,
+    dense_ref,
+    bias_ref,
+    spread_ref,
+    sums_all_ref,
+    parts_ref,
+    dense_part_ref,
+    bias_sum_ref,
+    land_one_ref,
+    land_two_ref,
+    land_three_ref,
+    mixed_scr,
+    other_scr,
+    kept_scr,
+    step_scrs,
+    sums_scr,
+    sums_got,
+    bias_scr,
+    bias_got,
+    dense_got,
+    rhs_scr,
+    lhs_scr,
+    turned_scr,
+    slot_scr,
+    sum_scr,
+    stage_scr,
+    dense_scr,
+    grad_scr,
+    stage_sems,
+    load_sems,
+    send_sems,
+    recv_sems,
+    local_sems,
+):
+    seq_size = 2 ** len(seq_bits)
+    items_here, length, features = grad_scr.shape
+    span = length // seq_size
+    heads_here = features // HEAD
+    seq_place = lax.axis_index("seq")
+    member = seq_place % 4
+    outer_bits = seq_bits[2:]
+    width = slice_ref.shape[1]
+    greet(partners(seq_size, item_bits))
+    copies = Copies(send_sems, recv_sems, local_sems)
+
+    one, two = item_bits
+    high = outer_bits[0]
+    ways = [[two, one, high], [one, two, high]]
+    blocks = [(grad_shared_ref, product_ref, 0)]
+    ff_part = product_ref.shape[1]
+    blocks += [(shared_ref, grad_in_ref, 0), (shared_ref, grad_in_ref, ff_part)]
+    group_rows = lhs_scr.shape[2]
+    half_rows = group_rows // 2
+    pairs = [(two, one), (two,), (one,), ()]
+
+    def masks_of(steps):
+        masks = (0, 0)
+        for step in steps:
+            masks = moved(masks, *step)
+        return masks
+
+    def load_rhs(block):
+        _, rhs, first = blocks[block]
+        return pltpu.make_async_copy(
+            rhs.at[:, pl.ds(first, ff_part)], rhs_scr, load_sems.at[0]
+        )
+
+    def load_lhs(block, pair, which):
+        masks = masks_of(pairs[pair] + ((high,) if which == 0 else ()))
+        group = ((copies.here[0] ^ masks[0]) * seq_size + (copies.here[1] ^ masks[1])) // 4
+        columns = pl.ds(pl.multiple_of(group * group_rows, 128), group_rows)
+        return pltpu.make_async_copy(
+            blocks[block][0].at[:, columns], lhs_scr.at[which], load_sems.at[1 + which]
+        )
+
+    landed, slots, sends = {}, {}, {}
+
+    def products(block):
+        load_rhs(block).wait()
+        for pair, steps in enumerate(pairs):
+            for which in range(2):
+                load_lhs(block, pair, which).wait()
+                rows = pl.ds(which * group_rows, group_rows)
+                turned_scr[rows, :] = lhs_scr[which].T
+            follow = (block, pair + 1) if pair + 1 < len(pairs) else (block + 1, 0)
+            if follow[0] < len(blocks):
+                for which in range(2):
+                    load_lhs(*follow, which).start()
+            targets = []
+            for which in range(2):
+                for way in range(2):
+                    away, other = ways[way][:2]
+                    place = 2 * (other in steps) + 1 - which
+                    if away in steps:
+                        if (way, place) in slots:
+                            copies.sent_now(slots.pop((way, place)))
+                        targets.append(slot_scr.at[way, place])
+                    else:
+                        targets.append(sum_scr.at[block, way, place])
+
+            def multiply(columns):
+                total = dot(turned_scr[...], rhs_scr[:, columns]).astype(bf16)
+                for order, target in enumerate(targets):
+                    target[:, columns] = total[order * half_rows : (order + 1) * half_rows]
+
+            @pl.loop(0, ff_part // 256)
+            def _(order):
+                multiply(pl.ds(pl.multiple_of(order * 256, 256), 256))
+
+            if ff_part % 256:
+                multiply(pl.ds(ff_part // 256 * 256, ff_part % 256))
+            for which in range(2):
+                for way in range(2):
+                    away, other = ways[way][:2]
+                    place = 2 * (other in steps) + 1 - which
+                    if away in steps:
+                        copy = copies.send(
+                            slot_scr.at[way, place],
+                            land_one_ref.at[block, way, place],
+                            mask_of(away),
+                        )
+                        slots[way, place] = copy
+                        landed[1, block, way, place] = copy
+        if block + 1 < len(blocks):
+            load_rhs(block + 1).start()
+
+    lands = {1: land_one_ref, 2: land_two_ref, 3: land_three_ref}
+
+    def absorb(level, block):
+        count = 2 ** (3 - level)
+        pending = []
+
+        def finish():
+            load, way, place, slot = pending.pop(0)
+            load.wait()
+            add_into(sum_scr.at[block, way, place], stage_scr.at[slot])
+            if level < 3 and place >= count // 2:
+                left = place - count // 2
+                landed[level + 1, block, way, left] = copies.send(
+                    sum_scr.at[block, way, place],
+                    lands[level + 1].at[block, way, left],
+                    mask_of(ways[way][level]),
+                )
+
+        order = 0
+        for place in range(count - 1, -1, -1):
+            for way in range(2):
+                landed[level, block, way, place].wait_recv()
+                slot = order % 2
+                load = pltpu.make_async_copy(
+                    lands[level].at[block, way, place], stage_scr.at[slot], stage_sems.at[slot]
+                )
+                load.start()
+                if pending:
+                    finish()
+                pending.append((load, way, place, slot))
+                order += 1
+        finish()
+
+    shares, local = [], []
+
+    def to_members(block):
+        rows = parts_ref.shape[2]
+        for mask in range(4):
+            other = member ^ mask
+            source = sum_scr.at[
+                block, other // 2, 0, pl.ds(pl.multiple_of(other % 2 * rows, 16), rows)
+            ]
+            if mask:
+                shares.append(copies.send(source, parts_ref.at[block, member], (0, mask)))
+            else:
+                local.append(copies.move(source, parts_ref.at[block, member]))
+
+    grads = {}
+
+    def send_grads(item):
+        target = grad_scr.at[item, pl.ds(pl.multiple_of(seq_place * span, span), span)]
+        arriving = []
+        for mask in range(seq_size):
+            columns = pl.ds(pl.multiple_of((seq_place ^ mask) * features, HEAD), features)
+            source = grad_ref.at[item, :, columns]
+            if mask:
+                arriving.append(copies.send(source, target, (0, mask)))
+            else:
+                own = copies.move(source, target)
+        grads[item] = arriving, own
+
+    send_grads(0)
+    load_rhs(0).start()
+    for which in range(2):
+        load_lhs(0, 0, which).start()
+    dense_steps = item_bits[::-1] + seq_bits[:0:-1]
+    dense_sum = Reduce(
+        copies,
+        dense_ref,
+        pl.ds(0, dense_ref.shape[-2]),
+        dense_steps,
+        dense_steps,
+        list(dense_got),
+        dense_scr,
+        stage_sems,
+    )
+    sums_scr[...] = jnp.zeros_like(sums_scr)
+    tile = 256
+    flying = {}
+    sums_copy = None
+
+    def next_sum(order):
+        nonlocal sums_copy
+        sums_copy.wait_recv()
+        sums_scr[order + 1] = sums_scr[order] + sums_got[order]
+        if order + 1 < len(item_bits):
+            sums_copy = copies.send(
+                sums_scr.at[order + 1], sums_got.at[order + 1], mask_of(item_bits[order + 1])
+            )
+
+    known, arrivals = [0], []
+
+    def spread_sums():
+        nonlocal known, arrivals
+        wait_all(arrivals)
+        arrivals = []
+        bit = seq_size // 2 // len(known)
+        for mask in known:
+            part = sums_all_ref.at[seq_place ^ mask]
+            arrivals.append(copies.send(part, part, (0, bit)))
+        known = known + [mask ^ bit for mask in known]
+
+    bias_scr[0] = bias_ref[...]
+    bias_steps = seq_bits + item_bits
+    bias_copies = [copies.send(bias_scr.at[0], bias_got.at[0], mask_of(bias_steps[0]))]
+
+    def attention(item):
+        arriving, own = grads[item]
+        wait_all(arriving)
+        own.wait()
+
+        @pl.loop(0, heads_here)
+        def _(head):
+            place = pl.ds(pl.multiple_of(head * HEAD, HEAD), HEAD)
+            packed = pl.ds(pl.multiple_of(head * 3 * HEAD, HEAD), 3 * HEAD)
+            attend_back_unit(
+                min(256, length),
+                visible_ref[item],
+                onehot_ref.at[item],
+                table_ref.at[head],
+                cosine_ref,
+                sine_ref,
+                lse_ref.at[item, head],
+                grad_scr.at[item, :, place],
+                mixed_scr.at[:, :, :, packed],
+                sums_scr.at[0, head],
+            )
+
+    def step_on(item, order):
+        copy, kept = flying[item]
+        copy.wait_recv()
+        got = step_scrs[order].at[item % step_scrs[order].shape[0]]
+        full = (slice(None),) * (len(kept.shape) - 3)
+        if order:
+            kept = kept.at[full + (my_bit(*seq_bits[order]),)]
+            full = full[1:]
+        if order + 1 < len(seq_bits):
+            add_into(kept, got)
+            step = seq_bits[order + 1]
+            target = step_scrs[order + 1]
+            copy = copies.send(
+                kept.at[full + (1 - my_bit(*step),)],
+                target.at[item % target.shape[0]],
+                mask_of(step),
+            )
+            flying[item] = copy, kept
+            flying["later", item].append(copy)
+        else:
+            add_into(kept, got)
+            flying["out", item] = copies.move(kept, spread_ref.at[item])
+
+    def partial(item):
+        core = my_bit(*seq_bits[0])
+        slot = item % 2
+        if item >= 1:
+            copies.sent_now(flying["first", item - 1])
+        kept_slot = item % len(seq_bits)
+        if item >= len(seq_bits):
+            for copy in flying["later", item - len(seq_bits)]:
+                copies.sent_now(copy)
+            flying.pop(("out", item - len(seq_bits))).wait()
+        half = mixed_scr.shape[0] * mixed_scr.shape[2]
+        other = mixed_scr[:, 1 - core].reshape(half, -1)
+        mine = mixed_scr[:, core].reshape(half, -1)
+
+        @pl.loop(0, width // tile)
+        def _(order):
+            place = pl.ds(pl.multiple_of(order * tile, tile), tile)
+            weights = slice_ref[:, place]
+            target = other_scr
+            target[..., place] = dot(other, weights).astype(bf16).reshape(
+                target.shape[:-1] + (tile,)
+            )
+            target = kept_scr.at[kept_slot]
+            target[..., place] = dot(mine, weights).astype(bf16).reshape(
+                target.shape[:-1] + (tile,)
+            )
+
+        copy = copies.send(other_scr, step_scrs[0].at[slot], mask_of(seq_bits[0]))
+        flying[item] = copy, kept_scr.at[kept_slot]
+        flying["first", item] = copy
+        flying["later", item] = []
+
+    def bias_step():
+        done = len(bias_copies)
+        bias_copies[-1].wait_recv()
+        bias_scr[done] = bias_scr[done - 1] + bias_got[done - 1]
+        if done < len(bias_steps):
+            bias_copies.append(
+                copies.send(bias_scr.at[done], bias_got.at[done], mask_of(bias_steps[done]))
+            )
+        else:
+            bias_sum_ref[...] = bias_scr[done]
+
+    dense_sum.start()
+    products(0)
+    send_grads(1)
+    attention(0)
+    partial(0)
+    send_grads(2)
+    bias_step()
+    attention(1)
+    step_on(0, 0)
+    partial(1)
+    products(1)
+    send_grads(3)
+    step_on(1, 0)
+    bias_step()
+    attention(2)
+    step_on(0, 1)
+    partial(2)
+    absorb(1, 0)
+    bias_step()
+    dense_sum.advance()
+    attention(3)
+    step_on(2, 0)
+    step_on(1, 1)
+    step_on(0, 2)
+    partial(3)
+    sums_copy = copies.send(sums_scr.at[0], sums_got.at[0], mask_of(item_bits[0]))
+    products(2)
+    step_on(3, 0)
+    absorb(1, 1)
+    step_on(2, 1)
+    absorb(2, 0)
+    next_sum(0)
+    bias_step()
+    dense_sum.advance()
+    step_on(1, 2)
+    absorb(1, 2)
+    step_on(3, 1)
+    next_sum(1)
+    bias_step()
+    sums_all_ref[seq_place] = sums_scr[len(item_bits)].astype(bf16)
+    spread_sums()
+    absorb(2, 1)
+    step_on(2, 2)
+    absorb(3, 0)
+    to_members(0)
+    absorb(2, 2)
+    spread_sums()
+    dense_sum.advance()
+    step_on(3, 2)
+    absorb(3, 1)
+    to_members(1)
+    spread_sums()
+    while dense_sum.order < len(dense_steps):
+        dense_sum.advance()
+    absorb(3, 2)
+    to_members(2)
+    wait_all(arrivals)
+    while dense_sum.order < len(dense_steps):
+        dense_sum.advance()
+    dense_part_ref[...] = dense_sum.kept[...]
+    wait_all(shares)
+    for item in range(items_here):
+        if ("out", item) in flying:
+            flying["out", item].wait()
+    for copy in local:
+        copy.wait()
+    copies.end()
+
+
+def merged_call(
+    item_bits,
+    seq_bits,
+    visible,
+    onehots,
+    tables,
+    cosine,
+    sine_part,
+    log_sums,
+    w_slice,
+    grad_context,
+    shared,
+    grad_in,
+    grad_shared,
+    product,
+    by_rows,
+    in_sum,
+):
+    items_here, length, vocab = onehots.shape
+    heads_here = tables.shape[0]
+    seq_size = 2 ** len(seq_bits)
+    span = length // seq_size
+    width = w_slice.shape[1]
+    packed = heads_here * 3 * HEAD
+    any_space = pl.BlockSpec(memory_space=pl.ANY)
+    near_space = pl.BlockSpec(memory_space=pltpu.VMEM)
+    ff_part = product.shape[1]
+    group_rows = width * 4 // 2 ** (len(item_bits) + len(seq_bits))
+    rows = group_rows // 4
+    dense_depth = len(item_bits) + len(seq_bits) - 1
+    spread = (2,) * (len(seq_bits) - 1) + (span, width)
+    all_bits = len(item_bits) + len(seq_bits)
+    spare = (8 + seq_size) * items_here + 64 + 16 * all_bits
+    half = (group_rows // 2, ff_part)
+    return pl.pallas_call(
+        functools.partial(merged_kernel, item_bits, seq_bits),
+        in_specs=[pl.BlockSpec(memory_space=pltpu.SMEM)]
+        + [near_space] * 6
+        + [any_space] * 6
+        + [near_space],
+        out_specs=[any_space, near_space, any_space, near_space, near_space] + [any_space] * 3,
+        out_shape=[
+            jax.ShapeDtypeStruct((items_here, span, width), bf16),
+            jax.ShapeDtypeStruct((seq_size, heads_here, vocab, 3 * HEAD), bf16),
+            jax.ShapeDtypeStruct((3, 4, rows, ff_part), bf16),
+            jax.ShapeDtypeStruct(by_rows.shape[-2:], bf16),
+            jax.ShapeDtypeStruct(in_sum.shape, f32),
+            jax.ShapeDtypeStruct((3, 2, 4) + half, bf16),
+            jax.ShapeDtypeStruct((3, 2, 2) + half, bf16),
+            jax.ShapeDtypeStruct((3, 2, 1) + half, bf16),
+        ],
+        scratch_shapes=[
+            pltpu.VMEM((seq_size // 2, 2, span, packed), bf16),
+            pltpu.VMEM(spread, bf16),
+            pltpu.VMEM((len(seq_bits),) + spread, bf16),
+            tuple(
+                pltpu.VMEM((2 if order == 0 else items_here,) + spread[order:], bf16)
+                for order in range(len(seq_bits))
+            ),
+            pltpu.VMEM((len(item_bits) + 1, heads_here, vocab, 3 * HEAD), f32),
+            pltpu.VMEM((len(item_bits), heads_here, vocab, 3 * HEAD), f32),
+            pltpu.VMEM((all_bits + 1,) + in_sum.shape, f32),
+            pltpu.VMEM((all_bits,) + in_sum.shape, f32),
+            tuple(
+                pltpu.VMEM((2,) * order + by_rows.shape[-2:], bf16)
+                for order in range(dense_depth - 1, -1, -1)
+            ),
+            pltpu.VMEM((product.shape[0], ff_part), bf16),
+            pltpu.VMEM((2, product.shape[0], group_rows), bf16),
+            pltpu.VMEM((2 * group_rows, product.shape[0]), bf16),
+            pltpu.VMEM((2, 4) + half, bf16),
+            pltpu.VMEM((3, 2, 4) + half, bf16),
+            pltpu.VMEM((2,) + half, bf16),
+            pltpu.VMEM((2,) + by_rows.shape[-2:], bf16),
+            pltpu.VMEM((items_here, length, heads_here * HEAD), bf16),
+            pltpu.SemaphoreType.DMA((2,)),
+            pltpu.SemaphoreType.DMA((3,)),
+            pltpu.SemaphoreType.DMA((spare,)),
+            pltpu.SemaphoreType.DMA((spare,)),
+            pltpu.SemaphoreType.DMA((16,)),
+        ],
+        compiler_params=pltpu.CompilerParams(
+            collective_id=4, has_side_effects=True, vmem_limit_bytes=62 * 2**20
+        ),
+        name="merged",
+    )(
+        visible,
+        onehots,
+        tables,
+        cosine,
+        sine_part,
+        log_sums,
+        w_slice,
+        grad_context,
+        shared,
+        grad_in,
+        grad_shared,
+        product,
+        by_rows,
+        in_sum,
+    )
+
+
 def ff_kernel(
     item_bits,
     shared_ref,
@@ -1586,22 +2085,25 @@
         (0, flat_place * heads_bias.shape[0]),
     )
     ones_row = jnp.zeros((16, vocab), bf16).at[0].set(1.0)
+    def rows_of(part):
+        part = part.reshape(-1)
+        return jnp.pad(part, (0, -part.shape[0] % 128)).reshape(-1, 128)
+
     small = [
-        embedding.reshape(-1),
-        ones_row.reshape(-1),
-        input_ids.astype(bf16).reshape(-1),
-        dense_bias,
-        first_gain,
-        first_bias,
-        down_bias,
-        second_gain,
-        second_bias,
+        embedding,
+        ones_row,
+        rows_of(input_ids.astype(bf16)),
+        rows_of(
+            jnp.concatenate(
+                [dense_bias, first_gain, first_bias, down_bias, second_gain, second_bias]
+            )
+        ),
     ]
     ends = [0]
     for part in small:
         ends.append(ends[-1] + part.shape[0])
-    flat = jnp.concatenate(small)
-    flat = jnp.pad(flat, (0, -flat.shape[0] % 2048)).reshape(-1, 128)
+    small.append(jnp.zeros((-ends[-1] % 16, 128), bf16))
+    flat = jnp.concatenate(small, axis=0)
 
     def by_member(part):
         padded = jnp.pad(part, ((0, 0), (0, ff_all - ff_width)))
@@ -1634,13 +2136,11 @@
     )
     w_dense = w_dense.reshape(width, width)
     w_block = w_block[:, :rows_here].reshape(seq_size * rows_here, packed_width)
-    everyone = everyone.reshape(count, -1)
-    pieces = [everyone[:, a:b] for a, b in zip(ends[:-1], ends[1:])]
+    pieces = [everyone[:, :, a:b] for a, b in zip(ends[:-1], ends[1:])]
     table = pieces[0].reshape(width, vocab)
-    b_dense, gain_one, shift_one, b_down, gain_two, shift_two = (
-        part.reshape(-1).astype(f32) for part in pieces[3:]
-    )
-    ids_here = pick(pieces[2].reshape(items_size, seq_size, items_here, span), item_place, 0)
+    vector_rows = pieces[3].reshape(count, -1)[:, : 6 * rows_here].reshape(count, 6, rows_here)
+    vectors = jnp.transpose(vector_rows, (1, 0, 2)).reshape(6, width).astype(f32)
+    ids_here = pick(pieces[2], item_place, 0).reshape(seq_size, items_here, span)
     ids_here = jnp.transpose(ids_here, (1, 0, 2)).reshape(items_here, length).astype(jnp.int32)
     in_bias = jnp.pad(
         up_bias.astype(f32).reshape(2, ff_width), ((0, 0), (0, ff_all - ff_width))
@@ -1649,19 +2149,16 @@
     in_bias = woven(in_bias[:1], in_bias[1:])
 
     vocab_index = jnp.arange(vocab, dtype=jnp.int32)
-    positions = jnp.arange(length, dtype=f32)
-    frequency = jnp.exp(jnp.arange(HEAD // 2, dtype=f32) * (-2.0 * math.log(10000.0) / HEAD))
-    angles = positions[:, None] * frequency[None, :]
-    cosine = jnp.cos(angles)
-    sine_part = jnp.sin(angles)
-    cosine = jnp.concatenate([cosine, cosine], axis=1)
-    sine_part = jnp.concatenate([-sine_part, sine_part], axis=1)
+    frequency = np.exp(np.arange(HEAD // 2) * (-2.0 * math.log(10000.0) / HEAD))
+    angles = np.arange(length)[:, None] * frequency[None, :]
+    cosine, sine_part = np.cos(angles), np.sin(angles)
+    cosine = jnp.asarray(np.concatenate([cosine, cosine], axis=1), f32)
+    sine_part = jnp.asarray(np.concatenate([-sine_part, sine_part], axis=1), f32)
     visible = jnp.where(item_flag == 1, length, prefix)
     tables = table_halves(mixed_table)
     onehots = (ids_here[:, :, None] == vocab_index).astype(bf16)
     own_onehot = (input_ids.reshape(-1)[:, None] == vocab_index[None, :]).astype(bf16)
-    vectors = jnp.stack([gain_one, shift_one, b_down, gain_two, shift_two, b_dense])
-    vectors = jnp.pad(vectors, ((0, 2), (0, 0)))
+    vectors = jnp.concatenate([vectors[1:], vectors[:1], jnp.zeros((2, width), f32)], axis=0)
     context, log_sums, w_in, w_out, shared, normed, inverse = second_call(
         item_bits,
         seq_bits,
@@ -1695,39 +2192,34 @@
     grad_resid = grad_resid.reshape(rows_all, width)
     grad_branch = grad_resid.astype(bf16)
     grad_context = contract_cols(grad_branch, w_dense).astype(bf16)
-    grad_context = lax.all_to_all(
-        jnp.transpose(
-            grad_context.reshape(items_here, span, seq_size, heads_here * HEAD), (0, 2, 1, 3)
-        ),
-        "seq",
-        split_axis=1,
-        concat_axis=1,
-        tiled=True,
-    ).reshape(items_here, length, heads_here * HEAD)
-
-    vector_sums = sums[:6].T
-    token_sum = contract_rows(grad_branch, own_onehot)
-    grad_dense = contract_rows(context, grad_branch)
-    by_rows = jnp.concatenate(
-        [grad_dense, token_sum, jnp.pad(vector_sums, ((0, 0), (0, 122)))], axis=1
+    core = my_bit(*seq_bits[0])
+
+    def of_core(columns, which):
+        parts = columns.reshape(columns.shape[0], count // 2, 2, rows_here)
+        return pick(parts, which, 2).reshape(columns.shape[0], -1)
+
+    def row_sums(which):
+        grads = of_core(grad_branch, which)
+        return jnp.concatenate(
+            [
+                contract_rows(of_core(context, which), grad_branch).astype(bf16),
+                contract_rows(grads, own_onehot).astype(bf16),
+                jnp.pad(of_core(sums, which).T, ((0, 0), (0, 120))).astype(bf16),
+            ],
+            axis=1,
+        )
+
+    by_rows = (
+        row_sums(core).astype(f32) + lines.swap(row_sums(1 - core), *seq_bits[0]).astype(f32)
     ).astype(bf16)
-    row_dims = item_bits[::-1] + seq_bits[::-1]
+    row_dims = item_bits[::-1] + seq_bits[:0:-1]
     by_rows = by_rows.reshape((2,) * len(row_dims) + (rows_here, -1))
-    by_rows = halve(lines, by_rows, len(row_dims) - 1, *seq_bits[0])
-    by_rows = halve(lines, by_rows, 0, *row_dims[0])
-    grad_out_weight = contract_rows(
-        grad_shared.reshape(group_all, width), product.reshape(group_all, ff_part)
-    )
-    grad_in_weight = contract_rows(
-        shared.reshape(group_all, width), grad_in.reshape(group_all, 2 * ff_part)
-    )
-    group_dims = (2,) * (len(item_bits) + len(outer_bits)) + (members * rows_here, -1)
     in_sum = jnp.concatenate(unwoven(in_sum), axis=0)
     in_all = lax.dynamic_update_slice(
         jnp.zeros((2, ff_all), f32), in_sum, (0, member * ff_part)
     ).reshape(-1, 128)
     w_slice = w_slice.reshape(width, packed_width)
-    spread, token_all, in_part, out_part, by_rows, in_all = third_call(
+    attention = (
         item_bits,
         seq_bits,
         visible,
@@ -1737,12 +2229,43 @@
         sine_part,
         log_sums,
         w_slice.T,
-        grad_context,
-        grad_in_weight.astype(bf16).reshape(group_dims),
-        grad_out_weight.astype(bf16).reshape(group_dims),
-        by_rows,
-        in_all,
     )
+    shared = shared.reshape(group_all, width)
+    grad_in = grad_in.reshape(group_all, 2 * ff_part)
+    grad_shared = grad_shared.reshape(group_all, width)
+    product = product.reshape(group_all, ff_part)
+    if len(item_bits) == 2 and len(seq_bits) == 3 and rows_here % 32 == 0:
+        spread, token_all, parts, by_rows, in_all = merged_call(
+            *attention,
+            grad_context.reshape(items_here, span, width),
+            shared,
+            grad_in,
+            grad_shared,
+            product,
+            by_rows,
+            in_all,
+        )[:5]
+        in_part = jnp.concatenate([parts[1], parts[2]], axis=-1)
+        out_part = parts[0]
+    else:
+        by_head = lax.all_to_all(
+            jnp.transpose(
+                grad_context.reshape(items_here, span, seq_size, heads_here * HEAD), (0, 2, 1, 3)
+            ),
+            "seq",
+            split_axis=1,
+            concat_axis=1,
+            tiled=True,
+        ).reshape(items_here, length, heads_here * HEAD)
+        group_dims = (2,) * (len(item_bits) + len(outer_bits)) + (members * rows_here, -1)
+        spread, token_all, in_part, out_part, by_rows, in_all = third_call(
+            *attention,
+            by_head,
+            contract_rows(shared, grad_in).astype(bf16).reshape(group_dims),
+            contract_rows(grad_shared, product).astype(bf16).reshape(group_dims),
+            by_rows,
+            in_all,
+        )
     input_grads = spread.astype(f32) + deep_alpha * grad_resid.reshape(spread.shape)
     token_all = jnp.transpose(token_all, (2, 0, 1, 3)).reshape(vocab, -1)
 

time: 1070 us -> 988 us (0.923)
  matrix products: 71.9 us -> 22.9 us
  waiting for transfers between devices: 30.3 us -> 0.01 us
  Pallas kernels: 835 us -> 858 us
  other arithmetic: 35.6 us -> 23.5 us
    dot_general x4, matrix products: 60.7 us -> 9.44 us  [contract_rows(): lax.dot_general(left, right, (((0,), (0,)), ((), ())), preferred_element_...]
    ppermute x2 -> x1, waiting for transfers between devices: 30.3 us -> 0.01 us  [swap(): got = lax.ppermute(part, axis, [(j, j ^ bit) for j in range(size)])]
    pallas_call x1, Pallas kernels: 343 us -> 366 us  [merged_call(): pl.pallas_call(functools.partial(merged_kernel, item_bits, seq_bits), in_...]
  transfers between devices with their start and end apart: 3 -> 1, of which waited for: 1 -> 0; matrix products, arithmetic and copies ran while one was open for 7% -> 2% of each run, Pallas kernels for 0% -> 0%
where the time goes in v5:
time: 988 us; the launch traced here: 983 us
  Pallas kernels  858 us (87%)
  local copies, waits for them, and re-layouts  74.5 us (8%)
  other arithmetic  23.5 us (2%)
  matrix products  22.9 us (2%)
    pallas_call x1, Pallas kernels, merged_call(): pl.pallas_call(functools.partial(merged_kernel, item_bits, seq_bits), in_...  366 us
    pallas_call x1, Pallas kernels, ff_call(): pl.pallas_call(functools.partial(ff_kernel, item_bits), in_specs=[any_spa...  205 us
    pallas_call x1, Pallas kernels, second_call(): pl.pallas_call(functools.partial(second_kernel, item_bits, seq_bits), in_...  184 us
    pallas_call x1, Pallas kernels, first_call(): pl.pallas_call(functools.partial(first_kernel, item_bits, seq_bits, row_c...  104 us
  transfers between devices with their start and end apart: 1, of which 0 were waited for; matrix products, arithmetic and copies ran while one was open for 2% of the time, Pallas kernels for 0%

profile of v5, /device:TPU:0, one launch (start us, length us, event | category | flops | bytes accessed | tf_op | source)
XLA Modules:
  0.0 982.7 jit_solution(5106973225678244971)
XLA Ops:
  5.2 2.2 copy.65
  12.9 104.4 %first.1 = (bf16[4,8,96,128]{3,2,1,0:T(8,128)(2,1)S(1)}, f32[128,768]{1,0:T(8,128)S(1)}, bf16[8,80,768]{2,1,0:T(8,128)(2,1)S(1)}, bf16[4,4,2,64,2048]{4,3,2,1,0:...) custom-call(bf16[96,128]{1,0:T(8,128)(2,1)S(1)} %concatenate.33.small_ref, ...), custom_call_target="tpu_custom_call" | custom-call | tf_op jit(solution)/shard_map/first/pallas_call | solution.py:348
  117.3 3.3 copy-done
  130.2 2.0 fusion.4.onehot_ref
  136.8 183.6 %second.1 = (bf16[4,128,2048]{2,1,0:T(8,128)(2,1)}, f32[4,2,1,1024]{3,2,1,0:T(1,128)}, bf16[8,256,2816]{2,1,0:T(8,128)(2,1)}, bf16[8,256,1408]{2,1,0:T(8,128)(2,...) custom-call(s32[4]{0:T(128)} %compare_select_fusion.1.visible_ref, ...), custom_call_target="tpu_custom_call" | custom-call | tf_op jit(solution)/shard_map/second/pallas_call | solution.py:635
  320.4 204.6 %feed_forward.1 = (bf16[4,512,1408]{2,1,0:T(8,128)(2,1)}, bf16[4,2,512,1408]{3,2,1,0:T(8,128)(2,1)}, bf16[4,4,128,2048]{3,2,1,0:T(8,128)(2,1)}, bf16[4,512,2816]...) custom-call(bf16[4,4,128,2048]{3,2,1,0:T(8,128)(2,1)} %get-tuple-ele, ...), custom_call_target="tpu_custom_call" | custom-call | tf_op jit(solution)/shard_map/feed_forward/pallas_call | solution.py:1999
  525.0 3.8 convert_element_type.114
  528.8 4.2 copy.72
  533.1 4.1 convert_element_type.118
  537.2 4.2 copy.71
  541.4 4.2 reshape_reshape.2
  545.6 3.6 constant_dynamic-slice_fusion.2
  550.9 4.0 convolution_convert_fusion
  554.9 2.3 fusion.3
  560.0 4.6 copy.85
  565.2 4.4 convolution_convert_fusion.1
  569.6 9.1 convolution_convert_fusion.2
  578.7 4.7 add_convert_fusion
  583.3 365.8 %merged.1 = (bf16[4,128,2048]{2,1,0:T(8,128)(2,1)}, bf16[8,2,128,384]{3,2,1,0:T(8,128)(2,1)}, bf16[3,4,64,1408]{3,2,1,0:T(8,128)(2,1)}, bf16[64,2304]{1,0:T(8,12...) custom-call(s32[4]{0:T(128)} %compare_select_fusion.1.visible_ref, ...), custom_call_target="tpu_custom_call" | custom-call | tf_op jit(solution)/shard_map/merged/pallas_call | solution.py:1592
  949.1 2.6 copy.77
  951.8 3.4 convolution_bitcast_fusion
  960.3 7.8 slice_reduce_fusion.1
  972.5 2.7 multiply_add_fusion
  979.3 3.2 copy.100
  (155 shorter events, 42.4 us)
Async XLA Ops:
  7.5 4.8 copy-start.28
  7.5 4.8 copy-start.29
  8.7 3.9 copy-start.30
  8.7 3.9 copy-start.31
  8.7 3.9 copy-start.32
  8.7 3.9 copy-start.33
  8.7 3.9 copy-start.34
  8.7 3.9 copy-start.35
  8.7 4.0 copy-start.21
  8.7 4.0 copy-start.27
  8.7 4.1 copy-start.1
  8.8 4.1 copy-start.8
  124.7 8.3 copy-start.24
  125.6 7.6 copy-start.5
  128.8 6.2 copy-start.36
  128.8 6.2 copy-start.37
  545.6 4.2 copy-start.22
  550.9 4.0 copy-start.19
  554.9 4.2 copy-start.25
  557.2 21.5 %collective-permute-start = (bf16[1024,2304]{1,0:T(8,128)(2,1)}, bf16[1024,2304]{1,0:T(8,128)(2,1)}, u32[]{:S(2)}, u32[]{:S(2)}) collective-permute-start(bf16[1024,2304]{1,0:T(8,128)(2,1)} %fusion.3), channel_id=1, source_target_pairs={{0,1},{1,0},{2,3},{3,2},{4,5},{5,4},{6,7},{7,6},{8,9},{9,8},{10,11... | collective-permute-start | bytes 14155784 | tf_op jit(solution)/shard_map/ppermute | solution.py:34
  565.1 4.4 copy-start.11
  951.8 5.9 copy-start.12
  972.5 3.5 copy-start.23
  972.5 4.3 copy-start.20
  (15 other events, 30.4 us)

commit v6 on v5

--- a/solution.py
+++ b/solution.py
@@ -1243,9 +1243,10 @@
 
     landed, slots, sends = {}, {}, {}
 
-    def products(block):
-        load_rhs(block).wait()
-        for pair, steps in enumerate(pairs):
+    def products(block, first):
+        if first == 0:
+            load_rhs(block).wait()
+        for pair, steps in list(enumerate(pairs))[first : first + 2]:
             for which in range(2):
                 load_lhs(block, pair, which).wait()
                 rows = pl.ds(which * group_rows, group_rows)
@@ -1289,7 +1290,7 @@
                         )
                         slots[way, place] = copy
                         landed[1, block, way, place] = copy
-        if block + 1 < len(blocks):
+        if first and block + 1 < len(blocks):
             load_rhs(block + 1).start()
 
     lands = {1: land_one_ref, 2: land_two_ref, 3: land_three_ref}
@@ -1358,16 +1359,25 @@
     for which in range(2):
         load_lhs(0, 0, which).start()
     dense_steps = item_bits[::-1] + seq_bits[:0:-1]
-    dense_sum = Reduce(
-        copies,
-        dense_ref,
-        pl.ds(0, dense_ref.shape[-2]),
-        dense_steps,
-        dense_steps,
-        list(dense_got),
-        dense_scr,
-        stage_sems,
-    )
+    dense_half = dense_ref.shape[-2] // 2
+    dense_sums = [
+        Reduce(
+            copies,
+            dense_ref,
+            pl.ds(order * dense_half, dense_half),
+            dense_steps,
+            steps + dense_steps[2:],
+            list(dense_got[order]),
+            dense_scr,
+            stage_sems,
+        )
+        for order, steps in enumerate(([two, one], [one, two]))
+    ]
+
+    def dense_advance():
+        for part in dense_sums:
+            part.advance()
+
     sums_scr[...] = jnp.zeros_like(sums_scr)
     tile = 256
     flying = {}
@@ -1486,66 +1496,68 @@
         else:
             bias_sum_ref[...] = bias_scr[done]
 
-    dense_sum.start()
-    products(0)
+    products(0, 0)
+    for part in dense_sums:
+        part.start()
     send_grads(1)
     attention(0)
     partial(0)
+    products(0, 2)
     send_grads(2)
     bias_step()
+    step_on(0, 0)
     attention(1)
-    step_on(0, 0)
     partial(1)
-    products(1)
+    products(1, 0)
     send_grads(3)
     step_on(1, 0)
     bias_step()
+    step_on(0, 1)
+    products(1, 2)
+    absorb(1, 0)
+    dense_advance()
     attention(2)
-    step_on(0, 1)
     partial(2)
-    absorb(1, 0)
-    bias_step()
-    dense_sum.advance()
-    attention(3)
+    products(2, 0)
     step_on(2, 0)
     step_on(1, 1)
+    bias_step()
+    products(2, 2)
+    dense_advance()
+    absorb(1, 1)
+    attention(3)
+    absorb(2, 0)
     step_on(0, 2)
     partial(3)
     sums_copy = copies.send(sums_scr.at[0], sums_got.at[0], mask_of(item_bits[0]))
-    products(2)
+    step_on(2, 1)
+    dense_advance()
     step_on(3, 0)
-    absorb(1, 1)
-    step_on(2, 1)
-    absorb(2, 0)
+    absorb(1, 2)
     next_sum(0)
     bias_step()
-    dense_sum.advance()
     step_on(1, 2)
-    absorb(1, 2)
+    absorb(2, 1)
+    dense_advance()
     step_on(3, 1)
     next_sum(1)
     bias_step()
     sums_all_ref[seq_place] = sums_scr[len(item_bits)].astype(bf16)
     spread_sums()
-    absorb(2, 1)
-    step_on(2, 2)
+    absorb(2, 2)
     absorb(3, 0)
     to_members(0)
-    absorb(2, 2)
+    step_on(2, 2)
     spread_sums()
-    dense_sum.advance()
-    step_on(3, 2)
     absorb(3, 1)
     to_members(1)
+    step_on(3, 2)
     spread_sums()
-    while dense_sum.order < len(dense_steps):
-        dense_sum.advance()
     absorb(3, 2)
     to_members(2)
+    for order, part in enumerate(dense_sums):
+        dense_part_ref[pl.ds(order * dense_half, dense_half)] = part.kept[...]
     wait_all(arrivals)
-    while dense_sum.order < len(dense_steps):
-        dense_sum.advance()
-    dense_part_ref[...] = dense_sum.kept[...]
     wait_all(shares)
     for item in range(items_here):
         if ("out", item) in flying:
@@ -1619,8 +1631,11 @@
             pltpu.VMEM((all_bits + 1,) + in_sum.shape, f32),
             pltpu.VMEM((all_bits,) + in_sum.shape, f32),
             tuple(
-                pltpu.VMEM((2,) * order + by_rows.shape[-2:], bf16)
-                for order in range(dense_depth - 1, -1, -1)
+                tuple(
+                    pltpu.VMEM((2,) * order + (by_rows.shape[-2] // 2, by_rows.shape[-1]), bf16)
+                    for order in range(dense_depth - 1, -1, -1)
+                )
+                for _ in range(2)
             ),
             pltpu.VMEM((product.shape[0], ff_part), bf16),
             pltpu.VMEM((2, product.shape[0], group_rows), bf16),
@@ -1658,6 +1673,85 @@
     )
 
 
+def weave_kernel(ff_width, members, padded_ref, woven_ref):
+    rows = padded_ref.shape[0]
+    tiles = woven_ref.shape[2] // 256
+    base, shift = ff_width // 128, ff_width % 128
+    lane = lax.broadcasted_iota(jnp.int32, (rows, 128), 1)
+    last = padded_ref.shape[1] // 128 - 1
+
+    def turned(tile):
+        part = padded_ref[:, tile * 128 : (tile + 1) * 128].astype(f32)
+        return pltpu.roll(part, (128 - shift) % 128, 1)
+
+    before = turned(base)
+    for order in range(members * tiles):
+        left = ff_width - order * 128
+        if left <= 0:
+            up_part = gate = jnp.zeros((rows, 128), bf16)
+        else:
+            up_part = padded_ref[:, order * 128 : (order + 1) * 128].astype(f32)
+            after = turned(min(base + order + 1, last))
+            gate = jnp.where(lane < 128 - shift, before, after)
+            before = after
+            if left < 128:
+                up_part = jnp.where(lane < left, up_part, 0.0)
+                gate = jnp.where(lane < left, gate, 0.0)
+            up_part, gate = up_part.astype(bf16), gate.astype(bf16)
+        member, tile = order // tiles, order % tiles
+        woven_ref[member, :, tile * 256 : tile * 256 + 128] = up_part
+        woven_ref[member, :, tile * 256 + 128 : (tile + 1) * 256] = gate
+
+
+def weave(up_weight, ff_width, members, ff_part):
+    rows, columns = up_weight.shape
+    wide = -(-columns // 128) * 128
+    padded = jnp.pad(up_weight, ((0, 0), (0, wide - columns)))
+    return pl.pallas_call(
+        functools.partial(weave_kernel, ff_width, members),
+        in_specs=[pl.BlockSpec(memory_space=pltpu.VMEM)],
+        out_specs=pl.BlockSpec(memory_space=pltpu.VMEM),
+        out_shape=jax.ShapeDtypeStruct((members, rows, 2 * ff_part), bf16),
+        compiler_params=pltpu.CompilerParams(vmem_limit_bytes=24 * 2**20),
+        name="weave",
+    )(padded)
+
+
+def unweave_kernel(ff_width, woven_ref, whole_ref):
+    members, rows, columns = woven_ref.shape
+    tiles = columns // 256
+    base, shift = ff_width // 128, ff_width % 128
+    lane = lax.broadcasted_iota(jnp.int32, (rows, 128), 1)
+
+    def part(order, which):
+        first = order % tiles * 256 + which * 128
+        return woven_ref[order // tiles, :, first : first + 128].astype(f32)
+
+    for order in range(base):
+        whole_ref[:, order * 128 : (order + 1) * 128] = part(order, 0)
+    before = part(base, 0)
+    width = whole_ref.shape[1]
+    for order in range(base, -(-width // 128)):
+        if order - base < members * tiles:
+            after = pltpu.roll(part(order - base, 1), shift, 1)
+        first = order * 128
+        count = min(128, width - first)
+        whole_ref[:, first : first + count] = jnp.where(lane < shift, before, after)[:, :count]
+        before = after
+
+
+def unweave(woven, ff_width):
+    rows = woven.shape[1]
+    return pl.pallas_call(
+        functools.partial(unweave_kernel, ff_width),
+        in_specs=[pl.BlockSpec(memory_space=pltpu.VMEM)],
+        out_specs=pl.BlockSpec(memory_space=pltpu.VMEM),
+        out_shape=jax.ShapeDtypeStruct((rows, 2 * ff_width), f32),
+        compiler_params=pltpu.CompilerParams(vmem_limit_bytes=24 * 2**20),
+        name="unweave",
+    )(woven)
+
+
 def ff_kernel(
     item_bits,
     shared_ref,
@@ -1678,6 +1772,7 @@
     sums_ref,
     in_sum_ref,
     slices_ref,
+    branch_ref,
     rows_scr,
     product_scr,
     save_scr,
@@ -1924,6 +2019,11 @@
         slot = chunk % 2
         state["far", ("back", chunk)].wait_recv()
         loaded(("normed", slot))
+        for key in ("low near", "low far"):
+            copy = state.pop((key, slot), None)
+            if copy is not None:
+                copies.sent_now(copy)
+        keep_done(("branch", slot))
 
         def body(rows):
             grad = parts_scr[slot, 0, rows].astype(f32) + far_got[chunk, rows].astype(f32)
@@ -1934,12 +2034,15 @@
             resid_scr[chunk, rows] = resid
             add_sum(0, grad * normed)
             add_sum(1, grad)
-            add_sum(2, resid.astype(bf16).astype(f32))
+            low = resid.astype(bf16)
+            low_scr[slot, rows] = low
+            add_sum(2, low.astype(f32))
 
         row_blocks(body)
         if chunk + 2 < chunks:
             load_normed(chunk + 2)
         keep(("resid", chunk), 7 + chunk, resid_scr.at[chunk], resid_ref.at[chunk])
+        keep(("branch", slot), 7 + chunks + slot, low_scr.at[slot], branch_ref.at[chunk])
 
     load_shared(0)
     load_normed(0)
@@ -1957,27 +2060,22 @@
     sum_near(last, last)
     second_norm(last - 1)
     pass_on(last - 2)
-    waiting = [("norm", last), ("pass", last - 1), ("pass", last)]
+    load_grads(0)
     for chunk in range(chunks):
+        backward_gate(chunk)
+        if chunk >= 2:
+            first_norm(chunk - 2)
+        backward_in(chunk)
+        spread_block()
         if chunk == 0:
-            load_grads(0)
-        backward_gate(chunk)
-        spread_block()
-        if waiting and waiting[0][0] == "norm":
-            second_norm(waiting.pop(0)[1])
+            second_norm(last)
             load_normed(0)
             load_normed(1)
-        if waiting:
-            pass_on(waiting.pop(0)[1])
-        if chunk >= 1:
-            sum_near(("back", chunk - 1), chunk - 1)
-        if chunk >= 2:
-            first_norm(chunk - 2)
+        elif chunk + 1 < chunks:
+            pass_on(chunk + 1)
         if chunk + 1 < chunks:
-            if chunk + 1 == last and waiting:
-                pass_on(waiting.pop(0)[1])
             load_grads(chunk + 1)
-        backward_in(chunk)
+            sum_near(("back", chunk), chunk)
     sum_near(("back", last), last)
     first_norm(last - 1)
     first_norm(last)
@@ -1999,7 +2097,7 @@
     return pl.pallas_call(
         functools.partial(ff_kernel, item_bits),
         in_specs=[any_space, any_space] + [near_space] * 6 + [any_space],
-        out_specs=[any_space] * 4 + [near_space, any_space, near_space, near_space, any_space],
+        out_specs=[any_space] * 4 + [near_space, any_space, near_space, near_space, any_space, any_space],
         out_shape=[
             jax.ShapeDtypeStruct((chunks, group_rows, ff_part), bf16),
             jax.ShapeDtypeStruct((chunks, 2, group_rows, ff_part), bf16),
@@ -2010,6 +2108,7 @@
             jax.ShapeDtypeStruct((8, width), f32),
             jax.ShapeDtypeStruct((1, 2 * ff_part), f32),
             jax.ShapeDtypeStruct((2 ** len(item_bits),) + block.shape, bf16),
+            jax.ShapeDtypeStruct((chunks, span, width), bf16),
         ],
         scratch_shapes=[
             pltpu.VMEM((2, blocks, span, width), bf16),
@@ -2026,7 +2125,7 @@
             pltpu.SemaphoreType.DMA((spare,)),
             pltpu.SemaphoreType.DMA((spare,)),
             pltpu.SemaphoreType.DMA((6,)),
-            pltpu.SemaphoreType.DMA((8 + chunks,)),
+            pltpu.SemaphoreType.DMA((10 + chunks,)),
         ],
         compiler_params=pltpu.CompilerParams(
             collective_id=3, has_side_effects=True, vmem_limit_bytes=60 * 2**20
@@ -2122,7 +2221,9 @@
         shape = both_parts.shape[:-1] + (ff_part,)
         return parts[..., 0, :].reshape(shape), parts[..., 1, :].reshape(shape)
 
-    parts_in = woven(by_member(up_weight[:, :ff_width]), by_member(up_weight[:, ff_width:]))
+    parts_in = weave(up_weight, ff_width, members, ff_part).reshape(
+        2, 2, rows_here, 2 * ff_part
+    )
     parts_out = by_member(down_weight.T)
     everyone, mixed_table, w_block, w_dense, own_in, own_out = first_call(
         item_bits,
@@ -2174,7 +2275,18 @@
         own_in,
         own_out,
     )
-    product, _, grad_shared, grad_in, layer_out, grad_resid, sums, in_sum, w_slice = ff_call(
+    (
+        product,
+        _,
+        grad_shared,
+        grad_in,
+        layer_out,
+        grad_resid,
+        sums,
+        in_sum,
+        w_slice,
+        grad_branch,
+    ) = ff_call(
         item_bits,
         shared,
         normed,
@@ -2189,29 +2301,26 @@
     rows_all = items_here * span
     group_all = members * rows_all
     context = context.reshape(rows_all, width)
-    grad_resid = grad_resid.reshape(rows_all, width)
-    grad_branch = grad_resid.astype(bf16)
+    grad_branch = grad_branch.reshape(rows_all, width)
     grad_context = contract_cols(grad_branch, w_dense).astype(bf16)
     core = my_bit(*seq_bits[0])
 
-    def of_core(columns, which):
-        parts = columns.reshape(columns.shape[0], count // 2, 2, rows_here)
-        return pick(parts, which, 2).reshape(columns.shape[0], -1)
-
-    def row_sums(which):
-        grads = of_core(grad_branch, which)
-        return jnp.concatenate(
-            [
-                contract_rows(of_core(context, which), grad_branch).astype(bf16),
-                contract_rows(grads, own_onehot).astype(bf16),
-                jnp.pad(of_core(sums, which).T, ((0, 0), (0, 120))).astype(bf16),
-            ],
-            axis=1,
-        )
-
-    by_rows = (
-        row_sums(core).astype(f32) + lines.swap(row_sums(1 - core), *seq_bits[0]).astype(f32)
-    ).astype(bf16)
+    def core_sum(whole):
+        parts = whole.reshape(count // 2, 2, rows_here, -1)
+        got = lines.swap(pick(parts, 1 - core, 1), *seq_bits[0])
+        return (pick(parts, core, 1).astype(f32) + got.astype(f32)).astype(bf16)
+
+    small_sums = jnp.concatenate(
+        [
+            contract_rows(grad_branch, own_onehot).astype(bf16),
+            contract_rows(sums.astype(bf16), jnp.eye(8, 128, dtype=bf16)).astype(bf16),
+        ],
+        axis=1,
+    )
+    by_rows = jnp.concatenate(
+        [core_sum(contract_rows(context, grad_branch).astype(bf16)), core_sum(small_sums)],
+        axis=-1,
+    )
     row_dims = item_bits[::-1] + seq_bits[:0:-1]
     by_rows = by_rows.reshape((2,) * len(row_dims) + (rows_here, -1))
     in_sum = jnp.concatenate(unwoven(in_sum), axis=0)
@@ -2273,7 +2382,7 @@
         taken = jnp.transpose(part, (1, 0, 2)).reshape(rows_here, ff_all)
         return taken[:, :ff_width].astype(f32)
 
-    grad_up, grad_gate = (from_members(part) for part in unwoven(in_part))
+    grad_up_weight = unweave(in_part, ff_width)
     grad_down = from_members(out_part)
     by_rows = by_rows.astype(f32)
     grad_dense = by_rows[:, :width]
@@ -2300,7 +2409,7 @@
         own_vectors[2],
         own_vectors[0],
         own_vectors[1],
-        jnp.concatenate([grad_up, grad_gate], axis=1),
+        grad_up_weight,
         grad_up_bias,
         grad_down.T,
         own_vectors[5],

time: 988 us -> 924 us (0.935)
  local copies, waits for them, and re-layouts: 74.5 us -> 37.5 us
  Pallas kernels: 858 us -> 831 us
    pallas_call x1, Pallas kernels: 366 us -> 333 us  [merged_call(): pl.pallas_call(functools.partial(merged_kernel, item_bits, seq_bits), in_...]
  transfers between devices with their start and end apart: 1 -> 2, of which waited for: 0 -> 0; matrix products, arithmetic and copies ran while one was open for 2% -> 3% of each run, Pallas kernels for 0% -> 0%
where the time goes in v6:
time: 924 us; the launch traced here: 916 us
  Pallas kernels  831 us (90%)
  local copies, waits for them, and re-layouts  37.5 us (4%)
  matrix products  25.2 us (3%)
  other arithmetic  19.4 us (2%)
    pallas_call x1, Pallas kernels, merged_call(): pl.pallas_call(functools.partial(merged_kernel, item_bits, seq_bits), in_...  333 us
    pallas_call x1, Pallas kernels, ff_call(): pl.pallas_call(functools.partial(ff_kernel, item_bits), in_specs=[any_spa...  209 us
    pallas_call x1, Pallas kernels, second_call(): pl.pallas_call(functools.partial(second_kernel, item_bits, seq_bits), in_...  184 us
    pallas_call x1, Pallas kernels, first_call(): pl.pallas_call(functools.partial(first_kernel, item_bits, seq_bits, row_c...  104 us
  transfers between devices with their start and end apart: 2, of which 0 were waited for; matrix products, arithmetic and copies ran while one was open for 3% of the time, Pallas kernels for 0%

profile of v6, /device:TPU:0, one launch (start us, length us, event | category | flops | bytes accessed | tf_op | source)
XLA Modules:
  0.0 915.8 jit_solution(6965155716361930532)
XLA Ops:
  1.4 1.4 pad.17.padded_ref
  4.4 1.2 copy.56
  6.3 104.4 %first.1 = (bf16[4,8,96,128]{3,2,1,0:T(8,128)(2,1)S(1)}, f32[128,768]{1,0:T(8,128)S(1)}, bf16[8,80,768]{2,1,0:T(8,128)(2,1)S(1)}, bf16[4,4,2,64,2048]{4,3,2,1,0:...) custom-call(bf16[96,128]{1,0:T(8,128)(2,1)S(1)} %concatenate.27.small_ref, ...), custom_call_target="tpu_custom_call" | custom-call | tf_op jit(solution)/shard_map/first/pallas_call | solution.py:348
  110.7 3.3 copy-done
  114.0 1.6 copy-done.2
  120.2 1.9 slice.93
  122.2 1.2 copy.42
  123.7 2.0 fusion.1.onehot_ref
  130.2 183.6 %second.1 = (bf16[4,128,2048]{2,1,0:T(8,128)(2,1)}, f32[4,2,1,1024]{3,2,1,0:T(1,128)}, bf16[8,256,2816]{2,1,0:T(8,128)(2,1)}, bf16[8,256,1408]{2,1,0:T(8,128)(2,...) custom-call(s32[4]{0:T(128)} %compare_select_fusion.1.visible_ref, ...), custom_call_target="tpu_custom_call" | custom-call | tf_op jit(solution)/shard_map/second/pallas_call | solution.py:635
  313.9 208.5 %feed_forward.1 = (bf16[4,512,1408]{2,1,0:T(8,128)(2,1)}, bf16[4,2,512,1408]{3,2,1,0:T(8,128)(2,1)}, bf16[4,4,128,2048]{3,2,1,0:T(8,128)(2,1)}, bf16[4,512,2816]...) custom-call(bf16[4,4,128,2048]{3,2,1,0:T(8,128)(2,1)} %get-tuple-ele, ...), custom_call_target="tpu_custom_call" | custom-call | tf_op jit(solution)/shard_map/feed_forward/pallas_call | solution.py:2097
  522.4 8.3 bitcast_convert_fusion
  530.8 4.8 dynamic-slice_bitcast_fusion
  536.7 2.1 convolution_convert_fusion.2
  539.5 4.9 copy.52
  544.5 10.0 %convolution_convert_fusion = bf16[512,2048]{1,0:T(8,128)(2,1)} fusion(bf16[512,2048]{1,0:T(8,128)(2,1)} %bitcast.111, bf16[2048,2048]{1,0:T(8,128)(2,1)} %bitcast.95), kind=kOutput, calls=%fused_computation.8 | convolution fusion | flops 4296015872 | bytes 12582912 | tf_op jit(solution)/shard_map/dot_general | solution.py:65
  555.0 4.1 fusion
  559.3 2.7 pad_maximum_fusion
  562.0 332.8 %merged.1 = (bf16[4,128,2048]{2,1,0:T(8,128)(2,1)}, bf16[8,2,128,384]{3,2,1,0:T(8,128)(2,1)}, bf16[3,4,64,1408]{3,2,1,0:T(8,128)(2,1)}, bf16[64,2304]{1,0:T(8,12...) custom-call(s32[4]{0:T(128)} %compare_select_fusion.1.visible_ref, ...), custom_call_target="tpu_custom_call" | custom-call | tf_op jit(solution)/shard_map/merged/pallas_call | solution.py:1604
  894.7 2.8 copy.49
  897.6 3.4 convolution_bitcast_fusion
  903.4 1.9 unweave.1
  905.4 1.2 convert_bitcast_fusion
  908.8 5.3 multiply_add_fusion
  914.1 1.3 copy.60
  (128 shorter events, 19.4 us)
Async XLA Ops:
  2.8 2.8 copy-start.22
  2.9 2.8 copy-start.23
  3.2 2.7 copy-start.24
  3.3 2.8 copy-start.16
  3.3 2.8 copy-start.21
  3.3 3.0 copy-start.1
  3.3 3.0 copy-start.8
  110.6 3.3 copy-start
  118.1 8.3 copy-start.19
  119.0 7.6 copy-start.5
  122.2 6.2 copy-start.31
  122.2 6.2 copy-start.32
  313.9 208.6 %copy-start.30 = (bf16[4,128,2048]{2,1,0:T(8,128)(2,1)S(1)}, bf16[4,128,2048]{2,1,0:T(8,128)(2,1)}, u32[]{:S(2)}) copy-start(bf16[4,128,2048]{2,1,0:T(8,128)(2,1)} %get-tuple-element.73) | copy-start | bytes 6291460
  530.8 4.8 copy-start.20
  530.8 5.6 copy-start.17
  535.6 18.9 %collective-permute-start = (bf16[16,64,2048]{2,1,0:T(8,128)(2,1)}, bf16[16,64,2048]{2,1,0:T(8,128)(2,1)}, u32[]{:S(2)}, u32[]{:S(2)}) collective-permute-start(bf16[16,64,2048]{2,1,0:T(8,128)(2,1)} %dynamic-slice_bitcast_fusion), channel_id=1, source_target_pairs={{0,1},{1,0},{2,3},{3,2},{4,5},{5,4},{6,7},{7,6},{8,9},{9,8},{10,11... | collective-permute-start | bytes 12582920 | tf_op jit(solution)/shard_map/ppermute | solution.py:34
  544.4 10.6 %slice-start = ((s8[8388608]{0:T(1024)(128)(4,1)}), s8[4194304]{0:T(1024)(128)(4,1)S(1)}, s32[]{:S(2)}) async-start(s8[8388608]{0:T(1024)(128)(4,1)} %bitcast.106), calls=%async_computation | async-start | bytes 8388608
  544.5 10.5 %slice-start.1 = ((s8[8388608]{0:T(1024)(128)(4,1)}), s8[4194304]{0:T(1024)(128)(4,1)S(1)}, s32[]{:S(2)}) async-start(s8[8388608]{0:T(1024)(128)(4,1)} %bitcast.106), calls=%async_computation.1 | async-start | bytes 8388608
  554.5 4.6 collective-permute-start.1
  894.7 2.8 copy-start.11
  897.6 3.4 copy-start.9
  897.6 5.2 copy-start.10
  905.3 3.5 copy-start.13
  908.8 5.3 copy-start.14
  (13 other events, 25.4 us)

commit v7 on v6

--- a/solution.py
+++ b/solution.py
@@ -838,7 +838,7 @@
     seq_place = lax.axis_index("seq")
     member = seq_place % 4
     outer_bits = seq_bits[2:]
-    width = slice_ref.shape[1]
+    width = slice_ref.shape[0]
     greet(partners(seq_size, item_bits))
     copies = Copies(send_sems, recv_sems, local_sems)
     dims = item_bits[::-1] + outer_bits[::-1]
@@ -955,13 +955,13 @@
             @pl.loop(0, width // tile)
             def _(order):
                 place = pl.ds(pl.multiple_of(order * tile, tile), tile)
-                weights = slice_ref[:, place]
+                weights = slice_ref[place, :]
                 target = other_scr.at[slot]
-                target[..., place] = dot(other, weights).astype(bf16).reshape(
+                target[..., place] = contract_cols(other, weights).astype(bf16).reshape(
                     target.shape[:-1] + (tile,)
                 )
                 target = kept_scr.at[kept_slot]
-                target[..., place] = dot(mine, weights).astype(bf16).reshape(
+                target[..., place] = contract_cols(mine, weights).astype(bf16).reshape(
                     target.shape[:-1] + (tile,)
                 )
 
@@ -1074,7 +1074,7 @@
     heads_here = tables.shape[0]
     seq_size = 2 ** len(seq_bits)
     span = length // seq_size
-    width = w_slice.shape[1]
+    width = w_slice.shape[0]
     packed = heads_here * 3 * HEAD
     outer = len(seq_bits) - 2
     levels = len(item_bits) + outer
@@ -1207,7 +1207,7 @@
     seq_place = lax.axis_index("seq")
     member = seq_place % 4
     outer_bits = seq_bits[2:]
-    width = slice_ref.shape[1]
+    width = slice_ref.shape[0]
     greet(partners(seq_size, item_bits))
     copies = Copies(send_sems, recv_sems, local_sems)
 
@@ -1470,13 +1470,13 @@
         @pl.loop(0, width // tile)
         def _(order):
             place = pl.ds(pl.multiple_of(order * tile, tile), tile)
-            weights = slice_ref[:, place]
+            weights = slice_ref[place, :]
             target = other_scr
-            target[..., place] = dot(other, weights).astype(bf16).reshape(
+            target[..., place] = contract_cols(other, weights).astype(bf16).reshape(
                 target.shape[:-1] + (tile,)
             )
             target = kept_scr.at[kept_slot]
-            target[..., place] = dot(mine, weights).astype(bf16).reshape(
+            target[..., place] = contract_cols(mine, weights).astype(bf16).reshape(
                 target.shape[:-1] + (tile,)
             )
 
@@ -1589,7 +1589,7 @@
     heads_here = tables.shape[0]
     seq_size = 2 ** len(seq_bits)
     span = length // seq_size
-    width = w_slice.shape[1]
+    width = w_slice.shape[0]
     packed = heads_here * 3 * HEAD
     any_space = pl.BlockSpec(memory_space=pl.ANY)
     near_space = pl.BlockSpec(memory_space=pltpu.VMEM)
@@ -1752,6 +1752,53 @@
     )(woven)
 
 
+def dense_back_kernel(rows_here, core_ref, context_ref, grad_ref, dense_ref, back_ref, mine_ref, other_ref):
+    core = core_ref[0]
+    back_ref[...] = contract_cols(grad_ref[...], dense_ref[...]).astype(bf16)
+    products = contract_rows(context_ref[...], grad_ref[...]).astype(bf16)
+    for order in range(products.shape[0] // (2 * rows_here)):
+        first, second = (
+            products[start : start + rows_here]
+            for start in (2 * order * rows_here, (2 * order + 1) * rows_here)
+        )
+        rows = slice(order * rows_here, (order + 1) * rows_here)
+        mine_ref[rows, :] = jnp.where(core == 0, first, second)
+        other_ref[rows, :] = jnp.where(core == 0, second, first)
+
+
+def dense_back(core, context, grad_branch, w_dense, rows_here):
+    rows, width = context.shape
+    tile = 256
+    grid_spec = pltpu.PrefetchScalarGridSpec(
+        num_scalar_prefetch=1,
+        grid=(width // tile,),
+        in_specs=[
+            pl.BlockSpec((rows, tile), lambda i, c: (0, i)),
+            pl.BlockSpec((rows, width), lambda i, c: (0, 0)),
+            pl.BlockSpec((tile, width), lambda i, c: (i, 0)),
+        ],
+        out_specs=[
+            pl.BlockSpec((rows, tile), lambda i, c: (0, i)),
+            pl.BlockSpec((tile // 2, width), lambda i, c: (i, 0)),
+            pl.BlockSpec((tile // 2, width), lambda i, c: (i, 0)),
+        ],
+    )
+    return pl.pallas_call(
+        functools.partial(dense_back_kernel, rows_here),
+        grid_spec=grid_spec,
+        out_shape=[
+            jax.ShapeDtypeStruct((rows, width), bf16),
+            jax.ShapeDtypeStruct((width // 2, width), bf16),
+            jax.ShapeDtypeStruct((width // 2, width), bf16),
+        ],
+        compiler_params=pltpu.CompilerParams(vmem_limit_bytes=32 * 2**20),
+        cost_estimate=pl.CostEstimate(
+            flops=4 * rows * width * width, bytes_accessed=6 * width * width, transcendentals=0
+        ),
+        name="dense_back",
+    )(core, context, grad_branch, w_dense)
+
+
 def ff_kernel(
     item_bits,
     shared_ref,
@@ -2302,9 +2349,10 @@
     group_all = members * rows_all
     context = context.reshape(rows_all, width)
     grad_branch = grad_branch.reshape(rows_all, width)
-    grad_context = contract_cols(grad_branch, w_dense).astype(bf16)
     core = my_bit(*seq_bits[0])
-
+    grad_context, dense_mine, dense_other = dense_back(
+        core.astype(jnp.int32).reshape(1), context, grad_branch, w_dense, rows_here
+    )
     def core_sum(whole):
         parts = whole.reshape(count // 2, 2, rows_here, -1)
         got = lines.swap(pick(parts, 1 - core, 1), *seq_bits[0])
@@ -2318,7 +2366,13 @@
         axis=1,
     )
     by_rows = jnp.concatenate(
-        [core_sum(contract_rows(context, grad_branch).astype(bf16)), core_sum(small_sums)],
+        [
+            (
+                dense_mine.astype(f32)
+                + lines.swap(dense_other, *seq_bits[0]).astype(f32)
+            ).astype(bf16),
+            core_sum(small_sums).reshape(width // 2, 256),
+        ],
         axis=-1,
     )
     row_dims = item_bits[::-1] + seq_bits[:0:-1]
@@ -2337,7 +2391,7 @@
         cosine,
         sine_part,
         log_sums,
-        w_slice.T,
+        w_slice,
     )
     shared = shared.reshape(group_all, width)
     grad_in = grad_in.reshape(group_all, 2 * ff_part)

time: 924 us -> 923 us (level)
  matrix products: 25.2 us -> 3.73 us
  Pallas kernels: 831 us -> 846 us
    pallas_call x0 -> x1, Pallas kernels: none -> 13.1 us  [dense_back(): pl.pallas_call(functools.partial(dense_back_kernel, rows_here), grid_spec...]
    dot_general x2 -> x1, matrix products: 11 us -> 1.03 us  [contract_cols(): lax.dot_general(left, right, (((1,), (1,)), ((), ())), preferred_element_...]
    dot_general x3 -> x2, matrix products: 10.8 us -> 0.89 us  [contract_rows(): lax.dot_general(left, right, (((0,), (0,)), ((), ())), preferred_element_...]
  transfers between devices with their start and end apart: 2 -> 2, of which waited for: 0 -> 1; matrix products, arithmetic and copies ran while one was open for 3% -> 1% of each run, Pallas kernels for 0% -> 0%
where the time goes in v7:
time: 923 us; the launch traced here: 913 us
  Pallas kernels  846 us (92%)
  local copies, waits for them, and re-layouts  35.5 us (4%)
  other arithmetic  21.4 us (2%)
    pallas_call x1, Pallas kernels, merged_call(): pl.pallas_call(functools.partial(merged_kernel, item_bits, seq_bits), in_...  333 us
    pallas_call x1, Pallas kernels, ff_call(): pl.pallas_call(functools.partial(ff_kernel, item_bits), in_specs=[any_spa...  208 us
    pallas_call x1, Pallas kernels, second_call(): pl.pallas_call(functools.partial(second_kernel, item_bits, seq_bits), in_...  184 us
    pallas_call x1, Pallas kernels, first_call(): pl.pallas_call(functools.partial(first_kernel, item_bits, seq_bits, row_c...  105 us
  transfers between devices with their start and end apart: 2, of which 1 were waited for; matrix products, arithmetic and copies ran while one was open for 1% of the time, Pallas kernels for 0%

profile of v7, /device:TPU:0, one launch (start us, length us, event | category | flops | bytes accessed | tf_op | source)
XLA Modules:
  0.0 913.3 jit_solution(15375074957633490316)
XLA Ops:
  1.4 1.4 pad.17.padded_ref
  4.2 2.8 reshape.163
  7.1 2.0 copy.47
  10.9 105.1 %first.1 = (bf16[4,8,96,128]{3,2,1,0:T(8,128)(2,1)}, f32[128,768]{1,0:T(8,128)S(1)}, bf16[8,80,768]{2,1,0:T(8,128)(2,1)S(1)}, bf16[4,4,2,64,2048]{4,3,2,1,0:T(8,...) custom-call(bf16[96,128]{1,0:T(8,128)(2,1)S(1)} %concatenate.32.small_ref, ...), custom_call_target="tpu_custom_call" | custom-call | tf_op jit(solution)/shard_map/first/pallas_call | solution.py:348
  116.0 3.3 copy-done
  119.3 1.6 copy-done.6
  124.7 1.9 slice.93
  127.2 2.0 fusion.onehot_ref
  133.8 183.8 %second.1 = (bf16[4,128,2048]{2,1,0:T(8,128)(2,1)}, f32[4,2,1,1024]{3,2,1,0:T(1,128)}, bf16[8,256,2816]{2,1,0:T(8,128)(2,1)}, bf16[8,256,1408]{2,1,0:T(8,128)(2,...) custom-call(s32[4]{0:T(128)} %compare_select_fusion.1.visible_ref, ...), custom_call_target="tpu_custom_call" | custom-call | tf_op jit(solution)/shard_map/second/pallas_call | solution.py:635
  317.5 208.2 %feed_forward.1 = (bf16[4,512,1408]{2,1,0:T(8,128)(2,1)}, bf16[4,2,512,1408]{3,2,1,0:T(8,128)(2,1)}, bf16[4,4,128,2048]{3,2,1,0:T(8,128)(2,1)}, bf16[4,512,2816]...) custom-call(bf16[4,4,128,2048]{3,2,1,0:T(8,128)(2,1)} %get-tuple-ele, ...), custom_call_target="tpu_custom_call" | custom-call | tf_op jit(solution)/shard_map/feed_forward/pallas_call | solution.py:2144
  525.8 1.6 copy-done.1
  527.4 1.6 copy-done.12
  529.0 13.1 %dense_back.1 = (bf16[512,2048]{1,0:T(8,128)(2,1)S(1)}, bf16[1024,2048]{1,0:T(8,128)(2,1)S(1)}, bf16[1024,2048]{1,0:T(8,128)(2,1)}) custom-call(s32[1]{0:T(128)} %bitcast.20.core_ref, bf16[512,2048]{1,0:T(8,128)(2,1)S(1)} %bitcast.89, bf16[512,2048]{1,0:T(8,128)(2,1)S(1)} %bitcast.84, bf16[2048,2048]{1,0:T(8,128)(2,1)} %bitcast.83), custom_call_target="tpu_custom_call" | custom-call | flops 8589934592 | bytes 25165824 | tf_op jit(solution)/shard_map/dense_back/pallas_call | solution.py:1786
  542.1 2.0 copy-done.3
  544.1 1.3 copy-done.7
  547.7 5.2 collective-permute-done
  553.0 5.4 add_convert_fusion
  558.6 2.6 pad_maximum_fusion.dense_ref
  561.2 333.2 %merged.1 = (bf16[4,128,2048]{2,1,0:T(8,128)(2,1)}, bf16[8,2,128,384]{3,2,1,0:T(8,128)(2,1)}, bf16[3,4,64,1408]{3,2,1,0:T(8,128)(2,1)}, bf16[64,2304]{1,0:T(8,12...) custom-call(s32[4]{0:T(128)} %compare_select_fusion.1.visible_ref, ...), custom_call_target="tpu_custom_call" | custom-call | tf_op jit(solution)/shard_map/merged/pallas_call | solution.py:1604
  894.5 2.2 copy.43
  896.7 1.8 convolution_bitcast_fusion
  900.9 1.9 unweave.1
  906.3 5.3 multiply_add_fusion
  911.6 1.3 copy.51
  (124 shorter events, 21.1 us)
Async XLA Ops:
  2.8 6.3 copy-start.25
  2.9 6.3 copy-start.26
  3.2 6.2 copy-start.27
  3.2 6.2 copy-start.28
  3.2 6.2 copy-start.29
  3.2 6.2 copy-start.30
  3.3 6.2 copy-start.31
  3.3 6.2 copy-start.32
  3.3 6.3 copy-start.19
  3.3 6.3 copy-start.24
  3.3 6.4 copy-start.4
  3.3 6.4 copy-start.11
  122.7 7.3 copy-start.22
  123.6 6.6 copy-start.10
  126.8 5.2 copy-start.33
  126.8 5.2 copy-start.34
  529.0 16.5 %copy-start.23 = (f32[1,2816]{1,0:T(1,128)S(1)}, f32[1,2816]{1,0:T(1,128)}, u32[]{:S(2)}) copy-start(f32[1,2816]{1,0:T(1,128)} %get-tuple-element.82) | copy-start | bytes 33796
  529.0 17.2 %copy-start.20 = (f32[8,2048]{1,0:T(8,128)S(1)}, f32[8,2048]{1,0:T(8,128)}, u32[]{:S(2)}) copy-start(f32[8,2048]{1,0:T(8,128)} %get-tuple-element.80) | copy-start | bytes 196612
  529.0 17.5 %copy-start.2 = (bf16[4,128,2048]{2,1,0:T(8,128)(2,1)S(1)}, bf16[4,128,2048]{2,1,0:T(8,128)(2,1)}, u32[]{:S(2)}) copy-start(bf16[4,128,2048]{2,1,0:T(8,128)(2,1)} %get-tuple-element.73) | copy-start | bytes 6291460
  545.4 7.5 collective-permute-start
  552.9 5.5 collective-permute-start.1
  896.7 3.7 copy-start.13
  902.8 3.5 copy-start.16
  906.3 5.3 copy-start.17
  (13 other events, 23.3 us)

commit v8 on v7

--- a/solution.py
+++ b/solution.py
@@ -1805,8 +1805,8 @@
     normed_ref,
     inverse_ref,
     cotangent_ref,
-    in_ref,
-    out_ref,
+    in_all_ref,
+    out_all_ref,
     vector_ref,
     bias_ref,
     block_ref,
@@ -1831,6 +1831,9 @@
     resid_scr,
     normed_scr,
     gate_scr,
+    in_ref,
+    out_ref,
+    weight_sems,
     send_sems,
     recv_sems,
     load_sems,
@@ -1841,6 +1844,10 @@
     tiles = product_scr.shape[-1] // 128
     tile = 256
     near, far = ("seq", 1), ("seq", 2)
+    in_copy = pltpu.make_async_copy(in_all_ref, in_ref, weight_sems.at[0])
+    out_copy = pltpu.make_async_copy(out_all_ref, out_ref, weight_sems.at[1])
+    in_copy.start()
+    out_copy.start()
     greet([mask_of(near), mask_of(far)] + [mask_of(step) for step in item_bits])
     copies = Copies(send_sems, recv_sems, keep_sems)
     item_place = copies.here[0]
@@ -2095,24 +2102,27 @@
     load_normed(0)
     load_normed(1)
     last = chunks - 1
+    in_copy.wait()
     for chunk in range(chunks):
         forward_gate(chunk)
-        if chunk >= 1:
-            sum_near(chunk - 1, chunk - 1)
-        if chunk >= 2:
-            second_norm(chunk - 2)
-        if chunk >= 3:
-            pass_on(chunk - 3)
+        if chunk == 0:
+            out_copy.wait()
+        if chunk == last:
+            pass_on(0)
         forward_out(chunk)
-    sum_near(last, last)
-    second_norm(last - 1)
-    pass_on(last - 2)
+        sum_near(chunk, chunk)
+        if chunk:
+            second_norm(chunk - 1)
+    pass_on(1)
     load_grads(0)
     for chunk in range(chunks):
         backward_gate(chunk)
+        if chunk == 0:
+            load_grads(1)
         if chunk >= 2:
             first_norm(chunk - 2)
         backward_in(chunk)
+        sum_near(("back", chunk), chunk)
         spread_block()
         if chunk == 0:
             second_norm(last)
@@ -2120,10 +2130,7 @@
             load_normed(1)
         elif chunk + 1 < chunks:
             pass_on(chunk + 1)
-        if chunk + 1 < chunks:
             load_grads(chunk + 1)
-            sum_near(("back", chunk), chunk)
-    sum_near(("back", last), last)
     first_norm(last - 1)
     first_norm(last)
     wait_all(spread[-1:])
@@ -2143,7 +2150,7 @@
     spare = 8 * chunks
     return pl.pallas_call(
         functools.partial(ff_kernel, item_bits),
-        in_specs=[any_space, any_space] + [near_space] * 6 + [any_space],
+        in_specs=[any_space] * 2 + [near_space] * 2 + [any_space] * 2 + [near_space] * 2 + [any_space],
         out_specs=[any_space] * 4 + [near_space, any_space, near_space, near_space, any_space, any_space],
         out_shape=[
             jax.ShapeDtypeStruct((chunks, group_rows, ff_part), bf16),
@@ -2169,6 +2176,9 @@
             pltpu.VMEM((chunks, span, width), f32),
             pltpu.VMEM((2, span, width), f32),
             pltpu.VMEM((2, group_rows, 256), f32),
+            pltpu.VMEM(w_in.shape, bf16),
+            pltpu.VMEM(w_out.shape, bf16),
+            pltpu.SemaphoreType.DMA((2,)),
             pltpu.SemaphoreType.DMA((spare,)),
             pltpu.SemaphoreType.DMA((spare,)),
             pltpu.SemaphoreType.DMA((6,)),

time: 923 us -> 916 us (level)
  no operation moved by 1% of the time
where the time goes in v8:
time: 916 us; the launch traced here: 907 us
  Pallas kernels  839 us (92%)
  local copies, waits for them, and re-layouts  35.5 us (4%)
  other arithmetic  21.4 us (2%)
    pallas_call x1, Pallas kernels, merged_call(): pl.pallas_call(functools.partial(merged_kernel, item_bits, seq_bits), in_...  333 us
    pallas_call x1, Pallas kernels, ff_call(): pl.pallas_call(functools.partial(ff_kernel, item_bits), in_specs=[any_spa...  202 us
    pallas_call x1, Pallas kernels, second_call(): pl.pallas_call(functools.partial(second_kernel, item_bits, seq_bits), in_...  184 us
    pallas_call x1, Pallas kernels, first_call(): pl.pallas_call(functools.partial(first_kernel, item_bits, seq_bits, row_c...  105 us
  transfers between devices with their start and end apart: 2, of which 1 were waited for; matrix products, arithmetic and copies ran while one was open for 1% of the time, Pallas kernels for 0%

profile of v8, /device:TPU:0, one launch (start us, length us, event | category | flops | bytes accessed | tf_op | source)
XLA Modules:
  0.0 906.9 jit_solution(5651517703106003460)
XLA Ops:
  1.4 1.4 pad.17.padded_ref
  4.2 2.8 reshape.163
  7.1 2.0 copy.47
  10.9 105.1 %first.1 = (bf16[4,8,96,128]{3,2,1,0:T(8,128)(2,1)}, f32[128,768]{1,0:T(8,128)S(1)}, bf16[8,80,768]{2,1,0:T(8,128)(2,1)S(1)}, bf16[4,4,2,64,2048]{4,3,2,1,0:T(8,...) custom-call(bf16[96,128]{1,0:T(8,128)(2,1)S(1)} %concatenate.32.small_ref, ...), custom_call_target="tpu_custom_call" | custom-call | tf_op jit(solution)/shard_map/first/pallas_call | solution.py:348
  116.0 3.3 copy-done
  119.3 1.6 copy-done.6
  124.7 1.9 slice.93
  127.2 2.0 fusion.onehot_ref
  133.8 183.8 %second.1 = (bf16[4,128,2048]{2,1,0:T(8,128)(2,1)}, f32[4,2,1,1024]{3,2,1,0:T(1,128)}, bf16[8,256,2816]{2,1,0:T(8,128)(2,1)}, bf16[8,256,1408]{2,1,0:T(8,128)(2,...) custom-call(s32[4]{0:T(128)} %compare_select_fusion.1.visible_ref, ...), custom_call_target="tpu_custom_call" | custom-call | tf_op jit(solution)/shard_map/second/pallas_call | solution.py:635
  317.5 201.8 %feed_forward.1 = (bf16[4,512,1408]{2,1,0:T(8,128)(2,1)}, bf16[4,2,512,1408]{3,2,1,0:T(8,128)(2,1)}, bf16[4,4,128,2048]{3,2,1,0:T(8,128)(2,1)}, bf16[4,512,2816]...) custom-call(bf16[4,4,128,2048]{3,2,1,0:T(8,128)(2,1)} %get-tuple-ele, ...), custom_call_target="tpu_custom_call" | custom-call | tf_op jit(solution)/shard_map/feed_forward/pallas_call | solution.py:2151
  519.4 1.6 copy-done.1
  521.0 1.6 copy-done.12
  522.6 13.1 %dense_back.1 = (bf16[512,2048]{1,0:T(8,128)(2,1)S(1)}, bf16[1024,2048]{1,0:T(8,128)(2,1)S(1)}, bf16[1024,2048]{1,0:T(8,128)(2,1)}) custom-call(s32[1]{0:T(128)} %bitcast.20.core_ref, bf16[512,2048]{1,0:T(8,128)(2,1)S(1)} %bitcast.89, bf16[512,2048]{1,0:T(8,128)(2,1)S(1)} %bitcast.84, bf16[2048,2048]{1,0:T(8,128)(2,1)} %bitcast.83), custom_call_target="tpu_custom_call" | custom-call | flops 8589934592 | bytes 25165824 | tf_op jit(solution)/shard_map/dense_back/pallas_call | solution.py:1786
  535.7 2.0 copy-done.3
  537.7 1.3 copy-done.7
  541.3 5.2 collective-permute-done
  546.6 5.4 add_convert_fusion
  552.2 2.6 pad_maximum_fusion.dense_ref
  554.8 333.2 %merged.1 = (bf16[4,128,2048]{2,1,0:T(8,128)(2,1)}, bf16[8,2,128,384]{3,2,1,0:T(8,128)(2,1)}, bf16[3,4,64,1408]{3,2,1,0:T(8,128)(2,1)}, bf16[64,2304]{1,0:T(8,12...) custom-call(s32[4]{0:T(128)} %compare_select_fusion.1.visible_ref, ...), custom_call_target="tpu_custom_call" | custom-call | tf_op jit(solution)/shard_map/merged/pallas_call | solution.py:1604
  888.0 2.2 copy.43
  890.3 1.8 convolution_bitcast_fusion
  894.5 1.9 unweave.1
  899.9 5.3 multiply_add_fusion
  905.2 1.3 copy.51
  (124 shorter events, 21.1 us)
Async XLA Ops:
  2.8 6.3 copy-start.25
  2.9 6.3 copy-start.26
  3.2 6.2 copy-start.27
  3.2 6.2 copy-start.28
  3.2 6.2 copy-start.29
  3.2 6.2 copy-start.30
  3.3 6.2 copy-start.31
  3.3 6.2 copy-start.32
  3.3 6.3 copy-start.19
  3.3 6.3 copy-start.24
  3.3 6.4 copy-start.4
  3.3 6.4 copy-start.11
  122.7 7.3 copy-start.22
  123.6 6.6 copy-start.10
  126.8 5.2 copy-start.33
  126.8 5.2 copy-start.34
  522.6 16.5 %copy-start.23 = (f32[1,2816]{1,0:T(1,128)S(1)}, f32[1,2816]{1,0:T(1,128)}, u32[]{:S(2)}) copy-start(f32[1,2816]{1,0:T(1,128)} %get-tuple-element.82) | copy-start | bytes 33796
  522.6 17.2 %copy-start.20 = (f32[8,2048]{1,0:T(8,128)S(1)}, f32[8,2048]{1,0:T(8,128)}, u32[]{:S(2)}) copy-start(f32[8,2048]{1,0:T(8,128)} %get-tuple-element.80) | copy-start | bytes 196612
  522.6 17.5 %copy-start.2 = (bf16[4,128,2048]{2,1,0:T(8,128)(2,1)S(1)}, bf16[4,128,2048]{2,1,0:T(8,128)(2,1)}, u32[]{:S(2)}) copy-start(bf16[4,128,2048]{2,1,0:T(8,128)(2,1)} %get-tuple-element.73) | copy-start | bytes 6291460
  539.0 7.5 collective-permute-start
  546.5 5.5 collective-permute-start.1
  890.3 3.7 copy-start.13
  896.4 3.5 copy-start.16
  899.9 5.3 copy-start.17
  (13 other events, 23.3 us)
